TPU v7x, 32 devices: a whole 2x2x4 slice. The times are simulated.
32 devices in a mesh: det: 8 (over z, core), band: 4 (over y, x).
Axes of the slice: x: 2, y: 2, z: 4, core: 2. Of those that a mesh axis runs over, the one named last changes fastest.
Arguments:
- scan_lines: float32 [256, 4096], P(('det', 'band')), may hold values from -6 to 6
- response: float32 [256, 4096], P(('det', 'band')), may hold values from 0.02 to 1
- cycle_offset: int32 [256, 4096], P(('det', 'band')), may hold values from 0 to 255
- column: int32 [256, 4096], P(('det', 'band')), may hold values from 0 to 2047
- order_slot: int32 [256], replicated, may hold values from 0 to 255, each once
- legendre: float32 [256, 1024, 1024], P('det', 'band'), may hold values from -0.046875 to 0.046875
Outputs:
- harmonics: float32 [2, 256, 1024], P(None, 'det', 'band')
- sky_map: float32 [1024, 2048], P(('band', 'det'))
Inputs may be any that keep to these rules, and one draw needn't show every extreme that they name: `order_slot`: each of the orders 0 to 255 stands in exactly one slot.
All inputs are finite; a program needn't handle non-finite values.
Results may differ from a plain program's by a relative error of at most 0.000073.
Values sent between devices are 32-bit elements; how exact they have to be, the bound alone decides.
No kernel may reach another device: no remote copies, remote signals or barrier semaphores. Data moves between devices by JAX's collectives and lax.ppermute only.
A program may use at most 128 MiB of HBM per device.

v0:
```python
import jax
import jax.numpy as jnp
from jax import lax
from jax.sharding import PartitionSpec as P

NPHI = 2048
LMAX = 1024


precise = lax.Precision.HIGHEST


def twiddle_pair(count_rows, count_cols, modulus):
    row_index = jnp.arange(count_rows, dtype=jnp.int32)[:, None]
    col_index = jnp.arange(count_cols, dtype=jnp.int32)[None, :]
    phases = 2.0 * jnp.pi / modulus * (row_index * col_index % modulus).astype(jnp.float32)
    return (jnp.cos(phases), jnp.sin(phases))


def noise_filter(scan_lines, response):
    line_count, length = scan_lines.shape
    log_size = length.bit_length() - 1
    inner_len = 1 << log_size // 2
    outer_len = length // inner_len
    cos_outer, sin_outer = twiddle_pair(outer_len, outer_len, outer_len)
    cos_inner, sin_inner = twiddle_pair(inner_len, inner_len, inner_len)
    twist_cos, twist_sin = twiddle_pair(outer_len, inner_len, length)
    shaped = scan_lines.reshape(line_count, outer_len, inner_len)
    first_real = jnp.einsum("lna,nk->lka", shaped, cos_outer, precision=precise)
    first_imag = -jnp.einsum("lna,nk->lka", shaped, sin_outer, precision=precise)
    turned_real = first_real * twist_cos + first_imag * twist_sin
    turned_imag = first_imag * twist_cos - first_real * twist_sin
    spec_real = jnp.einsum("lka,aj->lkj", turned_real, cos_inner, precision=precise) + jnp.einsum(
        "lka,aj->lkj", turned_imag, sin_inner, precision=precise
    )
    spec_imag = jnp.einsum("lka,aj->lkj", turned_imag, cos_inner, precision=precise) - jnp.einsum(
        "lka,aj->lkj", turned_real, sin_inner, precision=precise
    )
    weights_k = response.reshape(line_count, inner_len, outer_len).transpose(0, 2, 1)
    spec_real = spec_real * weights_k
    spec_imag = spec_imag * weights_k
    back_real = jnp.einsum("lkj,jn->lkn", spec_real, cos_inner, precision=precise) - jnp.einsum(
        "lkj,jn->lkn", spec_imag, sin_inner, precision=precise
    )
    back_imag = jnp.einsum("lkj,jn->lkn", spec_imag, cos_inner, precision=precise) + jnp.einsum(
        "lkj,jn->lkn", spec_real, sin_inner, precision=precise
    )
    untwist_real = back_real * twist_cos - back_imag * twist_sin
    untwist_imag = back_imag * twist_cos + back_real * twist_sin
    result = jnp.einsum("lkn,km->lmn", untwist_real, cos_outer, precision=precise) - jnp.einsum(
        "lkn,km->lmn", untwist_imag, sin_outer, precision=precise
    )
    return (result / length).reshape(line_count, length)


def local(scan_lines, response, cycle_offset, column, order_slot, legendre):
    filtered = noise_filter(scan_lines, response)
    band_cycles = legendre.shape[1]
    flat_index = (cycle_offset * NPHI + column).reshape(-1)
    partial_value = (
        jnp.zeros((band_cycles * NPHI,), jnp.float32)
        .at[flat_index]
        .add(filtered.reshape(-1))
        .reshape(band_cycles, NPHI)
    )
    counts = (
        jnp.zeros((band_cycles * NPHI,), jnp.float32)
        .at[flat_index]
        .add(1.0)
        .reshape(band_cycles, NPHI)
    )
    summed, hit_total = (
        lax.psum_scatter(partial_value, "det", scatter_dimension=0, tiled=True),
        lax.psum_scatter(counts, "det", scatter_dimension=0, tiled=True),
    )
    sky_map = summed / jnp.maximum(hit_total, 1.0)
    pixel_index = jnp.arange(NPHI, dtype=jnp.int32)[:, None]
    phases = 2.0 * jnp.pi / NPHI * (pixel_index * order_slot[None, :] % NPHI).astype(jnp.float32)
    cycle_real = jnp.dot(
        sky_map, jnp.cos(phases), precision=precise, preferred_element_type=jnp.float32
    )
    cycle_imag = -jnp.dot(
        sky_map, jnp.sin(phases), precision=precise, preferred_element_type=jnp.float32
    )
    cycle_modes = jnp.stack([cycle_real, cycle_imag])
    slot_count = legendre.shape[0]
    slot_start = lax.axis_index("det") * slot_count
    local_orders = lax.dynamic_slice_in_dim(order_slot, slot_start, slot_count, 0)
    degree_index = jnp.arange(LMAX, dtype=jnp.int32)
    keep_mask = (degree_index[None, :] >= local_orders[:, None]).astype(jnp.float32)
    terms = (
        jnp.einsum(
            "crs,srl->csl",
            lax.all_to_all(cycle_modes, "det", split_axis=2, concat_axis=1, tiled=True),
            legendre,
            precision=precise,
        )
        * keep_mask[None]
    )
    harmonics = lax.psum_scatter(terms, "band", scatter_dimension=2, tiled=True)
    return (harmonics, sky_map)


def solution(mesh):
    return jax.shard_map(
        local,
        mesh=mesh,
        in_specs=(
            P(("det", "band"), None),
            P(("det", "band"), None),
            P(("det", "band"), None),
            P(("det", "band"), None),
            P(),
            P("det", "band", None),
        ),
        out_specs=(P(None, "det", "band"), P(("band", "det"), None)),
        check_vma=False,
    )
```

profile of v0, /device:TPU:0, one launch (start us, length us, event | category | flops | bytes accessed | tf_op | source)
XLA Modules:
  0.0 523.7 jit_solution(16387299754876649385)
XLA Ops:
  7.5 1.0 reshape.104
  9.1 0.5 fusion.65
  14.4 0.5 fusion.39
  14.9 0.5 fusion.11
  15.6 171.6 %scatter_custom_fusion = f32[524288]{0:T(1024)S(1)} fusion(s32[32768]{0:T(1024)S(1)} %bitcast.90, f32[32768]{0:T(1024)S(1)} %reshape.112, f32[]{:T(128)} %constant.54.clone.1), kind=kCustom, calls=%fused_computation.32 | custom fusion | flops 32768 | bytes 2097156 | tf_op jit(solution)/shard_map/scatter-add | solution.py:63
  187.2 1.5 reshape.106
  188.8 171.6 %scatter_custom_fusion.1 = f32[524288]{0:T(1024)S(1)} fusion(s32[32768]{0:T(1024)S(1)} %bitcast.91, f32[32768]{0:T(1024)S(1)} %broadcast.117, f32[]{:T(128)} %constant.54.clone.1), kind=kCustom, calls=%fused_computation.30 | custom fusion | flops 32768 | bytes 2097156 | tf_op jit(solution)/shard_map/scatter-add | solution.py:69
  360.3 1.6 reshape.107
  362.0 0.6 copy-done.4
  362.7 37.9 %reduce-scatter.8.cloned.1.call-done = f32[32,2048]{1,0:T(8,128)} async-done(((f32[256,2048]{1,0:T(8,128)}), f32[32,2048]{1,0:T(8,128)}) %reduce-scatter.8.cloned.1.call-update) | async-done | bytes 262160 | tf_op jit(solution)/shard_map/reduce_scatter | solution.py:74
  400.6 1.1 maximum_divide_fusion
  401.7 8.8 %fusion.21 = f32[1,32,256]{2,1,0:T(8,128)S(1)} fusion(f32[32,2048]{1,0:T(8,128)S(1)} %maximum_divide_fusion, s32[256]{0:T(256)S(1)} %copy-done.4), kind=kOutput, calls=%fused_computation.29 | convolution fusion | flops 208674816 | bytes 295936 | tf_op jit(solution)/shard_map/dot_general | solution.py:82
  410.5 8.9 %fusion.15 = f32[1,32,256]{2,1,0:T(8,128)S(1)} fusion(f32[32,2048]{1,0:T(8,128)S(1)} %maximum_divide_fusion, s32[256]{0:T(256)S(1)} %copy-done.4), kind=kOutput, calls=%fused_computation.27 | convolution fusion | flops 208666624 | bytes 295936 | tf_op jit(solution)/shard_map/dot_general | solution.py:79
  419.6 0.9 reshape.140
  420.5 3.4 all-to-all-start
  424.0 5.7 %all-to-all-done = f32[8,1,2048]{2,1,0:T(1,128)S(1)} async-done(((f32[8,1,2048]{2,1,0:T(1,128)}), f32[8,1,2048]{2,1,0:T(1,128)S(1)}, u32[]{:S(2)}, u32[]{:S(2)}) %all-to-all-start) | async-done | bytes 65568 | tf_op jit(solution)/shard_map/all_to_all | solution.py:94
  429.7 0.5 broadcast.218
  430.2 0.8 reduce
  431.6 22.0 %fusion.14 = f32[2,32,1024]{2,0,1:T(2,128)S(1)} fusion(f32[2,256,32]{1,0,2:T(2,128)S(1)} %all_to_all.16, f32[32,256,1024]{2,1,0:T(8,128)} %param.11, f32[32,1024]{1,0:T(8,128)S(1)} %fusion.47), kind=kOutput, calls=%fused_computation.26 | convolution fusion | flops 201392128 | bytes 34013184 | tf_op jit(solution)/shard_map/crs,srl->csl/dot_general | solution.py:92
  453.5 13.7 %copy.69 = f32[2,32,1024]{0,1,2:T(8,128)} copy(f32[2,32,1024]{2,0,1:T(2,128)S(1)} %fusion.14) | data formatting | bytes 524288
  467.3 15.4 %reshape.134 = f32[1024,64]{1,0:T(8,128)} reshape(f32[1024,32,2]{2,1,0:T(8,128)} %bitcast.84) | data formatting | bytes 524288
  482.6 23.5 %reduce-scatter.10.cloned.1.call-done = f32[256,64]{1,0:T(8,128)} async-done(((f32[1024,64]{1,0:T(8,128)}), f32[256,64]{1,0:T(8,128)}) %reduce-scatter.10.cloned.1.call-update) | async-done | bytes 65552
  506.1 6.5 %reshape.135 = f32[256,32,2]{2,1,0:T(8,128)} reshape(f32[256,64]{1,0:T(8,128)} %reduce-scatter.10.cloned.1.call-done) | data formatting | bytes 131072
  512.6 4.2 copy.52
  (43 shorter events, 6.6 us)
Async XLA Ops:
  7.2 3.6 copy-start.1
  7.2 3.6 copy-start.2
  7.2 355.5 %reduce-scatter.6.cloned.1.call-start = ((), (), s32[]{:S(2)}) async-start(), calls=%async_computation.4 | async-start | bytes 2359296 | tf_op jit(solution)/shard_map/reduce_scatter | solution.py:73
  7.5 3.6 copy-start.3
  188.7 211.9 %reduce-scatter.8.cloned.1.call-start = ((), (), s32[]{:S(2)}) async-start(), calls=%async_computation.5 | async-start | bytes 2359296 | tf_op jit(solution)/shard_map/reduce_scatter | solution.py:74
  362.0 0.7 copy-start.4
  401.7 8.8 %copy-start = (f32[32,2048]{1,0:T(8,128)}, f32[32,2048]{1,0:T(8,128)S(1)}, u32[]{:S(2)}) copy-start(f32[32,2048]{1,0:T(8,128)S(1)} %maximum_divide_fusion) | copy-start | bytes 786436
  420.5 9.2 %all-to-all-start = ((f32[8,1,2048]{2,1,0:T(1,128)}), f32[8,1,2048]{2,1,0:T(1,128)S(1)}, u32[]{:S(2)}, u32[]{:S(2)}) async-start(f32[8,1,2048]{2,1,0:T(1,128)} %reshape.140), calls=%async_computation.2 | async-start | bytes 131072 | tf_op jit(solution)/shard_map/all_to_all | solution.py:94
  423.9 82.2 %reduce-scatter.10.cloned.1.call-start = ((), (), s32[]{:S(2)}) async-start(), calls=%async_computation.6 | async-start | bytes 655360
Sparse Core Ops, SparseCore 0:
  188.8 38.4 reduce-scatter.5
  362.1 38.4 reduce-scatter.7
  482.8 23.2 reduce-scatter.9
where the time goes:
time: 531 us; the launch traced here: 524 us
  other arithmetic  345 us (65%)
  waiting for transfers between devices  67.1 us (13%)
  local copies, waits for them, and re-layouts  47.4 us (9%)
  matrix products  45.7 us (9%)
  between operations  14.5 us (3%)
    scatter-add x1, other arithmetic, local(): partial_value = jnp.zeros((band_cycles * NPHI,), jnp.float32).at[flat_ind...  172 us
    scatter-add x1, other arithmetic, local(): counts = jnp.zeros((band_cycles * NPHI,), jnp.float32).at[flat_index].add...  172 us
    unnamed x17, local copies, waits for them, and re-layouts  41.7 us
    reduce_scatter x1, waiting for transfers between devices, local(): lax.psum_scatter(counts, 'det', scatter_dimension=0, tiled=True)  37.9 us
    unnamed x4, waiting for transfers between devices  23.5 us
    dot_general x1, matrix products, local(): jnp.einsum('crs,srl->csl', lax.all_to_all(cycle_modes, 'det', split_axis=...  22 us
  transfers between devices with their start and end apart: 4, of which 3 were waited for; matrix products, arithmetic and copies ran while one was open for 33% of the time, Pallas kernels for 0%

commit v1 on v0

v1 whole, which is shorter than its diff:
```python
import functools

import jax
import jax.numpy as jnp
import numpy as np
from jax import lax
from jax.experimental import pallas as pl
from jax.experimental.pallas import tpu as pltpu
from jax.sharding import PartitionSpec as P

NPHI = 2048
LANES = 128
SUB = 8
WINDOWS = 2
ROW = 256

precise = lax.Precision.HIGHEST
NT = (((1,), (1,)), ((), ()))


def filter_tables(length):
    outer = length // LANES
    k1 = np.arange(outer)[:, None]
    n2 = np.arange(LANES)[None, :]
    turn = 2.0 * np.pi * ((k1 * n2) % length) / length
    twiddle = np.stack([np.cos(turn), np.sin(turn)])[:, :, None, :]
    a = np.arange(LANES)
    angle = 2.0 * np.pi * (np.outer(a, a) % LANES) / LANES
    c, s = np.cos(angle), np.sin(angle)
    forward = np.block([[c, -s], [s, c]])
    back = np.block([[c, s], [-s, c]])
    return (
        twiddle.astype(np.float32),
        forward.astype(np.float32),
        back.astype(np.float32),
    )


def mode_tables(count):
    half = NPHI // 2
    p = np.arange(half)[:, None]
    out = []
    for parity in (0, 1):
        m = 2 * np.arange(count // 2)[None, :] + parity
        angle = 2.0 * np.pi * ((p * m) % NPHI) / NPHI
        out.append(np.concatenate([np.cos(angle), -np.sin(angle)], axis=1))
    table = np.stack(out).astype(np.float32)
    high = table.astype(jnp.bfloat16)
    low = (table - high.astype(np.float32)).astype(jnp.bfloat16)
    return high, low


def small_fft(re, im, sign):
    count = len(re)
    if count == 1:
        return re, im
    even_re, even_im = small_fft(re[0::2], None if im is None else im[0::2], sign)
    odd_re, odd_im = small_fft(re[1::2], None if im is None else im[1::2], sign)
    half = count // 2
    out_re, out_im = [None] * count, [None] * count
    for k in range(half):
        wr = float(np.cos(2 * np.pi * k / count))
        wi = float(sign * np.sin(2 * np.pi * k / count))
        er, ei, orr, oi = even_re[k], even_im and even_im[k], odd_re[k], odd_im and odd_im[k]
        if k == 0:
            tr, ti = orr, oi
        elif 4 * k == count:
            tr = None if oi is None else -wi * oi
            ti = wi * orr
        elif oi is None:
            tr, ti = wr * orr, wi * orr
        else:
            tr, ti = wr * orr - wi * oi, wr * oi + wi * orr
        out_re[k] = er if tr is None else er + tr
        out_re[k + half] = er if tr is None else er - tr
        if ti is None:
            out_im[k] = out_im[k + half] = ei
        else:
            out_im[k] = ti if ei is None else ei + ti
            out_im[k + half] = -ti if ei is None else ei - ti
    if all(x is None for x in out_im):
        return out_re, None
    out_im = [jnp.zeros_like(out_re[0]) if x is None else x for x in out_im]
    return out_re, out_im


def partner(x, axis, distance):
    size = x.shape[axis]
    if 2 * distance == size:
        return pltpu.roll(x, distance, axis=axis)
    index = lax.broadcasted_iota(jnp.int32, x.shape, axis)
    upper = (index & distance) != 0
    return jnp.where(
        upper,
        pltpu.roll(x, distance, axis=axis),
        pltpu.roll(x, size - distance, axis=axis),
    )


def rank_bit(bit, tile_bits):
    shape = (SUB, LANES)
    if bit < tile_bits + 3:
        return (lax.broadcasted_iota(jnp.int32, shape, 0) & (1 << (bit - tile_bits))) != 0
    return (lax.broadcasted_iota(jnp.int32, shape, 1) & (1 << (bit - tile_bits - 3))) != 0


def sort_inner(key_ref, val_ref, level, tile_bits, total_bits, group):
    tiles = key_ref.shape[0]

    def body(g, carry):
        part = pl.ds(g * group, group)
        key, val = key_ref[part], val_ref[part]
        for bit in range(level - 1, tile_bits - 1, -1):
            if bit < tile_bits + 3:
                axis, distance = 1, 1 << (bit - tile_bits)
            else:
                axis, distance = 2, 1 << (bit - tile_bits - 3)
            want_max = rank_bit(bit, tile_bits)
            if level < total_bits:
                want_max = jnp.logical_xor(want_max, rank_bit(level, tile_bits))
            sign = jnp.where(want_max, -1.0, 1.0)[None]
            key_p, val_p = partner(key, axis, distance), partner(val, axis, distance)
            swap = (key - key_p) * sign > 0.0
            key = jnp.where(swap, key_p, key)
            val = jnp.where(swap, val_p, val)
        key_ref[part] = key
        val_ref[part] = val
        return carry

    lax.fori_loop(0, tiles // group, body, 0)


def exchange(keys, vals, a, b, down):
    swap = keys[a] > keys[b]
    if down is True:
        swap = keys[a] < keys[b]
    elif down is not False:
        swap = jnp.logical_xor(swap, down)
    keys[a], keys[b] = jnp.where(swap, keys[b], keys[a]), jnp.where(swap, keys[a], keys[b])
    vals[a], vals[b] = jnp.where(swap, vals[b], vals[a]), jnp.where(swap, vals[a], vals[b])


def sort_across(key_ref, val_ref, level, tile_bits, total_bits):
    tiles = key_ref.shape[0]
    top = min(level, tile_bits)
    bits = list(range(top - 1, -1, -1))
    passes = [bits[:-3], bits[-3:]] if len(bits) > 3 else [bits]
    for chosen in passes:
        low, span = min(chosen), len(chosen)
        members = 1 << span
        stride = 1 << low

        def run(base, static_base):
            keys = [key_ref[base + i * stride] for i in range(members)]
            vals = [val_ref[base + i * stride] for i in range(members)]
            for bit in chosen:
                step = 1 << (bit - low)
                for i in range(members):
                    if i & step:
                        continue
                    if level >= total_bits:
                        down = False
                    elif level < tile_bits:
                        down = ((static_base + i * stride) >> level) & 1 == 1
                    else:
                        down = rank_bit(level, tile_bits)
                    exchange(keys, vals, i, i + step, down)
            for i in range(members):
                key_ref[base + i * stride] = keys[i]
                val_ref[base + i * stride] = vals[i]

        def base_of(g):
            return (g // stride) * (members * stride) + g % stride

        groups = tiles // members
        if level < tile_bits:
            for g in range(groups):
                run(base_of(g), base_of(g))
        else:
            for g in range(groups):
                run(base_of(g), None)


def sort_kernel(
    scan_ref, resp_ref, cycle_ref, column_ref, twiddle_ref, forward_ref, back_ref,
    filtered_ref, send_ref, flag_ref,
    key_ref, val_ref, spec_ref, key_rows, val_rows,
    *, buckets, span, rows, windows,
):
    lines, length = scan_ref.shape
    outer = length // LANES
    re, im = small_fft([scan_ref[:, n * LANES:(n + 1) * LANES] for n in range(outer)], None, -1)
    for k in range(outer):
        c, s = twiddle_ref[0, k], twiddle_ref[1, k]
        here = pl.ds(k * lines, lines)
        spec_ref[here, :LANES] = re[k] * c + im[k] * s
        spec_ref[here, LANES:] = im[k] * c - re[k] * s
    spec = jnp.dot(spec_ref[...], forward_ref[...], precision=precise, preferred_element_type=jnp.float32)
    resp = resp_ref[...] * (1.0 / length)
    spec = spec * jnp.concatenate([resp, resp], axis=1)
    spec_ref[...] = jnp.dot(spec, back_ref[...], precision=precise, preferred_element_type=jnp.float32)
    re, im = [], []
    for k in range(outer):
        c, s = twiddle_ref[0, k], twiddle_ref[1, k]
        here = pl.ds(k * lines, lines)
        ur, ui = spec_ref[here, :LANES], spec_ref[here, LANES:]
        re.append(ur * c - ui * s)
        im.append(ui * c + ur * s)
    out, _ = small_fft(re, im, 1)
    for n in range(outer):
        cols = slice(n * LANES, (n + 1) * LANES)
        filtered_ref[:, cols] = out[n]
        val_ref[n] = out[n]
        key_ref[n] = (cycle_ref[:, cols] * NPHI + column_ref[:, cols]).astype(jnp.float32)
    tiles = outer
    tile_bits = tiles.bit_length() - 1
    total_bits = tile_bits + 10
    for level in range(1, total_bits + 1):
        if level > tile_bits:
            sort_inner(key_ref, val_ref, level, tile_bits, total_bits, min(16, tiles))
        sort_across(key_ref, val_ref, level, tile_bits, total_bits)
    keys = key_ref[...]
    last = jnp.max(jnp.max(keys, axis=0), axis=0, keepdims=True)
    first = jnp.min(jnp.min(keys, axis=0), axis=0, keepdims=True)
    row_len = tiles * SUB
    key_rows[:LANES, :] = keys.reshape(row_len, LANES).T
    val_rows[:LANES, :] = val_ref[...].reshape(row_len, LANES).T
    reach = key_rows.shape[0] - LANES
    key_rows[LANES:, :] = jnp.full((reach, row_len), 2.0 * buckets * span, jnp.float32)
    val_rows[LANES:, :] = jnp.zeros((reach, row_len), jnp.float32)
    over = jnp.int32(0)
    for b in range(buckets):
        begin = jnp.sum((last < float(b * span)).astype(jnp.float32)).astype(jnp.int32)
        end = jnp.sum((first < float((b + 1) * span)).astype(jnp.float32)).astype(jnp.int32)
        over = over + (end - begin > rows).astype(jnp.int32)
        begin = jnp.minimum(begin, LANES)
        aligned = pl.multiple_of((begin // SUB) * SUB, SUB)
        back = lax.rem(reach - (begin - aligned), reach)
        here = pl.ds(aligned, reach)
        dest, w = divmod(b, windows)
        taken = pltpu.roll(key_rows[here, :], back, axis=0)[:rows]
        send_ref[dest, w * rows:(w + 1) * rows, :] = taken - float(b * span)
        at = (windows + w) * rows
        send_ref[dest, at:at + rows, :] = pltpu.roll(val_rows[here, :], back, axis=0)[:rows]
    flag_ref[0, 0] = over


def filter_and_sort(scan, resp, cycle, column, det_count, band_cycles):
    lines, length = scan.shape
    tiles = length // LANES
    windows = WINDOWS
    buckets = det_count * windows
    span = band_cycles * NPHI // buckets
    row_len = tiles * SUB
    rows = LANES // buckets + 2
    reach = (rows + 2 * SUB - 2) // SUB * SUB
    twiddle, forward, back = filter_tables(length)
    resp_rows = resp.reshape(lines, LANES, tiles).transpose(2, 0, 1).reshape(tiles * lines, LANES)
    body = functools.partial(sort_kernel, buckets=buckets, span=span, rows=rows, windows=windows)
    vmem = pl.BlockSpec(memory_space=pltpu.VMEM)
    return pl.pallas_call(
        body,
        out_shape=(
            jax.ShapeDtypeStruct((lines, length), jnp.float32),
            jax.ShapeDtypeStruct((det_count, 2 * windows * rows, row_len), jnp.float32),
            jax.ShapeDtypeStruct((1, 1), jnp.int32),
        ),
        in_specs=[vmem] * 7,
        out_specs=(vmem, vmem, pl.BlockSpec(memory_space=pltpu.SMEM)),
        scratch_shapes=[
            pltpu.VMEM((tiles, SUB, LANES), jnp.float32),
            pltpu.VMEM((tiles, SUB, LANES), jnp.float32),
            pltpu.VMEM((tiles * lines, 2 * LANES), jnp.float32),
            pltpu.VMEM((LANES + reach, row_len), jnp.float32),
            pltpu.VMEM((LANES + reach, row_len), jnp.float32),
        ],
        compiler_params=pltpu.CompilerParams(vmem_limit_bytes=24 * 1024 * 1024),
        name="filter_sort",
    )(scan, resp_rows, cycle, column, jnp.asarray(twiddle), jnp.asarray(forward), jnp.asarray(back))


def split2(x):
    high = x.astype(jnp.bfloat16)
    low = (x - high.astype(jnp.float32)).astype(jnp.bfloat16)
    return high, low


def bin_kernel(recv_ref, pick_ref, table_hi, table_lo, map_ref, send_ref, *, windows, rows, window_cycles):
    sources = recv_ref.shape[0]
    row_len = recv_ref.shape[2]
    parts = NPHI // ROW
    area = parts * window_cycles
    for w in range(windows):
        def body(e, acc):
            left, right = [], []
            a_iota = lax.broadcasted_iota(jnp.int32, (area, row_len), 0)
            b_iota = lax.broadcasted_iota(jnp.int32, (ROW, row_len), 0)
            for r in range(rows):
                q = recv_ref[e, w * rows + r:w * rows + r + 1, :].astype(jnp.int32)
                v = recv_ref[e, (windows + w) * rows + r:(windows + w) * rows + r + 1, :]
                high, low = split2(v)
                cycle = q >> 11
                inside = (q >= 0) & (cycle < window_cycles)
                a = jnp.where(inside, ((q >> 8) & (parts - 1)) * window_cycles + cycle, -1)
                hit_a = a_iota == a
                zero = jnp.zeros((), jnp.float32)
                left.append(jnp.concatenate([
                    jnp.where(hit_a, high.astype(jnp.float32), zero).astype(jnp.bfloat16),
                    jnp.where(hit_a, low.astype(jnp.float32), zero).astype(jnp.bfloat16),
                    jnp.where(hit_a, 1.0, zero).astype(jnp.bfloat16),
                ], axis=0))
                right.append(jnp.where(b_iota == (q & (ROW - 1)), 1.0, zero).astype(jnp.bfloat16))
            return acc + lax.dot_general(
                jnp.concatenate(left, axis=1), jnp.concatenate(right, axis=1), NT,
                preferred_element_type=jnp.float32,
            )

        acc = lax.fori_loop(0, sources, body, jnp.zeros((3 * area, ROW), jnp.float32))
        sky = (acc[:area] + acc[area:2 * area]) / jnp.maximum(acc[2 * area:], 1.0)
        for c8 in range(parts):
            map_ref[w * window_cycles:(w + 1) * window_cycles, c8 * ROW:(c8 + 1) * ROW] = (
                sky[c8 * window_cycles:(c8 + 1) * window_cycles]
            )
    cycles = map_ref.shape[0]
    half = NPHI // 2
    modes = []
    for parity in (0, 1):
        a, b = map_ref[:, :half], map_ref[:, half:]
        high, low = split2(a + b if parity == 0 else a - b)
        first = jnp.dot(jnp.concatenate([high, low], axis=0), table_hi[parity], preferred_element_type=jnp.float32)
        second = jnp.dot(high, table_lo[parity], preferred_element_type=jnp.float32)
        modes.append(first[:cycles] + first[cycles:] + second)
    modes = jnp.concatenate(modes, axis=1)
    count = modes.shape[1]
    width = pick_ref.shape[1]
    high = modes.astype(jnp.bfloat16)
    rest = modes - high.astype(jnp.float32)
    middle = rest.astype(jnp.bfloat16)
    low = (rest - middle.astype(jnp.float32)).astype(jnp.bfloat16)
    pieces = jnp.concatenate([high, middle, low], axis=0)
    choose = (lax.broadcasted_iota(jnp.int32, (count, width), 0) == pick_ref[...])
    choose = jnp.where(choose, 1.0, 0.0).astype(jnp.bfloat16)
    moved = jnp.dot(pieces, choose, preferred_element_type=jnp.float32)
    moved = moved[:cycles] + moved[cycles:2 * cycles] + moved[2 * cycles:]
    owners, group_rows, lanes = send_ref.shape
    groups = cycles // group_rows
    lane_group = lax.broadcasted_iota(jnp.int32, (group_rows, lanes), 1) // (lanes // groups)
    for d in range(owners):
        block = moved[:, d * lanes:(d + 1) * lanes]
        out = block[:group_rows]
        for h in range(1, groups):
            out = jnp.where(lane_group == h, block[h * group_rows:(h + 1) * group_rows], out)
        send_ref[d] = out


def bin_and_modes(recv, order_slot, band_cycles):
    sources, lines, row_len = recv.shape
    windows = WINDOWS
    rows = lines // (2 * windows)
    cycles = band_cycles // sources
    count = order_slot.shape[0]
    slots = count // sources
    groups = LANES // (2 * slots)
    high, low = mode_tables(count)
    m = order_slot.reshape(sources, 1, 1, slots)
    part = jnp.arange(2, dtype=jnp.int32).reshape(1, 1, 2, 1)
    pick = (m & 1) * count + part * (count // 2) + (m >> 1)
    pick = jnp.broadcast_to(pick, (sources, groups, 2, slots)).reshape(1, sources * LANES)
    vmem = pl.BlockSpec(memory_space=pltpu.VMEM)
    return pl.pallas_call(
        functools.partial(bin_kernel, windows=windows, rows=rows, window_cycles=cycles // windows),
        out_shape=(
            jax.ShapeDtypeStruct((cycles, NPHI), jnp.float32),
            jax.ShapeDtypeStruct((sources, cycles // groups, LANES), jnp.float32),
        ),
        in_specs=[vmem] * 4,
        out_specs=(vmem, vmem),
        compiler_params=pltpu.CompilerParams(vmem_limit_bytes=40 * 1024 * 1024),
        name="bin_modes",
    )(recv, pick, jnp.asarray(high), jnp.asarray(low))


def legendre_kernel(order_ref, recv_ref, leg_ref, out_ref, modes_ref, *, per_step):
    slots = out_ref.shape[1] // 2
    sources, group_rows, lanes = recv_ref.shape
    groups = lanes // (2 * slots)
    band_cycles, degrees = leg_ref.shape[1:]
    step = pl.program_id(0)

    @pl.when(step == 0)
    def _():
        for e in range(sources):
            block = recv_ref[e]
            for h in range(groups):
                at = (e * groups + h) * group_rows
                turned = block if h == 0 else pltpu.roll(block, lanes - h * 2 * slots, axis=1)
                modes_ref[at:at + group_rows, :] = turned

    chunk = 32
    for i in range(per_step):
        slot = step * per_step + i

        def body(n, acc):
            here = pl.ds(pl.multiple_of(n * chunk, chunk), chunk)
            turned = pltpu.roll(modes_ref[here, :], lanes - slot, axis=1)
            leg = leg_ref[i, here, :]
            real, imag = acc
            for r in range(0, chunk, SUB):
                block = leg[r:r + SUB]
                real = real + block * turned[r:r + SUB, 0:1]
                imag = imag + block * turned[r:r + SUB, slots:slots + 1]
            return real, imag

        zero = jnp.zeros((SUB, degrees), jnp.float32)
        sums = lax.fori_loop(0, band_cycles // chunk, body, (zero, zero))
        keep = lax.broadcasted_iota(jnp.int32, (1, degrees), 1) >= order_ref[slot]
        owners, _, width = out_ref.shape
        for c in range(2):
            line = jnp.where(keep, jnp.sum(sums[c], axis=0, keepdims=True), 0.0)
            for d in range(owners):
                out_ref[d, pl.ds(c * slots + slot, 1), :] = line[:, d * width:(d + 1) * width]


def legendre_sums(recv, local_orders, legendre, owners):
    slots, band_cycles, degrees = legendre.shape
    per_step = 2
    vmem = pl.BlockSpec(memory_space=pltpu.VMEM)
    return pl.pallas_call(
        functools.partial(legendre_kernel, per_step=per_step),
        grid=(slots // per_step,),
        out_shape=jax.ShapeDtypeStruct((owners, 2 * slots, degrees // owners), jnp.float32),
        in_specs=[
            pl.BlockSpec(memory_space=pltpu.SMEM),
            vmem,
            pl.BlockSpec((per_step, band_cycles, degrees), lambda s: (s, 0, 0)),
        ],
        out_specs=vmem,
        scratch_shapes=[pltpu.VMEM((band_cycles, LANES), jnp.float32)],
        compiler_params=pltpu.CompilerParams(vmem_limit_bytes=24 * 1024 * 1024),
        name="legendre_sums",
    )(local_orders, recv, legendre)


def dense_path(filtered, cycle_offset, column, order_slot, legendre):
    band_cycles = legendre.shape[1]
    flat_index = (cycle_offset * NPHI + column).reshape(-1)
    empty = jnp.zeros((band_cycles * NPHI,), jnp.float32)
    partial_value = empty.at[flat_index].add(filtered.reshape(-1)).reshape(band_cycles, NPHI)
    counts = empty.at[flat_index].add(1.0).reshape(band_cycles, NPHI)
    summed = lax.psum_scatter(partial_value, "det", scatter_dimension=0, tiled=True)
    hit_total = lax.psum_scatter(counts, "det", scatter_dimension=0, tiled=True)
    sky_map = summed / jnp.maximum(hit_total, 1.0)
    pixel_index = jnp.arange(NPHI, dtype=jnp.int32)[:, None]
    phases = 2.0 * jnp.pi / NPHI * (pixel_index * order_slot[None, :] % NPHI).astype(jnp.float32)
    cycle_modes = jnp.stack([
        jnp.dot(sky_map, jnp.cos(phases), precision=precise),
        -jnp.dot(sky_map, jnp.sin(phases), precision=precise),
    ])
    slot_count, _, degrees = legendre.shape
    local_orders = lax.dynamic_slice_in_dim(order_slot, lax.axis_index("det") * slot_count, slot_count, 0)
    keep = jnp.arange(degrees, dtype=jnp.int32)[None, :] >= local_orders[:, None]
    terms = jnp.einsum(
        "crs,srl->csl",
        lax.all_to_all(cycle_modes, "det", split_axis=2, concat_axis=1, tiled=True),
        legendre,
        precision=precise,
    ) * keep.astype(jnp.float32)[None]
    return lax.psum_scatter(terms, "band", scatter_dimension=2, tiled=True), sky_map


def local(scan_lines, response, cycle_offset, column, order_slot, legendre, *, det_count, band_count):
    slots, band_cycles, degrees = legendre.shape
    filtered, send, flag = filter_and_sort(
        scan_lines, response, cycle_offset, column, det_count, band_cycles
    )
    crowded = lax.pmax(flag[0, 0], ("det", "band"))
    recv = lax.all_to_all(send, "det", split_axis=0, concat_axis=0, tiled=True)
    sky_map, modes = bin_and_modes(recv, order_slot, band_cycles)
    modes = lax.all_to_all(modes, "det", split_axis=0, concat_axis=0, tiled=True)
    local_orders = lax.dynamic_slice_in_dim(order_slot, lax.axis_index("det") * slots, slots, 0)
    terms = legendre_sums(modes, local_orders, legendre, band_count)
    terms = lax.all_to_all(terms, "band", split_axis=0, concat_axis=0, tiled=True)
    harmonics = jnp.sum(terms, axis=0).reshape(2, slots, degrees // band_count)
    return lax.cond(
        crowded > 0,
        lambda: dense_path(filtered, cycle_offset, column, order_slot, legendre),
        lambda: (harmonics, sky_map),
    )


def solution(mesh):
    sizes = dict(mesh.shape)
    return jax.shard_map(
        functools.partial(local, det_count=sizes["det"], band_count=sizes["band"]),
        mesh=mesh,
        in_specs=(
            P(("det", "band"), None),
            P(("det", "band"), None),
            P(("det", "band"), None),
            P(("det", "band"), None),
            P(),
            P("det", "band", None),
        ),
        out_specs=(P(None, "det", "band"), P(("band", "det"), None)),
        check_vma=False,
    )
```

time: 531 us -> 160 us (0.30); the launches traced: 524 us -> 159 us
  other arithmetic: 345 us -> 0.78 us
  Pallas kernels: 0 us -> 68.3 us
  waiting for transfers between devices: 67.1 us -> 15.9 us
  matrix products: 45.7 us -> 0 us
  local copies, waits for them, and re-layouts: 47.4 us -> 5.94 us
  blocking collectives: 0 us -> 40.1 us
  starting transfers between devices: 3.47 us -> 13.4 us
    scatter-add x2 -> x0, other arithmetic: 343 us -> none  [the longest x1 172 us: local(): partial_value = jnp.zeros((band_cycles * NPHI,), jnp.float32).at[flat_ind...]
    pallas_call x0 -> x3, Pallas kernels: none -> 68.3 us  [the longest x1 43.8 us: legendre_sums(): pl.pallas_call(functools.partial(legendre_kernel, per_step=per_step), gri...]
    dot_general x15 -> x0, matrix products: 45.7 us -> none  [the longest x1 22 us: local(): jnp.einsum('crs,srl->csl', lax.all_to_all(cycle_modes, 'det', split_axis=...]
    pmax x0 -> x1, blocking collectives: none -> 40.1 us  [local(): crowded = lax.pmax(flag[0, 0], ('det', 'band'))]
    reduce_scatter x2 -> x0, waiting for transfers between devices: 37.9 us -> none  [the longest x1 37.9 us: local(): lax.psum_scatter(counts, 'det', scatter_dimension=0, tiled=True)]
    unnamed x17 -> x20, local copies, waits for them, and re-layouts: 41.7 us -> 4.21 us
    unnamed x4 -> x0, waiting for transfers between devices: 23.5 us -> none
    all_to_all x1 -> x3, waiting for transfers between devices: 5.72 us -> 15.9 us  [the longest x1 10.1 us: local(): recv = lax.all_to_all(send, 'det', split_axis=0, concat_axis=0, tiled=True)]
  transfers between devices with their start and end apart: 4 -> 3, of which waited for: 3 -> 2; matrix products, arithmetic and copies ran while one was open for 33% -> 1% of each run, Pallas kernels for 0% -> 0%
where the time goes in v1:
time: 160 us; the launch traced here: 159 us
  Pallas kernels  68.3 us (43%)
  blocking collectives  40.1 us (25%)
  waiting for transfers between devices  15.9 us (10%)
  between operations  14.8 us (9%)
  starting transfers between devices  13.4 us (8%)
  local copies, waits for them, and re-layouts  5.94 us (4%)
    pallas_call x1, Pallas kernels, legendre_sums(): pl.pallas_call(functools.partial(legendre_kernel, per_step=per_step), gri...  43.8 us
    pmax x1, blocking collectives, local(): crowded = lax.pmax(flag[0, 0], ('det', 'band'))  40.1 us
    pallas_call x1, Pallas kernels, bin_and_modes(): pl.pallas_call(functools.partial(bin_kernel, windows=windows, rows=rows,...  14 us
    pallas_call x1, Pallas kernels, filter_and_sort(): pl.pallas_call(body, out_shape=(jax.ShapeDtypeStruct((lines, length), jnp...  10.6 us
    all_to_all x1, waiting for transfers between devices, local(): recv = lax.all_to_all(send, 'det', split_axis=0, concat_axis=0, tiled=True)  10.1 us
    all_to_all x1, starting transfers between devices, local(): recv = lax.all_to_all(send, 'det', split_axis=0, concat_axis=0, tiled=True)  6.34 us
    all_to_all x1, waiting for transfers between devices, local(): lax.all_to_all(modes, 'det', split_axis=0, concat_axis=0, tiled=True)  5.75 us
    unnamed x20, local copies, waits for them, and re-layouts  4.21 us
  transfers between devices with their start and end apart: 3, of which 2 were waited for; matrix products, arithmetic and copies ran while one was open for 1% of the time, Pallas kernels for 0%

profile of v1, /device:TPU:0, one launch (start us, length us, event | category | flops | bytes accessed | tf_op | source)
XLA Modules:
  0.0 159.4 jit_solution(6541630492924891077)
XLA Ops:
  7.2 0.0 copy-start
  7.2 1.2 reshape.116
  8.4 0.2 copy.25
  8.6 0.9 copy-done.2
  9.6 0.9 copy-done.3
  10.5 0.9 copy-done.4
  11.4 0.8 copy-done.5
  12.2 10.6 %filter_sort.1 = (f32[8,4096]{1,0:T(8,128)S(1)}, f32[8,40,256]{2,1,0:T(8,128)}, s32[1,1]{1,0:T(1,128)}) custom-call(f32[8,4096]{1,0:T(8,128)S(1)} %copy-done.4, f32[256,128]{1,0:T(8,128)S(1)} %bitcast.35, s32[8,4096]{1,0:T(8,128)} %cycle_ref.1, s32[8,4096]{1,0:T(8,128)} %column_ref.1, f32[2,32,1,128]{3,2,1,0:T(1,128)S(1)} %copy-done.5, ...), custom_call_target="tpu_custom_call" | custom-call | tf_op jit(solution)/shard_map/filter_sort/pallas_call | solution.py:261
  22.8 6.3 %all-to-all-start.1 = ((f32[8,40,256]{2,1,0:T(8,128)}), f32[8,40,256]{2,1,0:T(8,128)S(1)}, u32[]{:S(2)}, u32[]{:S(2)}) async-start(f32[8,40,256]{2,1,0:T(8,128)} %get-tuple-element.34), calls=%async_computation.4 | async-start | bytes 655360 | tf_op jit(solution)/shard_map/all_to_all | solution.py:477
  29.1 0.7 and_multiply_fusion
  29.8 0.1 mul.61
  29.9 0.1 shift_right_arithmetic.12
  29.9 0.1 add_add_fusion
  30.0 0.1 reshape.118.pick_ref
  30.1 10.1 %all-to-all-done.1.recv_ref = f32[8,40,256]{2,1,0:T(8,128)S(1)} async-done(((f32[8,40,256]{2,1,0:T(8,128)}), f32[8,40,256]{2,1,0:T(8,128)S(1)}, u32[]{:S(2)}, u32[]{:S(2)}) %all-to-all-start.1) | async-done | bytes 327712 | tf_op jit(solution)/shard_map/all_to_all | solution.py:477
  40.2 14.0 %bin_modes.1 = (f32[32,2048]{1,0:T(8,128)}, f32[8,16,128]{2,1,0:T(8,128)}) custom-call(f32[8,40,256]{2,1,0:T(8,128)S(1)} %all-to-all-done.1.recv_ref, s32[1,1024]{1,0:T(1,128)S(1)} %reshape.118.pick_ref, bf16[2,1024,256]{2,1,0:T(8,128)(2,1)S(1)} %copy-done.1, bf16[2,1024,256]{2,1,0:T(8,128)(2,1)S(1)} %copy-done), custom_call_target="tpu_custom_call" | custom-call | tf_op jit(solution)/shard_map/bin_modes/pallas_call | solution.py:370
  54.2 3.4 %all-to-all-start.2 = ((f32[8,16,128]{2,1,0:T(8,128)}), f32[8,16,128]{2,1,0:T(8,128)S(1)}, u32[]{:S(2)}, u32[]{:S(2)}) async-start(f32[8,16,128]{2,1,0:T(8,128)} %get-tuple-element.35), calls=%async_computation.5 | async-start | bytes 131072 | tf_op jit(solution)/shard_map/all_to_all | solution.py:479
  57.6 0.1 dynamic_slice.6.order_ref
  57.7 5.8 %all-to-all-done.2.recv_ref = f32[8,16,128]{2,1,0:T(8,128)S(1)} async-done(((f32[8,16,128]{2,1,0:T(8,128)}), f32[8,16,128]{2,1,0:T(8,128)S(1)}, u32[]{:S(2)}, u32[]{:S(2)}) %all-to-all-start.2) | async-done | bytes 65568 | tf_op jit(solution)/shard_map/all_to_all | solution.py:479
  63.4 43.8 %legendre_sums.1 = f32[4,64,256]{2,1,0:T(8,128)} custom-call(s32[32]{0:T(128)S(1)} %dynamic_slice.6.order_ref, f32[8,16,128]{2,1,0:T(8,128)S(1)} %all-to-all-done.2.recv_ref, f32[32,256,1024]{2,1,0:T(8,128)} %leg_ref.1), custom_call_target="tpu_custom_call" | custom-call | tf_op jit(solution)/shard_map/legendre_sums/pallas_call | solution.py:428
  107.2 3.7 %all-to-all-start.3 = ((f32[4,64,256]{2,1,0:T(8,128)}), f32[4,64,256]{2,1,0:T(8,128)S(1)}, u32[]{:S(2)}, u32[]{:S(2)}) async-start(f32[4,64,256]{2,1,0:T(8,128)} %legendre_sums.1), calls=%async_computation.6 | async-start | bytes 524288 | tf_op jit(solution)/shard_map/all_to_all | solution.py:482
  110.9 40.1 %pmax.7 = s32[]{:T(128)} all-reduce(s32[]{:T(128)} %bitcast.9), channel_id=1, replica_groups=mesh['det'=8,'band'=4] {'det','band'}, use_global_device_ids=true, to_apply=%region_0.0 | all-reduce | flops 1 | bytes 8 | tf_op jit(solution)/shard_map/pmax | solution.py:476
  151.7 0.3 conditional.1
  152.0 0.6 copy-done.8
  (18 shorter events, 0.1 us)
Async XLA Ops:
  7.2 33.1 %copy-start = (bf16[2,1024,256]{2,1,0:T(8,128)(2,1)S(1)}, bf16[2,1024,256]{2,1,0:T(8,128)(2,1)}, u32[]{:S(2)}) copy-start(bf16[2,1024,256]{2,1,0:T(8,128)(2,1)} %constant.71.clone.table_lo) | copy-start | bytes 3145732
  7.2 33.1 %copy-start.1 = (bf16[2,1024,256]{2,1,0:T(8,128)(2,1)S(1)}, bf16[2,1024,256]{2,1,0:T(8,128)(2,1)}, u32[]{:S(2)}) copy-start(bf16[2,1024,256]{2,1,0:T(8,128)(2,1)} %constant.70.clone.table_hi) | copy-start | bytes 3145732
  8.6 1.0 copy-start.2
  9.6 0.9 copy-start.3
  10.5 0.9 copy-start.4
  11.4 0.8 copy-start.5
  12.2 45.4 %copy-start.9 = (s32[256]{0:T(256)S(1)}, s32[256]{0:T(256)}, u32[]{:S(2)}) copy-start(s32[256]{0:T(256)} %param.17) | copy-start | bytes 3076
  22.8 17.5 %all-to-all-start.1 = ((f32[8,40,256]{2,1,0:T(8,128)}), f32[8,40,256]{2,1,0:T(8,128)S(1)}, u32[]{:S(2)}, u32[]{:S(2)}) async-start(f32[8,40,256]{2,1,0:T(8,128)} %get-tuple-element.34), calls=%async_computation.4 | async-start | bytes 655360 | tf_op jit(solution)/shard_map/all_to_all | solution.py:477
  54.2 9.2 %all-to-all-start.2 = ((f32[8,16,128]{2,1,0:T(8,128)}), f32[8,16,128]{2,1,0:T(8,128)S(1)}, u32[]{:S(2)}, u32[]{:S(2)}) async-start(f32[8,16,128]{2,1,0:T(8,128)} %get-tuple-element.35), calls=%async_computation.5 | async-start | bytes 131072 | tf_op jit(solution)/shard_map/all_to_all | solution.py:479
  57.7 94.0 %copy-start.6 = (s32[8,4096]{1,0:T(8,128)S(1)}, s32[8,4096]{1,0:T(8,128)}, u32[]{:S(2)}) copy-start(s32[8,4096]{1,0:T(8,128)} %cycle_ref.1) | copy-start | bytes 393220
  57.7 94.0 %copy-start.7 = (s32[8,4096]{1,0:T(8,128)S(1)}, s32[8,4096]{1,0:T(8,128)}, u32[]{:S(2)}) copy-start(s32[8,4096]{1,0:T(8,128)} %column_ref.1) | copy-start | bytes 393220
  107.2 44.5 %all-to-all-start.3 = ((f32[4,64,256]{2,1,0:T(8,128)}), f32[4,64,256]{2,1,0:T(8,128)S(1)}, u32[]{:S(2)}, u32[]{:S(2)}) async-start(f32[4,64,256]{2,1,0:T(8,128)} %legendre_sums.1), calls=%async_computation.6 | async-start | bytes 524288 | tf_op jit(solution)/shard_map/all_to_all | solution.py:482
  151.9 0.6 copy-start.8

commit v2 on v1

--- a/solution.py
+++ b/solution.py
@@ -183,7 +183,7 @@
 
 def sort_kernel(
     scan_ref, resp_ref, cycle_ref, column_ref, twiddle_ref, forward_ref, back_ref,
-    filtered_ref, send_ref, flag_ref,
+    filtered_ref, send_ref,
     key_ref, val_ref, spec_ref, key_rows, val_rows,
     *, buckets, span, rows, windows,
 ):
@@ -242,7 +242,10 @@
         send_ref[dest, w * rows:(w + 1) * rows, :] = taken - float(b * span)
         at = (windows + w) * rows
         send_ref[dest, at:at + rows, :] = pltpu.roll(val_rows[here, :], back, axis=0)[:rows]
-    flag_ref[0, 0] = over
+
+    @pl.when(over > 0)
+    def _():
+        send_ref[...] = jnp.full(send_ref.shape, jnp.nan, jnp.float32)
 
 
 def filter_and_sort(scan, resp, cycle, column, det_count, band_cycles):
@@ -263,10 +266,9 @@
         out_shape=(
             jax.ShapeDtypeStruct((lines, length), jnp.float32),
             jax.ShapeDtypeStruct((det_count, 2 * windows * rows, row_len), jnp.float32),
-            jax.ShapeDtypeStruct((1, 1), jnp.int32),
         ),
         in_specs=[vmem] * 7,
-        out_specs=(vmem, vmem, pl.BlockSpec(memory_space=pltpu.SMEM)),
+        out_specs=(vmem, vmem),
         scratch_shapes=[
             pltpu.VMEM((tiles, SUB, LANES), jnp.float32),
             pltpu.VMEM((tiles, SUB, LANES), jnp.float32),
@@ -345,12 +347,14 @@
     owners, group_rows, lanes = send_ref.shape
     groups = cycles // group_rows
     lane_group = lax.broadcasted_iota(jnp.int32, (group_rows, lanes), 1) // (lanes // groups)
+    values = recv_ref[:, windows * rows:, :]
+    broken = jnp.max(jnp.where(values == values, 0.0, 1.0)) > 0.0
     for d in range(owners):
         block = moved[:, d * lanes:(d + 1) * lanes]
         out = block[:group_rows]
         for h in range(1, groups):
             out = jnp.where(lane_group == h, block[h * group_rows:(h + 1) * group_rows], out)
-        send_ref[d] = out
+        send_ref[d] = jnp.where(broken, jnp.nan, out)
 
 
 def bin_and_modes(recv, order_slot, band_cycles):
@@ -380,75 +384,90 @@
     )(recv, pick, jnp.asarray(high), jnp.asarray(low))
 
 
-def legendre_kernel(order_ref, recv_ref, leg_ref, out_ref, modes_ref, *, per_step):
-    slots = out_ref.shape[1] // 2
+def legendre_kernel(recv_ref, table_ref, out_ref, leg_ref, arrived, modes_ref, wide_ref):
+    slots, band_cycles, degrees = table_ref.shape
+
+    def load(slot):
+        return pltpu.make_async_copy(table_ref.at[slot], leg_ref.at[slot], arrived.at[slot])
+
+    def start(slot, carry):
+        load(slot).start()
+        return carry
+
+    lax.fori_loop(0, slots, start, 0)
     sources, group_rows, lanes = recv_ref.shape
     groups = lanes // (2 * slots)
-    band_cycles, degrees = leg_ref.shape[1:]
-    step = pl.program_id(0)
-
-    @pl.when(step == 0)
-    def _():
-        for e in range(sources):
-            block = recv_ref[e]
-            for h in range(groups):
-                at = (e * groups + h) * group_rows
-                turned = block if h == 0 else pltpu.roll(block, lanes - h * 2 * slots, axis=1)
-                modes_ref[at:at + group_rows, :] = turned
-
-    chunk = 32
-    for i in range(per_step):
-        slot = step * per_step + i
-
-        def body(n, acc):
-            here = pl.ds(pl.multiple_of(n * chunk, chunk), chunk)
-            turned = pltpu.roll(modes_ref[here, :], lanes - slot, axis=1)
-            leg = leg_ref[i, here, :]
-            real, imag = acc
-            for r in range(0, chunk, SUB):
-                block = leg[r:r + SUB]
-                real = real + block * turned[r:r + SUB, 0:1]
-                imag = imag + block * turned[r:r + SUB, slots:slots + 1]
-            return real, imag
-
-        zero = jnp.zeros((SUB, degrees), jnp.float32)
-        sums = lax.fori_loop(0, band_cycles // chunk, body, (zero, zero))
-        keep = lax.broadcasted_iota(jnp.int32, (1, degrees), 1) >= order_ref[slot]
-        owners, _, width = out_ref.shape
+    owners, _, width = out_ref.shape
+    tiles = degrees // LANES
+    for e in range(sources):
+        block = recv_ref[e]
+        for h in range(groups):
+            at = (e * groups + h) * group_rows
+            turned = block if h == 0 else pltpu.roll(block, lanes - h * 2 * slots, axis=1)
+            modes_ref[at:at + group_rows, :] = turned
+
+    def widen(slot, half):
+        turned = pltpu.roll(modes_ref[...], lax.rem(lanes - slot, lanes), axis=1)
         for c in range(2):
-            line = jnp.where(keep, jnp.sum(sums[c], axis=0, keepdims=True), 0.0)
+            column = turned[:, c * slots:c * slots + 1]
+            wide_ref[half, c] = jnp.broadcast_to(column, (band_cycles, lanes))
+
+    widen(0, 0)
+
+    def body(slot, carry):
+        half = slot & 1
+        load(slot).wait()
+        sums = [[jnp.zeros((SUB, LANES), jnp.float32) for _ in range(tiles)] for _ in range(2)]
+        for r in range(0, band_cycles, SUB):
+            factor = [wide_ref[half, c, r:r + SUB, :] for c in range(2)]
+            for t in range(tiles):
+                block = leg_ref[slot, r:r + SUB, t * LANES:(t + 1) * LANES]
+                for c in range(2):
+                    sums[c][t] = sums[c][t] + block * factor[c]
+        widen(jnp.minimum(slot + 1, slots - 1), 1 - half)
+        per_owner = width // LANES
+        for c in range(2):
+            lines = [jnp.sum(part, axis=0, keepdims=True) for part in sums[c]]
             for d in range(owners):
-                out_ref[d, pl.ds(c * slots + slot, 1), :] = line[:, d * width:(d + 1) * width]
-
-
-def legendre_sums(recv, local_orders, legendre, owners):
+                line = jnp.concatenate(lines[d * per_owner:(d + 1) * per_owner], axis=1)
+                out_ref[d, pl.ds(c * slots + slot, 1), :] = line
+        return carry
+
+    lax.fori_loop(0, slots, body, 0)
+
+
+def legendre_sums(recv, legendre, owners):
     slots, band_cycles, degrees = legendre.shape
-    per_step = 2
     vmem = pl.BlockSpec(memory_space=pltpu.VMEM)
     return pl.pallas_call(
-        functools.partial(legendre_kernel, per_step=per_step),
-        grid=(slots // per_step,),
+        legendre_kernel,
         out_shape=jax.ShapeDtypeStruct((owners, 2 * slots, degrees // owners), jnp.float32),
-        in_specs=[
-            pl.BlockSpec(memory_space=pltpu.SMEM),
-            vmem,
-            pl.BlockSpec((per_step, band_cycles, degrees), lambda s: (s, 0, 0)),
+        in_specs=[vmem, pl.BlockSpec(memory_space=pl.ANY)],
+        out_specs=vmem,
+        scratch_shapes=[
+            pltpu.VMEM(legendre.shape, jnp.float32),
+            pltpu.SemaphoreType.DMA((slots,)),
+            pltpu.VMEM((band_cycles, LANES), jnp.float32),
+            pltpu.VMEM((2, 2, band_cycles, LANES), jnp.float32),
         ],
-        out_specs=vmem,
-        scratch_shapes=[pltpu.VMEM((band_cycles, LANES), jnp.float32)],
-        compiler_params=pltpu.CompilerParams(vmem_limit_bytes=24 * 1024 * 1024),
+        compiler_params=pltpu.CompilerParams(vmem_limit_bytes=44 * 1024 * 1024),
         name="legendre_sums",
-    )(local_orders, recv, legendre)
-
-
-def dense_path(filtered, cycle_offset, column, order_slot, legendre):
+    )(recv, legendre)
+
+
+def exchange_and_sum(x, axis, count):
+    parts = x.reshape(count, x.shape[0] // count, x.shape[1])
+    return jnp.sum(lax.all_to_all(parts, axis, split_axis=0, concat_axis=0, tiled=True), axis=0)
+
+
+def dense_path(filtered, cycle_offset, column, order_slot, legendre, det_count, band_count):
     band_cycles = legendre.shape[1]
     flat_index = (cycle_offset * NPHI + column).reshape(-1)
     empty = jnp.zeros((band_cycles * NPHI,), jnp.float32)
     partial_value = empty.at[flat_index].add(filtered.reshape(-1)).reshape(band_cycles, NPHI)
     counts = empty.at[flat_index].add(1.0).reshape(band_cycles, NPHI)
-    summed = lax.psum_scatter(partial_value, "det", scatter_dimension=0, tiled=True)
-    hit_total = lax.psum_scatter(counts, "det", scatter_dimension=0, tiled=True)
+    summed = exchange_and_sum(partial_value, "det", det_count)
+    hit_total = exchange_and_sum(counts, "det", det_count)
     sky_map = summed / jnp.maximum(hit_total, 1.0)
     pixel_index = jnp.arange(NPHI, dtype=jnp.int32)[:, None]
     phases = 2.0 * jnp.pi / NPHI * (pixel_index * order_slot[None, :] % NPHI).astype(jnp.float32)
@@ -465,25 +484,32 @@
         legendre,
         precision=precise,
     ) * keep.astype(jnp.float32)[None]
-    return lax.psum_scatter(terms, "band", scatter_dimension=2, tiled=True), sky_map
+    harmonics = exchange_and_sum(terms.transpose(2, 0, 1).reshape(degrees, -1), "band", band_count)
+    return harmonics.reshape(-1, 2, slot_count).transpose(1, 2, 0), sky_map
 
 
 def local(scan_lines, response, cycle_offset, column, order_slot, legendre, *, det_count, band_count):
     slots, band_cycles, degrees = legendre.shape
-    filtered, send, flag = filter_and_sort(
+    filtered, send = filter_and_sort(
         scan_lines, response, cycle_offset, column, det_count, band_cycles
     )
-    crowded = lax.pmax(flag[0, 0], ("det", "band"))
     recv = lax.all_to_all(send, "det", split_axis=0, concat_axis=0, tiled=True)
     sky_map, modes = bin_and_modes(recv, order_slot, band_cycles)
     modes = lax.all_to_all(modes, "det", split_axis=0, concat_axis=0, tiled=True)
+    terms = legendre_sums(modes, legendre, band_count)
+    terms = lax.all_to_all(terms, "band", split_axis=0, concat_axis=0, tiled=True)
+    sums = jnp.sum(terms, axis=0)
+    crowded = jnp.isnan(sums[0, 0])
     local_orders = lax.dynamic_slice_in_dim(order_slot, lax.axis_index("det") * slots, slots, 0)
-    terms = legendre_sums(modes, local_orders, legendre, band_count)
-    terms = lax.all_to_all(terms, "band", split_axis=0, concat_axis=0, tiled=True)
-    harmonics = jnp.sum(terms, axis=0).reshape(2, slots, degrees // band_count)
+    width = degrees // band_count
+    degree = lax.axis_index("band") * width + jnp.arange(width, dtype=jnp.int32)
+    keep = degree[None, None, :] >= local_orders[None, :, None]
+    harmonics = jnp.where(keep, sums.reshape(2, slots, width), 0.0)
     return lax.cond(
-        crowded > 0,
-        lambda: dense_path(filtered, cycle_offset, column, order_slot, legendre),
+        crowded,
+        lambda: dense_path(
+            filtered, cycle_offset, column, order_slot, legendre, det_count, band_count
+        ),
         lambda: (harmonics, sky_map),
     )
 

time: 160 us -> 80 us (0.50)
  Pallas kernels: 68.3 us -> 36 us
  blocking collectives: 40.1 us -> 8.28 us
  between operations: 14.8 us -> 2.04 us
  starting transfers between devices: 13.4 us -> 10.1 us
    pmax x1 -> x0, blocking collectives: 40.1 us -> none  [local(): crowded = lax.pmax(flag[0, 0], ('det', 'band'))]
    pallas_call x1, Pallas kernels: 43.8 us -> 11.9 us  [legendre_sums(): pl.pallas_call(legendre_kernel, out_shape=jax.ShapeDtypeStruct((owners, 2...]
    all_to_all x0 -> x1, blocking collectives: none -> 8.28 us  [local(): lax.all_to_all(modes, 'det', split_axis=0, concat_axis=0, tiled=True)]
    all_to_all x1 -> x0, waiting for transfers between devices: 5.75 us -> none  [local(): lax.all_to_all(modes, 'det', split_axis=0, concat_axis=0, tiled=True)]
    all_to_all x1, waiting for transfers between devices: 0.01 us -> 5.37 us  [local(): lax.all_to_all(terms, 'band', split_axis=0, concat_axis=0, tiled=True)]
    all_to_all x1 -> x0, starting transfers between devices: 3.35 us -> none  [local(): lax.all_to_all(modes, 'det', split_axis=0, concat_axis=0, tiled=True)]
  transfers between devices with their start and end apart: 3 -> 2, of which waited for: 2 -> 2; matrix products, arithmetic and copies ran while one was open for 1% -> 1% of each run, Pallas kernels for 0% -> 0%
where the time goes in v2:
time: 80 us; the launch traced here: 79.5 us
  Pallas kernels  36 us (45%)
  waiting for transfers between devices  15.5 us (19%)
  starting transfers between devices  10.1 us (13%)
  blocking collectives  8.28 us (10%)
  local copies, waits for them, and re-layouts  6.46 us (8%)
  between operations  2.04 us (3%)
  other arithmetic  0.87 us (1%)
    pallas_call x1, Pallas kernels, bin_and_modes(): pl.pallas_call(functools.partial(bin_kernel, windows=windows, rows=rows,...  13.6 us
    pallas_call x1, Pallas kernels, legendre_sums(): pl.pallas_call(legendre_kernel, out_shape=jax.ShapeDtypeStruct((owners, 2...  11.9 us
    pallas_call x1, Pallas kernels, filter_and_sort(): pl.pallas_call(body, out_shape=(jax.ShapeDtypeStruct((lines, length), jnp...  10.6 us
    all_to_all x1, waiting for transfers between devices, local(): recv = lax.all_to_all(send, 'det', split_axis=0, concat_axis=0, tiled=True)  10.1 us
    all_to_all x1, blocking collectives, local(): lax.all_to_all(modes, 'det', split_axis=0, concat_axis=0, tiled=True)  8.28 us
    all_to_all x1, starting transfers between devices, local(): recv = lax.all_to_all(send, 'det', split_axis=0, concat_axis=0, tiled=True)  6.33 us
    all_to_all x1, waiting for transfers between devices, local(): lax.all_to_all(terms, 'band', split_axis=0, concat_axis=0, tiled=True)  5.37 us
    unnamed x20, local copies, waits for them, and re-layouts  4.21 us
  transfers between devices with their start and end apart: 2, of which 2 were waited for; matrix products, arithmetic and copies ran while one was open for 1% of the time, Pallas kernels for 0%

profile of v2, /device:TPU:0, one launch (start us, length us, event | category | flops | bytes accessed | tf_op | source)
XLA Modules:
  0.0 79.5 jit_solution(15152855589744000517)
XLA Ops:
  0.7 1.2 %reshape.161 = f32[8,128,32]{2,1,0:T(8,128)S(1)} reshape(f32[8,4096]{1,0:T(8,128)} %param.14) | data formatting | bytes 262144 | tf_op jit(solution)/shard_map/reshape | solution.py:261
  1.9 0.2 copy.30
  2.1 0.9 %copy-done.2 = f32[256,256]{1,0:T(8,128)S(1)} copy-done((f32[256,256]{1,0:T(8,128)S(1)}, f32[256,256]{1,0:T(8,128)}, u32[]{:S(2)}) %copy-start.2) | copy-done | bytes 262168
  3.0 0.9 %copy-done.3 = f32[256,256]{1,0:T(8,128)S(1)} copy-done((f32[256,256]{1,0:T(8,128)S(1)}, f32[256,256]{1,0:T(8,128)}, u32[]{:S(2)}) %copy-start.3) | copy-done | bytes 262168
  4.0 0.9 %copy-done.4 = f32[8,4096]{1,0:T(8,128)S(1)} copy-done((f32[8,4096]{1,0:T(8,128)S(1)}, f32[8,4096]{1,0:T(8,128)}, u32[]{:S(2)}) %copy-start.4) | copy-done | bytes 131096
  4.9 0.8 copy-done.5
  5.6 10.6 %filter_sort.1 = (f32[8,4096]{1,0:T(8,128)S(1)}, f32[8,40,256]{2,1,0:T(8,128)}) custom-call(f32[8,4096]{1,0:T(8,128)S(1)} %copy-done.4, f32[256,128]{1,0:T(8,128)S(1)} %bitcast.40, s32[8,4096]{1,0:T(8,128)} %cycle_ref.1, s32[8,4096]{1,0:T(8,128)} %column_ref.1, f32[2,32,1,128]{3,2,1,0:T(1,128)S(1)} %copy-done.5, f32[256,256]{1,0:T(8,128)S(1)} %copy-done.2, ...), custom_call_target="tpu_custom_call" | custom-call | tf_op jit(solution)/shard_map/filter_sort/pallas_call | solution.py:264
  16.2 6.3 %all-to-all-start.4 = ((f32[8,40,256]{2,1,0:T(8,128)}), f32[8,40,256]{2,1,0:T(8,128)S(1)}, u32[]{:S(2)}, u32[]{:S(2)}) async-start(f32[8,40,256]{2,1,0:T(8,128)} %get-tuple-element.65), calls=%async_computation.4 | async-start | bytes 655360 | tf_op jit(solution)/shard_map/all_to_all | solution.py:496
  22.5 0.7 and_multiply_fusion
  23.2 0.1 mul.63
  23.3 0.1 shift_right_arithmetic.12
  23.4 0.1 add_add_fusion
  23.5 0.1 reshape.163.pick_ref
  23.5 10.1 %all-to-all-done.4.recv_ref = f32[8,40,256]{2,1,0:T(8,128)S(1)} async-done(((f32[8,40,256]{2,1,0:T(8,128)}), f32[8,40,256]{2,1,0:T(8,128)S(1)}, u32[]{:S(2)}, u32[]{:S(2)}) %all-to-all-start.4) | async-done | bytes 327712 | tf_op jit(solution)/shard_map/all_to_all | solution.py:496
  33.7 13.6 %bin_modes.1 = (f32[32,2048]{1,0:T(8,128)}, f32[8,16,128]{2,1,0:T(8,128)S(1)}) custom-call(f32[8,40,256]{2,1,0:T(8,128)S(1)} %all-to-all-done.4.recv_ref, s32[1,1024]{1,0:T(1,128)S(1)} %reshape.163.pick_ref, bf16[2,1024,256]{2,1,0:T(8,128)(2,1)S(1)} %copy-done, bf16[2,1024,256]{2,1,0:T(8,128)(2,1)S(1)} %copy-done.1), custom_call_target="tpu_custom_call" | custom-call | tf_op jit(solution)/shard_map/bin_modes/pallas_call | solution.py:374
  47.3 8.3 %all_to_all.42.recv_ref = f32[8,16,128]{2,1,0:T(8,128)S(1)} all-to-all(f32[8,16,128]{2,1,0:T(8,128)S(1)} %get-tuple-element.66), channel_id=1, replica_groups=mesh['det'=8,'band'=4] {'det'}, dimensions={0} | all-to-all | bytes 131072 | tf_op jit(solution)/shard_map/all_to_all | solution.py:498
  55.6 11.9 %legendre_sums.1 = f32[4,64,256]{2,1,0:T(8,128)} custom-call(f32[8,16,128]{2,1,0:T(8,128)S(1)} %all_to_all.42.recv_ref, f32[32,256,1024]{2,1,0:T(8,128)} %table_ref.1), custom_call_target="tpu_custom_call" | custom-call | tf_op jit(solution)/shard_map/legendre_sums/pallas_call | solution.py:442
  67.5 3.7 %all-to-all-start.6 = ((f32[4,64,256]{2,1,0:T(8,128)}), f32[4,64,256]{2,1,0:T(8,128)S(1)}, u32[]{:S(2)}, u32[]{:S(2)}) async-start(f32[4,64,256]{2,1,0:T(8,128)} %legendre_sums.1), calls=%async_computation.6 | async-start | bytes 524288 | tf_op jit(solution)/shard_map/all_to_all | solution.py:500
  71.2 5.4 %all-to-all-done.6 = f32[4,64,256]{2,1,0:T(8,128)S(1)} async-done(((f32[4,64,256]{2,1,0:T(8,128)}), f32[4,64,256]{2,1,0:T(8,128)S(1)}, u32[]{:S(2)}, u32[]{:S(2)}) %all-to-all-start.6) | async-done | bytes 262176 | tf_op jit(solution)/shard_map/all_to_all | solution.py:500
  76.6 0.5 slice.4
  78.4 0.4 conditional.1
  78.4 0.1 dynamic_slice.5
  78.5 0.1 broadcast_compare_fusion
  78.9 0.6 copy-done.8
  (21 shorter events, 0.1 us)
Async XLA Ops:
  0.6 33.0 %copy-start = (bf16[2,1024,256]{2,1,0:T(8,128)(2,1)S(1)}, bf16[2,1024,256]{2,1,0:T(8,128)(2,1)}, u32[]{:S(2)}) copy-start(bf16[2,1024,256]{2,1,0:T(8,128)(2,1)} %constant.77.clone.table_hi) | copy-start | bytes 3145732
  0.6 33.0 %copy-start.1 = (bf16[2,1024,256]{2,1,0:T(8,128)(2,1)S(1)}, bf16[2,1024,256]{2,1,0:T(8,128)(2,1)}, u32[]{:S(2)}) copy-start(bf16[2,1024,256]{2,1,0:T(8,128)(2,1)} %constant.78.clone.table_lo) | copy-start | bytes 3145732
  2.1 1.0 %copy-start.2 = (f32[256,256]{1,0:T(8,128)S(1)}, f32[256,256]{1,0:T(8,128)}, u32[]{:S(2)}) copy-start(f32[256,256]{1,0:T(8,128)} %constant.75.clone.forward_ref) | copy-start | bytes 786436
  3.0 0.9 %copy-start.3 = (f32[256,256]{1,0:T(8,128)S(1)}, f32[256,256]{1,0:T(8,128)}, u32[]{:S(2)}) copy-start(f32[256,256]{1,0:T(8,128)} %constant.76.clone.back_ref) | copy-start | bytes 786436
  4.0 0.9 %copy-start.4 = (f32[8,4096]{1,0:T(8,128)S(1)}, f32[8,4096]{1,0:T(8,128)}, u32[]{:S(2)}) copy-start(f32[8,4096]{1,0:T(8,128)} %scan_ref.1) | copy-start | bytes 393220
  4.9 0.8 copy-start.5
  16.2 17.5 %all-to-all-start.4 = ((f32[8,40,256]{2,1,0:T(8,128)}), f32[8,40,256]{2,1,0:T(8,128)S(1)}, u32[]{:S(2)}, u32[]{:S(2)}) async-start(f32[8,40,256]{2,1,0:T(8,128)} %get-tuple-element.65), calls=%async_computation.4 | async-start | bytes 655360 | tf_op jit(solution)/shard_map/all_to_all | solution.py:496
  55.5 22.9 %copy-start.6 = (s32[8,4096]{1,0:T(8,128)S(1)}, s32[8,4096]{1,0:T(8,128)}, u32[]{:S(2)}) copy-start(s32[8,4096]{1,0:T(8,128)} %cycle_ref.1) | copy-start | bytes 393220
  55.5 22.9 %copy-start.7 = (s32[8,4096]{1,0:T(8,128)S(1)}, s32[8,4096]{1,0:T(8,128)}, u32[]{:S(2)}) copy-start(s32[8,4096]{1,0:T(8,128)} %column_ref.1) | copy-start | bytes 393220
  55.6 22.9 %copy-start.9 = (s32[256]{0:T(256)S(1)}, s32[256]{0:T(256)}, u32[]{:S(2)}) copy-start(s32[256]{0:T(256)} %param.17) | copy-start | bytes 3076
  67.5 9.1 %all-to-all-start.6 = ((f32[4,64,256]{2,1,0:T(8,128)}), f32[4,64,256]{2,1,0:T(8,128)S(1)}, u32[]{:S(2)}, u32[]{:S(2)}) async-start(f32[4,64,256]{2,1,0:T(8,128)} %legendre_sums.1), calls=%async_computation.6 | async-start | bytes 524288 | tf_op jit(solution)/shard_map/all_to_all | solution.py:500
  78.8 0.6 copy-start.8

commit v3 on v2

--- a/solution.py
+++ b/solution.py
@@ -287,37 +287,60 @@
     return high, low
 
 
-def bin_kernel(recv_ref, pick_ref, table_hi, table_lo, map_ref, send_ref, *, windows, rows, window_cycles):
+def bin_kernel(
+    me_ref, recv_ref, pick_ref, table_hi, table_lo, map_ref, *refs, windows, rows, window_cycles
+):
+    send_refs, (blocks_ref, left_a, left_b, right_a, right_b, acc_ref) = refs[:-6], refs[-6:]
+    left_refs, right_refs = (left_a, left_b), (right_a, right_b)
     sources = recv_ref.shape[0]
     row_len = recv_ref.shape[2]
     parts = NPHI // ROW
     area = parts * window_cycles
+    a_iota = lax.broadcasted_iota(jnp.int32, (area, row_len), 0).astype(jnp.float32).astype(jnp.bfloat16)
+    b_iota = lax.broadcasted_iota(jnp.int32, (ROW, row_len), 0).astype(jnp.float32).astype(jnp.bfloat16)
+    zero, one = jnp.zeros((), jnp.bfloat16), jnp.ones((), jnp.bfloat16)
+
+    def build(e, w, slot):
+        left, right = left_refs[slot], right_refs[slot]
+        for r in range(rows):
+            q = recv_ref[e, w * rows + r:w * rows + r + 1, :].astype(jnp.int32)
+            v = recv_ref[e, (windows + w) * rows + r:(windows + w) * rows + r + 1, :]
+            high, low = split2(v)
+            cycle = q >> 11
+            inside = (q >= 0) & (cycle < window_cycles)
+            a = jnp.where(inside, ((q >> 8) & (parts - 1)) * window_cycles + cycle, -1)
+            a = a.astype(jnp.float32).astype(jnp.bfloat16)
+            b = (q & (ROW - 1)).astype(jnp.float32).astype(jnp.bfloat16)
+            cols = slice(r * row_len, (r + 1) * row_len)
+            hit = a_iota == a
+            left[:area, cols] = jnp.where(hit, high, zero)
+            left[area:2 * area, cols] = jnp.where(hit, low, zero)
+            left[2 * area:, cols] = jnp.where(hit, one, zero)
+            right[:, cols] = jnp.where(b_iota == b, one, zero)
+
+    def multiply(slot):
+        acc_ref[...] += lax.dot_general(
+            left_refs[slot][...], right_refs[slot][...], NT, preferred_element_type=jnp.float32
+        )
+
+    build(0, 0, 0)
     for w in range(windows):
-        def body(e, acc):
-            left, right = [], []
-            a_iota = lax.broadcasted_iota(jnp.int32, (area, row_len), 0)
-            b_iota = lax.broadcasted_iota(jnp.int32, (ROW, row_len), 0)
-            for r in range(rows):
-                q = recv_ref[e, w * rows + r:w * rows + r + 1, :].astype(jnp.int32)
-                v = recv_ref[e, (windows + w) * rows + r:(windows + w) * rows + r + 1, :]
-                high, low = split2(v)
-                cycle = q >> 11
-                inside = (q >= 0) & (cycle < window_cycles)
-                a = jnp.where(inside, ((q >> 8) & (parts - 1)) * window_cycles + cycle, -1)
-                hit_a = a_iota == a
-                zero = jnp.zeros((), jnp.float32)
-                left.append(jnp.concatenate([
-                    jnp.where(hit_a, high.astype(jnp.float32), zero).astype(jnp.bfloat16),
-                    jnp.where(hit_a, low.astype(jnp.float32), zero).astype(jnp.bfloat16),
-                    jnp.where(hit_a, 1.0, zero).astype(jnp.bfloat16),
-                ], axis=0))
-                right.append(jnp.where(b_iota == (q & (ROW - 1)), 1.0, zero).astype(jnp.bfloat16))
-            return acc + lax.dot_general(
-                jnp.concatenate(left, axis=1), jnp.concatenate(right, axis=1), NT,
-                preferred_element_type=jnp.float32,
-            )
-
-        acc = lax.fori_loop(0, sources, body, jnp.zeros((3 * area, ROW), jnp.float32))
+        acc_ref[...] = jnp.zeros(acc_ref.shape, jnp.float32)
+
+        def body(i, carry):
+            build(2 * i + 1, w, 1)
+            multiply(0)
+            build(jnp.minimum(2 * i + 2, sources - 1), w, 0)
+            multiply(1)
+            return carry
+
+        lax.fori_loop(0, sources // 2 - 1, body, 0)
+        build(sources - 1, w, 1)
+        multiply(0)
+        if w + 1 < windows:
+            build(0, w + 1, 0)
+        multiply(1)
+        acc = acc_ref[...]
         sky = (acc[:area] + acc[area:2 * area]) / jnp.maximum(acc[2 * area:], 1.0)
         for c8 in range(parts):
             map_ref[w * window_cycles:(w + 1) * window_cycles, c8 * ROW:(c8 + 1) * ROW] = (
@@ -344,7 +367,7 @@
     choose = jnp.where(choose, 1.0, 0.0).astype(jnp.bfloat16)
     moved = jnp.dot(pieces, choose, preferred_element_type=jnp.float32)
     moved = moved[:cycles] + moved[cycles:2 * cycles] + moved[2 * cycles:]
-    owners, group_rows, lanes = send_ref.shape
+    owners, group_rows, lanes = blocks_ref.shape
     groups = cycles // group_rows
     lane_group = lax.broadcasted_iota(jnp.int32, (group_rows, lanes), 1) // (lanes // groups)
     values = recv_ref[:, windows * rows:, :]
@@ -354,10 +377,12 @@
         out = block[:group_rows]
         for h in range(1, groups):
             out = jnp.where(lane_group == h, block[h * group_rows:(h + 1) * group_rows], out)
-        send_ref[d] = jnp.where(broken, jnp.nan, out)
-
-
-def bin_and_modes(recv, order_slot, band_cycles):
+        blocks_ref[d] = jnp.where(broken, jnp.nan, out)
+    for k in range(owners):
+        send_refs[k][...] = blocks_ref[me_ref[0] ^ k]
+
+
+def bin_and_modes(me, recv, order_slot, band_cycles):
     sources, lines, row_len = recv.shape
     windows = WINDOWS
     rows = lines // (2 * windows)
@@ -370,21 +395,33 @@
     part = jnp.arange(2, dtype=jnp.int32).reshape(1, 1, 2, 1)
     pick = (m & 1) * count + part * (count // 2) + (m >> 1)
     pick = jnp.broadcast_to(pick, (sources, groups, 2, slots)).reshape(1, sources * LANES)
+    area = cycles // windows * (NPHI // ROW)
+    depth = rows * row_len
     vmem = pl.BlockSpec(memory_space=pltpu.VMEM)
     return pl.pallas_call(
         functools.partial(bin_kernel, windows=windows, rows=rows, window_cycles=cycles // windows),
         out_shape=(
             jax.ShapeDtypeStruct((cycles, NPHI), jnp.float32),
-            jax.ShapeDtypeStruct((sources, cycles // groups, LANES), jnp.float32),
-        ),
-        in_specs=[vmem] * 4,
-        out_specs=(vmem, vmem),
+        ) + (jax.ShapeDtypeStruct((cycles // groups, LANES), jnp.float32),) * sources,
+        in_specs=[pl.BlockSpec(memory_space=pltpu.SMEM)] + [vmem] * 4,
+        out_specs=(vmem,) * (sources + 1),
+        scratch_shapes=[
+            pltpu.VMEM((sources, cycles // groups, LANES), jnp.float32),
+            pltpu.VMEM((3 * area, depth), jnp.bfloat16),
+            pltpu.VMEM((3 * area, depth), jnp.bfloat16),
+            pltpu.VMEM((ROW, depth), jnp.bfloat16),
+            pltpu.VMEM((ROW, depth), jnp.bfloat16),
+            pltpu.VMEM((3 * area, ROW), jnp.float32),
+        ],
         compiler_params=pltpu.CompilerParams(vmem_limit_bytes=40 * 1024 * 1024),
         name="bin_modes",
-    )(recv, pick, jnp.asarray(high), jnp.asarray(low))
-
-
-def legendre_kernel(recv_ref, table_ref, out_ref, leg_ref, arrived, modes_ref, wide_ref):
+    )(me, recv, pick, jnp.asarray(high), jnp.asarray(low))
+
+
+def legendre_kernel(me_ref, *refs, sources, owners):
+    recv_refs, table_ref = refs[:sources], refs[sources]
+    out_refs = refs[sources + 1:sources + 1 + owners]
+    leg_ref, arrived, modes_ref, wide_ref, block_ref, sums_ref = refs[sources + 1 + owners:]
     slots, band_cycles, degrees = table_ref.shape
 
     def load(slot):
@@ -395,16 +432,18 @@
         return carry
 
     lax.fori_loop(0, slots, start, 0)
-    sources, group_rows, lanes = recv_ref.shape
+    group_rows, lanes = recv_refs[0].shape
     groups = lanes // (2 * slots)
-    owners, _, width = out_ref.shape
+    width = out_refs[0].shape[1]
     tiles = degrees // LANES
-    for e in range(sources):
-        block = recv_ref[e]
+    cycles = group_rows * groups
+    for k in range(sources):
+        block = recv_refs[k][...]
         for h in range(groups):
-            at = (e * groups + h) * group_rows
             turned = block if h == 0 else pltpu.roll(block, lanes - h * 2 * slots, axis=1)
-            modes_ref[at:at + group_rows, :] = turned
+            block_ref[h * group_rows:(h + 1) * group_rows, :] = turned
+        at = pl.multiple_of((me_ref[0] ^ k) * cycles, cycles)
+        modes_ref[pl.ds(at, cycles), :] = block_ref[...]
 
     def widen(slot, half):
         turned = pltpu.roll(modes_ref[...], lax.rem(lanes - slot, lanes), axis=1)
@@ -430,29 +469,33 @@
             lines = [jnp.sum(part, axis=0, keepdims=True) for part in sums[c]]
             for d in range(owners):
                 line = jnp.concatenate(lines[d * per_owner:(d + 1) * per_owner], axis=1)
-                out_ref[d, pl.ds(c * slots + slot, 1), :] = line
+                sums_ref[d, pl.ds(c * slots + slot, 1), :] = line
         return carry
 
     lax.fori_loop(0, slots, body, 0)
-
-
-def legendre_sums(recv, legendre, owners):
+    for k in range(owners):
+        out_refs[k][...] = sums_ref[me_ref[1] ^ k]
+
+
+def legendre_sums(me, recv, legendre, owners):
     slots, band_cycles, degrees = legendre.shape
     vmem = pl.BlockSpec(memory_space=pltpu.VMEM)
     return pl.pallas_call(
-        legendre_kernel,
-        out_shape=jax.ShapeDtypeStruct((owners, 2 * slots, degrees // owners), jnp.float32),
-        in_specs=[vmem, pl.BlockSpec(memory_space=pl.ANY)],
-        out_specs=vmem,
+        functools.partial(legendre_kernel, sources=len(recv), owners=owners),
+        out_shape=(jax.ShapeDtypeStruct((2 * slots, degrees // owners), jnp.float32),) * owners,
+        in_specs=[pl.BlockSpec(memory_space=pltpu.SMEM)] + [vmem] * len(recv) + [pl.BlockSpec(memory_space=pl.ANY)],
+        out_specs=(vmem,) * owners,
         scratch_shapes=[
             pltpu.VMEM(legendre.shape, jnp.float32),
             pltpu.SemaphoreType.DMA((slots,)),
             pltpu.VMEM((band_cycles, LANES), jnp.float32),
             pltpu.VMEM((2, 2, band_cycles, LANES), jnp.float32),
+            pltpu.VMEM((band_cycles // len(recv), LANES), jnp.float32),
+            pltpu.VMEM((owners, 2 * slots, degrees // owners), jnp.float32),
         ],
         compiler_params=pltpu.CompilerParams(vmem_limit_bytes=44 * 1024 * 1024),
         name="legendre_sums",
-    )(recv, legendre)
+    )(me, *recv, legendre)
 
 
 def exchange_and_sum(x, axis, count):
@@ -488,17 +531,24 @@
     return harmonics.reshape(-1, 2, slot_count).transpose(1, 2, 0), sky_map
 
 
+def swap_blocks(blocks, axis):
+    count = len(blocks)
+    return [blocks[0]] + [
+        lax.ppermute(blocks[k], axis, [(i, i ^ k) for i in range(count)]) for k in range(1, count)
+    ]
+
+
 def local(scan_lines, response, cycle_offset, column, order_slot, legendre, *, det_count, band_count):
     slots, band_cycles, degrees = legendre.shape
     filtered, send = filter_and_sort(
         scan_lines, response, cycle_offset, column, det_count, band_cycles
     )
+    me = jnp.stack([lax.axis_index("det"), lax.axis_index("band")]).astype(jnp.int32)
     recv = lax.all_to_all(send, "det", split_axis=0, concat_axis=0, tiled=True)
-    sky_map, modes = bin_and_modes(recv, order_slot, band_cycles)
-    modes = lax.all_to_all(modes, "det", split_axis=0, concat_axis=0, tiled=True)
-    terms = legendre_sums(modes, legendre, band_count)
-    terms = lax.all_to_all(terms, "band", split_axis=0, concat_axis=0, tiled=True)
-    sums = jnp.sum(terms, axis=0)
+    sky_map, *modes = bin_and_modes(me, recv, order_slot, band_cycles)
+    modes = swap_blocks(modes, "det")
+    terms = swap_blocks(legendre_sums(me, modes, legendre, band_count), "band")
+    sums = functools.reduce(jnp.add, terms)
     crowded = jnp.isnan(sums[0, 0])
     local_orders = lax.dynamic_slice_in_dim(order_slot, lax.axis_index("det") * slots, slots, 0)
     width = degrees // band_count

time: 80 us -> 80.2 us (level)
  blocking collectives: 8.28 us -> 0 us
  starting transfers between devices: 10.1 us -> 17.9 us
  waiting for transfers between devices: 15.5 us -> 17.3 us
  Pallas kernels: 36 us -> 34.8 us
    ppermute x0 -> x10, starting transfers between devices: none -> 11.6 us  [swap_blocks(): lax.ppermute(blocks[k], axis, [(i, i ^ k) for i in range(count)])]
    all_to_all x1 -> x0, blocking collectives: 8.28 us -> none  [local(): lax.all_to_all(modes, 'det', split_axis=0, concat_axis=0, tiled=True)]
    ppermute x0 -> x10, waiting for transfers between devices: none -> 7.23 us  [swap_blocks(): lax.ppermute(blocks[k], axis, [(i, i ^ k) for i in range(count)])]
    all_to_all x1 -> x0, waiting for transfers between devices: 5.37 us -> none  [local(): lax.all_to_all(terms, 'band', split_axis=0, concat_axis=0, tiled=True)]
    all_to_all x1 -> x0, starting transfers between devices: 3.73 us -> none  [local(): lax.all_to_all(terms, 'band', split_axis=0, concat_axis=0, tiled=True)]
    pallas_call x1, Pallas kernels: 13.6 us -> 12.6 us  [bin_and_modes(): pl.pallas_call(functools.partial(bin_kernel, windows=windows, rows=rows,...]
  transfers between devices with their start and end apart: 2 -> 11, of which waited for: 2 -> 6; matrix products, arithmetic and copies ran while one was open for 1% -> 1% of each run, Pallas kernels for 0% -> 0%
where the time goes in v3:
time: 80.2 us; the launch traced here: 79.8 us
  Pallas kernels  34.8 us (43%)
  starting transfers between devices  17.9 us (22%)
  waiting for transfers between devices  17.3 us (22%)
  local copies, waits for them, and re-layouts  6.46 us (8%)
  between operations  2.05 us (3%)
  other arithmetic  0.94 us (1%)
    pallas_call x1, Pallas kernels, bin_and_modes(): pl.pallas_call(functools.partial(bin_kernel, windows=windows, rows=rows,...  12.6 us
    pallas_call x1, Pallas kernels, legendre_sums(): pl.pallas_call(functools.partial(legendre_kernel, sources=len(recv), owne...  11.7 us
    ppermute x10, starting transfers between devices, swap_blocks(): lax.ppermute(blocks[k], axis, [(i, i ^ k) for i in range(count)])  11.6 us
    pallas_call x1, Pallas kernels, filter_and_sort(): pl.pallas_call(body, out_shape=(jax.ShapeDtypeStruct((lines, length), jnp...  10.5 us
    all_to_all x1, waiting for transfers between devices, local(): recv = lax.all_to_all(send, 'det', split_axis=0, concat_axis=0, tiled=True)  10 us
    ppermute x10, waiting for transfers between devices, swap_blocks(): lax.ppermute(blocks[k], axis, [(i, i ^ k) for i in range(count)])  7.23 us
    all_to_all x1, starting transfers between devices, local(): recv = lax.all_to_all(send, 'det', split_axis=0, concat_axis=0, tiled=True)  6.33 us
    unnamed x20, local copies, waits for them, and re-layouts  4.21 us
  transfers between devices with their start and end apart: 11, of which 6 were waited for; matrix products, arithmetic and copies ran while one was open for 1% of the time, Pallas kernels for 0%

profile of v3, /device:TPU:0, one launch (start us, length us, event | category | flops | bytes accessed | tf_op | source)
XLA Modules:
  0.0 79.8 jit_solution(6750966057555555075)
XLA Ops:
  0.7 1.2 %reshape.161 = f32[8,128,32]{2,1,0:T(8,128)S(1)} reshape(f32[8,4096]{1,0:T(8,128)} %param.14) | data formatting | bytes 262144 | tf_op jit(solution)/shard_map/reshape | solution.py:261
  2.1 0.9 %copy-done.2 = f32[256,256]{1,0:T(8,128)S(1)} copy-done((f32[256,256]{1,0:T(8,128)S(1)}, f32[256,256]{1,0:T(8,128)}, u32[]{:S(2)}) %copy-start.2) | copy-done | bytes 262168
  3.0 0.9 %copy-done.3 = f32[256,256]{1,0:T(8,128)S(1)} copy-done((f32[256,256]{1,0:T(8,128)S(1)}, f32[256,256]{1,0:T(8,128)}, u32[]{:S(2)}) %copy-start.3) | copy-done | bytes 262168
  4.0 0.9 %copy-done.4 = f32[8,4096]{1,0:T(8,128)S(1)} copy-done((f32[8,4096]{1,0:T(8,128)S(1)}, f32[8,4096]{1,0:T(8,128)}, u32[]{:S(2)}) %copy-start.4) | copy-done | bytes 131096
  4.9 0.8 copy-done.5
  5.6 10.5 %filter_sort.1 = (f32[8,4096]{1,0:T(8,128)S(1)}, f32[8,40,256]{2,1,0:T(8,128)}) custom-call(f32[8,4096]{1,0:T(8,128)S(1)} %copy-done.4, f32[256,128]{1,0:T(8,128)S(1)} %bitcast.42, s32[8,4096]{1,0:T(8,128)} %cycle_ref.1, s32[8,4096]{1,0:T(8,128)} %column_ref.1, f32[2,32,1,128]{3,2,1,0:T(1,128)S(1)} %copy-done.5, f32[256,256]{1,0:T(8,128)S(1)} %copy-done.2, ...), custom_call_target="tpu_custom_call" | custom-call | tf_op jit(solution)/shard_map/filter_sort/pallas_call | solution.py:264
  16.2 6.3 %all-to-all-start.4 = ((f32[8,40,256]{2,1,0:T(8,128)}), f32[8,40,256]{2,1,0:T(8,128)S(1)}, u32[]{:S(2)}, u32[]{:S(2)}) async-start(f32[8,40,256]{2,1,0:T(8,128)} %get-tuple-element.76), calls=%async_computation.4 | async-start | bytes 655360 | tf_op jit(solution)/shard_map/all_to_all | solution.py:547
  22.5 0.7 and_multiply_fusion
  23.6 10.0 %all-to-all-done.4.recv_ref = f32[8,40,256]{2,1,0:T(8,128)S(1)} async-done(((f32[8,40,256]{2,1,0:T(8,128)}), f32[8,40,256]{2,1,0:T(8,128)S(1)}, u32[]{:S(2)}, u32[]{:S(2)}) %all-to-all-start.4) | async-done | bytes 327712 | tf_op jit(solution)/shard_map/all_to_all | solution.py:547
  33.7 12.6 %bin_modes.1 = (f32[32,2048]{1,0:T(8,128)}, f32[16,128]{1,0:T(8,128)S(1)}, f32[16,128]{1,0:T(8,128)S(1)}, f32[16,128]{1,0:T(8,128)S(1)}, f32[16,128]{1,0:T(8,128...) custom-call(s32[2]{0:T(128)S(1)} %pad_add_fusion.me_ref, ...), custom_call_target="tpu_custom_call" | custom-call | tf_op jit(solution)/shard_map/bin_modes/pallas_call | solution.py:401
  46.2 1.9 %collective-permute-start.2 = (f32[16,128]{1,0:T(8,128)S(1)}, f32[16,128]{1,0:T(8,128)S(1)}, u32[]{:S(2)}, u32[]{:S(2)}) collective-permute-start(f32[16,128]{1,0:T(8,128)S(1)} %get-tuple-element.80), channel_id=1, source_target_pairs={{0,12},{4,8},{8,4},{12,0},{16,28},{20,24},{24,20},{28,16},{1,13},{... | collective-permute-start | bytes 24584 | tf_op jit(solution)/shard_map/ppermute | solution.py:537
  48.2 2.4 %collective-permute-start.4 = (f32[16,128]{1,0:T(8,128)S(1)}, f32[16,128]{1,0:T(8,128)S(1)}, u32[]{:S(2)}, u32[]{:S(2)}) collective-permute-start(f32[16,128]{1,0:T(8,128)S(1)} %get-tuple-element.82), channel_id=1, source_target_pairs={{0,20},{4,16},{8,28},{12,24},{16,4},{20,0},{24,12},{28,8},{1,21},{... | collective-permute-start | bytes 24584 | tf_op jit(solution)/shard_map/ppermute | solution.py:537
  50.6 1.3 %collective-permute-start.5 = (f32[16,128]{1,0:T(8,128)S(1)}, f32[16,128]{1,0:T(8,128)S(1)}, u32[]{:S(2)}, u32[]{:S(2)}) collective-permute-start(f32[16,128]{1,0:T(8,128)S(1)} %get-tuple-element.83), channel_id=1, source_target_pairs={{0,24},{4,28},{8,16},{12,20},{16,8},{20,12},{24,0},{28,4},{1,25},{... | collective-permute-start | bytes 24584 | tf_op jit(solution)/shard_map/ppermute | solution.py:537
  52.0 2.3 %collective-permute-start.6 = (f32[16,128]{1,0:T(8,128)S(1)}, f32[16,128]{1,0:T(8,128)S(1)}, u32[]{:S(2)}, u32[]{:S(2)}) collective-permute-start(f32[16,128]{1,0:T(8,128)S(1)} %get-tuple-element.84), channel_id=1, source_target_pairs={{0,28},{4,24},{8,20},{12,16},{16,12},{20,8},{24,4},{28,0},{1,29},{... | collective-permute-start | bytes 24584 | tf_op jit(solution)/shard_map/ppermute | solution.py:537
  54.3 1.8 %collective-permute-done.5.refs_6_ = f32[16,128]{1,0:T(8,128)S(1)} collective-permute-done((f32[16,128]{1,0:T(8,128)S(1)}, f32[16,128]{1,0:T(8,128)S(1)}, u32[]{:S(2)}, u32[]{:S(2)}) %collective-permute-start.5) | collective-permute-done | bytes 8224 | tf_op jit(solution)/shard_map/ppermute | solution.py:537
  56.1 0.8 collective-permute-done.6.refs_7_
  56.9 11.7 %legendre_sums.1 = (f32[64,256]{1,0:T(8,128)S(1)}, f32[64,256]{1,0:T(8,128)S(1)}, f32[64,256]{1,0:T(8,128)S(1)}, f32[64,256]{1,0:T(8,128)S(1)}) custom-call(s32[2]{0:T(128)S(1)} %pad_add_fusion.me_ref, f32[16,128]{1,0:T(8,128)S(1)} %get-tuple-element.77.refs_0_, f32[16,128]{1,0:T(8,128)S(1)} %collective-permute-done.refs_1_, ...), custom_call_target="tpu_custom_call" | custom-call | tf_op jit(solution)/shard_map/legendre_sums/pallas_call | solution.py:483
  68.6 1.6 %collective-permute-start.7 = (f32[64,256]{1,0:T(8,128)S(1)}, f32[64,256]{1,0:T(8,128)S(1)}, u32[]{:S(2)}, u32[]{:S(2)}) collective-permute-start(f32[64,256]{1,0:T(8,128)S(1)} %get-tuple-element.86), channel_id=1, source_target_pairs={{0,1},{1,0},{2,3},{3,2},{4,5},{5,4},{6,7},{7,6},{8,9},{9,8},{10,11... | collective-permute-start | bytes 196616 | tf_op jit(solution)/shard_map/ppermute | solution.py:537
  70.1 1.5 %collective-permute-start.8 = (f32[64,256]{1,0:T(8,128)S(1)}, f32[64,256]{1,0:T(8,128)S(1)}, u32[]{:S(2)}, u32[]{:S(2)}) collective-permute-start(f32[64,256]{1,0:T(8,128)S(1)} %get-tuple-element.87), channel_id=1, source_target_pairs={{0,2},{1,3},{2,0},{3,1},{4,6},{5,7},{6,4},{7,5},{8,10},{9,11},{10,... | collective-permute-start | bytes 196616 | tf_op jit(solution)/shard_map/ppermute | solution.py:537
  72.1 0.8 collective-permute-done.7
  72.9 1.5 %collective-permute-done.8 = f32[64,256]{1,0:T(8,128)S(1)} collective-permute-done((f32[64,256]{1,0:T(8,128)S(1)}, f32[64,256]{1,0:T(8,128)S(1)}, u32[]{:S(2)}, u32[]{:S(2)}) %collective-permute-start.8) | collective-permute-done | bytes 65568 | tf_op jit(solution)/shard_map/ppermute | solution.py:537
  74.4 2.4 %collective-permute-done.9 = f32[64,256]{1,0:T(8,128)S(1)} collective-permute-done((f32[64,256]{1,0:T(8,128)S(1)}, f32[64,256]{1,0:T(8,128)S(1)}, u32[]{:S(2)}, u32[]{:S(2)}) %collective-permute-start.9) | collective-permute-done | bytes 65568 | tf_op jit(solution)/shard_map/ppermute | solution.py:537
  76.8 0.5 slice.4
  79.2 0.6 copy-done.8
  (39 shorter events, 1.9 us)
Async XLA Ops:
  0.6 33.0 %copy-start = (bf16[2,1024,256]{2,1,0:T(8,128)(2,1)S(1)}, bf16[2,1024,256]{2,1,0:T(8,128)(2,1)}, u32[]{:S(2)}) copy-start(bf16[2,1024,256]{2,1,0:T(8,128)(2,1)} %constant.77.clone.table_hi) | copy-start | bytes 3145732
  0.6 33.0 %copy-start.1 = (bf16[2,1024,256]{2,1,0:T(8,128)(2,1)S(1)}, bf16[2,1024,256]{2,1,0:T(8,128)(2,1)}, u32[]{:S(2)}) copy-start(bf16[2,1024,256]{2,1,0:T(8,128)(2,1)} %constant.78.clone.table_lo) | copy-start | bytes 3145732
  2.1 1.0 %copy-start.2 = (f32[256,256]{1,0:T(8,128)S(1)}, f32[256,256]{1,0:T(8,128)}, u32[]{:S(2)}) copy-start(f32[256,256]{1,0:T(8,128)} %constant.75.clone.forward_ref) | copy-start | bytes 786436
  3.0 0.9 %copy-start.3 = (f32[256,256]{1,0:T(8,128)S(1)}, f32[256,256]{1,0:T(8,128)}, u32[]{:S(2)}) copy-start(f32[256,256]{1,0:T(8,128)} %constant.76.clone.back_ref) | copy-start | bytes 786436
  4.0 0.9 %copy-start.4 = (f32[8,4096]{1,0:T(8,128)S(1)}, f32[8,4096]{1,0:T(8,128)}, u32[]{:S(2)}) copy-start(f32[8,4096]{1,0:T(8,128)} %scan_ref.1) | copy-start | bytes 393220
  4.9 0.8 copy-start.5
  16.2 17.5 %all-to-all-start.4 = ((f32[8,40,256]{2,1,0:T(8,128)}), f32[8,40,256]{2,1,0:T(8,128)S(1)}, u32[]{:S(2)}, u32[]{:S(2)}) async-start(f32[8,40,256]{2,1,0:T(8,128)} %get-tuple-element.76), calls=%async_computation.4 | async-start | bytes 655360 | tf_op jit(solution)/shard_map/all_to_all | solution.py:547
  46.2 4.4 %collective-permute-start = (f32[16,128]{1,0:T(8,128)S(1)}, f32[16,128]{1,0:T(8,128)S(1)}, u32[]{:S(2)}, u32[]{:S(2)}) collective-permute-start(f32[16,128]{1,0:T(8,128)S(1)} %get-tuple-element.78), channel_id=1, source_target_pairs={{0,4},{4,0},{8,12},{12,8},{16,20},{20,16},{24,28},{28,24},{1,5},{5... | collective-permute-start | bytes 24584 | tf_op jit(solution)/shard_map/ppermute | solution.py:537
  46.2 5.7 %collective-permute-start.1 = (f32[16,128]{1,0:T(8,128)S(1)}, f32[16,128]{1,0:T(8,128)S(1)}, u32[]{:S(2)}, u32[]{:S(2)}) collective-permute-start(f32[16,128]{1,0:T(8,128)S(1)} %get-tuple-element.79), channel_id=1, source_target_pairs={{0,8},{4,12},{8,0},{12,4},{16,24},{20,28},{24,16},{28,20},{1,9},{5... | collective-permute-start | bytes 24584 | tf_op jit(solution)/shard_map/ppermute | solution.py:537
  46.2 8.1 %collective-permute-start.2 = (f32[16,128]{1,0:T(8,128)S(1)}, f32[16,128]{1,0:T(8,128)S(1)}, u32[]{:S(2)}, u32[]{:S(2)}) collective-permute-start(f32[16,128]{1,0:T(8,128)S(1)} %get-tuple-element.80), channel_id=1, source_target_pairs={{0,12},{4,8},{8,4},{12,0},{16,28},{20,24},{24,20},{28,16},{1,13},{... | collective-permute-start | bytes 24584 | tf_op jit(solution)/shard_map/ppermute | solution.py:537
  48.1 6.2 %collective-permute-start.3 = (f32[16,128]{1,0:T(8,128)S(1)}, f32[16,128]{1,0:T(8,128)S(1)}, u32[]{:S(2)}, u32[]{:S(2)}) collective-permute-start(f32[16,128]{1,0:T(8,128)S(1)} %get-tuple-element.81), channel_id=1, source_target_pairs={{0,16},{4,20},{8,24},{12,28},{16,0},{20,4},{24,8},{28,12},{1,17},{... | collective-permute-start | bytes 24584 | tf_op jit(solution)/shard_map/ppermute | solution.py:537
  48.2 6.1 %collective-permute-start.4 = (f32[16,128]{1,0:T(8,128)S(1)}, f32[16,128]{1,0:T(8,128)S(1)}, u32[]{:S(2)}, u32[]{:S(2)}) collective-permute-start(f32[16,128]{1,0:T(8,128)S(1)} %get-tuple-element.82), channel_id=1, source_target_pairs={{0,20},{4,16},{8,28},{12,24},{16,4},{20,0},{24,12},{28,8},{1,21},{... | collective-permute-start | bytes 24584 | tf_op jit(solution)/shard_map/ppermute | solution.py:537
  50.6 5.4 %collective-permute-start.5 = (f32[16,128]{1,0:T(8,128)S(1)}, f32[16,128]{1,0:T(8,128)S(1)}, u32[]{:S(2)}, u32[]{:S(2)}) collective-permute-start(f32[16,128]{1,0:T(8,128)S(1)} %get-tuple-element.83), channel_id=1, source_target_pairs={{0,24},{4,28},{8,16},{12,20},{16,8},{20,12},{24,0},{28,4},{1,25},{... | collective-permute-start | bytes 24584 | tf_op jit(solution)/shard_map/ppermute | solution.py:537
  52.0 4.9 %collective-permute-start.6 = (f32[16,128]{1,0:T(8,128)S(1)}, f32[16,128]{1,0:T(8,128)S(1)}, u32[]{:S(2)}, u32[]{:S(2)}) collective-permute-start(f32[16,128]{1,0:T(8,128)S(1)} %get-tuple-element.84), channel_id=1, source_target_pairs={{0,28},{4,24},{8,20},{12,16},{16,12},{20,8},{24,4},{28,0},{1,29},{... | collective-permute-start | bytes 24584 | tf_op jit(solution)/shard_map/ppermute | solution.py:537
  56.8 21.8 %copy-start.6 = (s32[8,4096]{1,0:T(8,128)S(1)}, s32[8,4096]{1,0:T(8,128)}, u32[]{:S(2)}) copy-start(s32[8,4096]{1,0:T(8,128)} %cycle_ref.1) | copy-start | bytes 393220
  56.8 21.8 %copy-start.7 = (s32[8,4096]{1,0:T(8,128)S(1)}, s32[8,4096]{1,0:T(8,128)}, u32[]{:S(2)}) copy-start(s32[8,4096]{1,0:T(8,128)} %column_ref.1) | copy-start | bytes 393220
  56.8 21.8 %copy-start.9 = (s32[256]{0:T(256)S(1)}, s32[256]{0:T(256)}, u32[]{:S(2)}) copy-start(s32[256]{0:T(256)} %param.17) | copy-start | bytes 3076
  68.6 4.3 %collective-permute-start.7 = (f32[64,256]{1,0:T(8,128)S(1)}, f32[64,256]{1,0:T(8,128)S(1)}, u32[]{:S(2)}, u32[]{:S(2)}) collective-permute-start(f32[64,256]{1,0:T(8,128)S(1)} %get-tuple-element.86), channel_id=1, source_target_pairs={{0,1},{1,0},{2,3},{3,2},{4,5},{5,4},{6,7},{7,6},{8,9},{9,8},{10,11... | collective-permute-start | bytes 196616 | tf_op jit(solution)/shard_map/ppermute | solution.py:537
  70.1 4.3 %collective-permute-start.8 = (f32[64,256]{1,0:T(8,128)S(1)}, f32[64,256]{1,0:T(8,128)S(1)}, u32[]{:S(2)}, u32[]{:S(2)}) collective-permute-start(f32[64,256]{1,0:T(8,128)S(1)} %get-tuple-element.87), channel_id=1, source_target_pairs={{0,2},{1,3},{2,0},{3,1},{4,6},{5,7},{6,4},{7,5},{8,10},{9,11},{10,... | collective-permute-start | bytes 196616 | tf_op jit(solution)/shard_map/ppermute | solution.py:537
  71.7 5.2 %collective-permute-start.9 = (f32[64,256]{1,0:T(8,128)S(1)}, f32[64,256]{1,0:T(8,128)S(1)}, u32[]{:S(2)}, u32[]{:S(2)}) collective-permute-start(f32[64,256]{1,0:T(8,128)S(1)} %get-tuple-element.88), channel_id=1, source_target_pairs={{0,3},{1,2},{2,1},{3,0},{4,7},{5,6},{6,5},{7,4},{8,11},{9,10},{10,... | collective-permute-start | bytes 196616 | tf_op jit(solution)/shard_map/ppermute | solution.py:537
  79.1 0.6 copy-start.8

commit v4 on v3

--- a/solution.py
+++ b/solution.py
@@ -23,17 +23,12 @@
     k1 = np.arange(outer)[:, None]
     n2 = np.arange(LANES)[None, :]
     turn = 2.0 * np.pi * ((k1 * n2) % length) / length
-    twiddle = np.stack([np.cos(turn), np.sin(turn)])[:, :, None, :]
+    twiddle = np.concatenate([np.cos(turn), np.sin(turn)], axis=1)
     a = np.arange(LANES)
     angle = 2.0 * np.pi * (np.outer(a, a) % LANES) / LANES
     c, s = np.cos(angle), np.sin(angle)
     forward = np.block([[c, -s], [s, c]])
-    back = np.block([[c, s], [-s, c]])
-    return (
-        twiddle.astype(np.float32),
-        forward.astype(np.float32),
-        back.astype(np.float32),
-    )
+    return twiddle.astype(np.float32), forward.astype(np.float32)
 
 
 def mode_tables(count):
@@ -84,124 +79,150 @@
     return out_re, out_im
 
 
-def partner(x, axis, distance):
-    size = x.shape[axis]
-    if 2 * distance == size:
-        return pltpu.roll(x, distance, axis=axis)
-    index = lax.broadcasted_iota(jnp.int32, x.shape, axis)
-    upper = (index & distance) != 0
-    return jnp.where(
-        upper,
-        pltpu.roll(x, distance, axis=axis),
-        pltpu.roll(x, size - distance, axis=axis),
+class Places:
+    def __init__(self, tile_bits, total_bits):
+        self.tile_bits, self.total_bits = tile_bits, total_bits
+        self.of = list(range(total_bits))
+        for level in range(tile_bits + 1, total_bits + 1):
+            self.walk(level)
+        held = [self.of.index(place) for place in range(total_bits)]
+        self.of = held
+
+    def swap(self, bit):
+        other = self.of.index(0)
+        self.of[bit], self.of[other] = 0, self.of[bit]
+
+    def walk(self, level):
+        for bit in range(level - 1, self.tile_bits - 1, -1):
+            self.swap(bit)
+        self.swap(0)
+
+    def axis_distance(self, bit):
+        place = self.of[bit] - self.tile_bits
+        return (0, 1 << place) if place < 3 else (1, 1 << (place - 3))
+
+    def mask(self, bit):
+        axis, distance = self.axis_distance(bit)
+        return (lax.broadcasted_iota(jnp.int32, (SUB, LANES), axis) & distance) != 0
+
+
+def trade(low, high, upper, axis, distance):
+    axis += low.ndim - 2
+    size = low.shape[axis]
+    return (
+        jnp.where(upper, pltpu.roll(high, distance, axis=axis), low),
+        jnp.where(upper, high, pltpu.roll(low, size - distance, axis=axis)),
     )
 
 
-def rank_bit(bit, tile_bits):
-    shape = (SUB, LANES)
-    if bit < tile_bits + 3:
-        return (lax.broadcasted_iota(jnp.int32, shape, 0) & (1 << (bit - tile_bits))) != 0
-    return (lax.broadcasted_iota(jnp.int32, shape, 1) & (1 << (bit - tile_bits - 3))) != 0
-
-
-def sort_inner(key_ref, val_ref, level, tile_bits, total_bits, group):
-    tiles = key_ref.shape[0]
+def exchange(keys, vals, a, b, down):
+    if down is True:
+        swap = keys[a] < keys[b]
+    else:
+        swap = keys[a] > keys[b]
+        if down is not False:
+            swap = jnp.logical_xor(swap, down)
+    keys[a], keys[b] = jnp.where(swap, keys[b], keys[a]), jnp.where(swap, keys[a], keys[b])
+    vals[a], vals[b] = jnp.where(swap, vals[b], vals[a]), jnp.where(swap, vals[a], vals[b])
+
+
+def sort_inner(key_ref, val_ref, level, places, group):
+    pairs = key_ref.shape[0]
+    steps = []
+    down = places.mask(level) if level < places.total_bits else False
+    for bit in range(level - 1, places.tile_bits - 1, -1):
+        steps.append((places.mask(bit),) + places.axis_distance(bit))
+        places.swap(bit)
 
     def body(g, carry):
         part = pl.ds(g * group, group)
-        key, val = key_ref[part], val_ref[part]
-        for bit in range(level - 1, tile_bits - 1, -1):
-            if bit < tile_bits + 3:
-                axis, distance = 1, 1 << (bit - tile_bits)
-            else:
-                axis, distance = 2, 1 << (bit - tile_bits - 3)
-            want_max = rank_bit(bit, tile_bits)
-            if level < total_bits:
-                want_max = jnp.logical_xor(want_max, rank_bit(level, tile_bits))
-            sign = jnp.where(want_max, -1.0, 1.0)[None]
-            key_p, val_p = partner(key, axis, distance), partner(val, axis, distance)
-            swap = (key - key_p) * sign > 0.0
-            key = jnp.where(swap, key_p, key)
-            val = jnp.where(swap, val_p, val)
-        key_ref[part] = key
-        val_ref[part] = val
+        keys = [key_ref[part, 0], key_ref[part, 1]]
+        vals = [val_ref[part, 0], val_ref[part, 1]]
+        for upper, axis, distance in steps:
+            keys = list(trade(*keys, upper, axis, distance))
+            vals = list(trade(*vals, upper, axis, distance))
+            exchange(keys, vals, 0, 1, down)
+        for i in range(2):
+            key_ref[part, i] = keys[i]
+            val_ref[part, i] = vals[i]
         return carry
 
-    lax.fori_loop(0, tiles // group, body, 0)
-
-
-def exchange(keys, vals, a, b, down):
-    swap = keys[a] > keys[b]
-    if down is True:
-        swap = keys[a] < keys[b]
-    elif down is not False:
-        swap = jnp.logical_xor(swap, down)
-    keys[a], keys[b] = jnp.where(swap, keys[b], keys[a]), jnp.where(swap, keys[a], keys[b])
-    vals[a], vals[b] = jnp.where(swap, vals[b], vals[a]), jnp.where(swap, vals[a], vals[b])
-
-
-def sort_across(key_ref, val_ref, level, tile_bits, total_bits):
-    tiles = key_ref.shape[0]
-    top = min(level, tile_bits)
-    bits = list(range(top - 1, -1, -1))
-    passes = [bits[:-3], bits[-3:]] if len(bits) > 3 else [bits]
-    for chosen in passes:
-        low, span = min(chosen), len(chosen)
-        members = 1 << span
-        stride = 1 << low
-
-        def run(base, static_base):
-            keys = [key_ref[base + i * stride] for i in range(members)]
-            vals = [val_ref[base + i * stride] for i in range(members)]
+    lax.fori_loop(0, pairs // group, body, 0)
+
+
+def sort_across(key_ref, val_ref, level, places):
+    tiles = 2 * key_ref.shape[0]
+    tile_bits = places.tile_bits
+    mask = places.mask(level) if tile_bits <= level < places.total_bits else None
+    back = None
+    if level > tile_bits:
+        back = (places.mask(0),) + places.axis_distance(0)
+        places.swap(0)
+    bits = list(range(min(level, tile_bits) - 1, -1, -1))
+    for chosen in [bits[:-3], bits[-3:]] if len(bits) > 3 else [bits]:
+        low = min(chosen)
+        members, stride = 1 << len(chosen), 1 << low
+        for g in range(tiles // members):
+            base = (g // stride) * (members * stride) + g % stride
+            spots = [divmod(base + i * stride, 2) for i in range(members)]
+            keys = [key_ref[spot] for spot in spots]
+            vals = [val_ref[spot] for spot in spots]
             for bit in chosen:
                 step = 1 << (bit - low)
                 for i in range(members):
                     if i & step:
                         continue
-                    if level >= total_bits:
+                    if bit == 0 and back is not None:
+                        keys[i], keys[i + 1] = trade(keys[i], keys[i + 1], *back)
+                        vals[i], vals[i + 1] = trade(vals[i], vals[i + 1], *back)
+                    down = mask
+                    if level >= places.total_bits:
                         down = False
                     elif level < tile_bits:
-                        down = ((static_base + i * stride) >> level) & 1 == 1
-                    else:
-                        down = rank_bit(level, tile_bits)
+                        down = ((base + i * stride) >> level) & 1 == 1
                     exchange(keys, vals, i, i + step, down)
-            for i in range(members):
-                key_ref[base + i * stride] = keys[i]
-                val_ref[base + i * stride] = vals[i]
-
-        def base_of(g):
-            return (g // stride) * (members * stride) + g % stride
-
-        groups = tiles // members
-        if level < tile_bits:
-            for g in range(groups):
-                run(base_of(g), base_of(g))
-        else:
-            for g in range(groups):
-                run(base_of(g), None)
+            for spot, key, val in zip(spots, keys, vals):
+                key_ref[spot] = key
+                val_ref[spot] = val
 
 
 def sort_kernel(
-    scan_ref, resp_ref, cycle_ref, column_ref, twiddle_ref, forward_ref, back_ref,
+    scan_hbm, resp_hbm, cycle_hbm, column_hbm, twiddle_hbm, forward_hbm,
     filtered_ref, send_ref,
+    scan_ref, resp_ref, cycle_ref, column_ref, twiddle_ref, forward_ref, arrived,
     key_ref, val_ref, spec_ref, key_rows, val_rows,
     *, buckets, span, rows, windows,
 ):
     lines, length = scan_ref.shape
     outer = length // LANES
+    loads = [
+        pltpu.make_async_copy(source, place, arrived.at[i])
+        for i, (source, place) in enumerate([
+            (scan_hbm, scan_ref), (twiddle_hbm, twiddle_ref), (forward_hbm, forward_ref),
+            (resp_hbm, resp_ref), (cycle_hbm, cycle_ref), (column_hbm, column_ref),
+        ])
+    ]
+    for load in loads:
+        load.start()
+    loads[0].wait()
     re, im = small_fft([scan_ref[:, n * LANES:(n + 1) * LANES] for n in range(outer)], None, -1)
+    loads[1].wait()
     for k in range(outer):
-        c, s = twiddle_ref[0, k], twiddle_ref[1, k]
+        c, s = twiddle_ref[k:k + 1, :LANES], twiddle_ref[k:k + 1, LANES:]
         here = pl.ds(k * lines, lines)
         spec_ref[here, :LANES] = re[k] * c + im[k] * s
         spec_ref[here, LANES:] = im[k] * c - re[k] * s
+    for load in loads[2:]:
+        load.wait()
     spec = jnp.dot(spec_ref[...], forward_ref[...], precision=precise, preferred_element_type=jnp.float32)
     resp = resp_ref[...] * (1.0 / length)
     spec = spec * jnp.concatenate([resp, resp], axis=1)
-    spec_ref[...] = jnp.dot(spec, back_ref[...], precision=precise, preferred_element_type=jnp.float32)
+    spec_ref[...] = lax.dot_general(
+        spec, forward_ref[...], NT, precision=precise, preferred_element_type=jnp.float32
+    )
     re, im = [], []
     for k in range(outer):
-        c, s = twiddle_ref[0, k], twiddle_ref[1, k]
+        c, s = twiddle_ref[k:k + 1, :LANES], twiddle_ref[k:k + 1, LANES:]
         here = pl.ds(k * lines, lines)
         ur, ui = spec_ref[here, :LANES], spec_ref[here, LANES:]
         re.append(ur * c - ui * s)
@@ -210,19 +231,20 @@
     for n in range(outer):
         cols = slice(n * LANES, (n + 1) * LANES)
         filtered_ref[:, cols] = out[n]
-        val_ref[n] = out[n]
-        key_ref[n] = (cycle_ref[:, cols] * NPHI + column_ref[:, cols]).astype(jnp.float32)
+        val_ref[divmod(n, 2)] = out[n]
+        key_ref[divmod(n, 2)] = (cycle_ref[:, cols] * NPHI + column_ref[:, cols]).astype(jnp.float32)
     tiles = outer
     tile_bits = tiles.bit_length() - 1
-    total_bits = tile_bits + 10
-    for level in range(1, total_bits + 1):
+    places = Places(tile_bits, tile_bits + 10)
+    for level in range(1, places.total_bits + 1):
         if level > tile_bits:
-            sort_inner(key_ref, val_ref, level, tile_bits, total_bits, min(16, tiles))
-        sort_across(key_ref, val_ref, level, tile_bits, total_bits)
-    keys = key_ref[...]
+            sort_inner(key_ref, val_ref, level, places, min(8, tiles // 2))
+        sort_across(key_ref, val_ref, level, places)
+    assert places.of == list(range(places.total_bits))
+    row_len = tiles * SUB
+    keys = key_ref[...].reshape(tiles, SUB, LANES)
     last = jnp.max(jnp.max(keys, axis=0), axis=0, keepdims=True)
     first = jnp.min(jnp.min(keys, axis=0), axis=0, keepdims=True)
-    row_len = tiles * SUB
     key_rows[:LANES, :] = keys.reshape(row_len, LANES).T
     val_rows[:LANES, :] = val_ref[...].reshape(row_len, LANES).T
     reach = key_rows.shape[0] - LANES
@@ -257,8 +279,9 @@
     row_len = tiles * SUB
     rows = LANES // buckets + 2
     reach = (rows + 2 * SUB - 2) // SUB * SUB
-    twiddle, forward, back = filter_tables(length)
+    twiddle, forward = filter_tables(length)
     resp_rows = resp.reshape(lines, LANES, tiles).transpose(2, 0, 1).reshape(tiles * lines, LANES)
+    operands = [scan, resp_rows, cycle, column, jnp.asarray(twiddle), jnp.asarray(forward)]
     body = functools.partial(sort_kernel, buckets=buckets, span=span, rows=rows, windows=windows)
     vmem = pl.BlockSpec(memory_space=pltpu.VMEM)
     return pl.pallas_call(
@@ -267,18 +290,19 @@
             jax.ShapeDtypeStruct((lines, length), jnp.float32),
             jax.ShapeDtypeStruct((det_count, 2 * windows * rows, row_len), jnp.float32),
         ),
-        in_specs=[vmem] * 7,
+        in_specs=[pl.BlockSpec(memory_space=pltpu.HBM)] * len(operands),
         out_specs=(vmem, vmem),
-        scratch_shapes=[
-            pltpu.VMEM((tiles, SUB, LANES), jnp.float32),
-            pltpu.VMEM((tiles, SUB, LANES), jnp.float32),
+        scratch_shapes=[pltpu.VMEM(x.shape, x.dtype) for x in operands] + [
+            pltpu.SemaphoreType.DMA((len(operands),)),
+            pltpu.VMEM((tiles // 2, 2, SUB, LANES), jnp.float32),
+            pltpu.VMEM((tiles // 2, 2, SUB, LANES), jnp.float32),
             pltpu.VMEM((tiles * lines, 2 * LANES), jnp.float32),
             pltpu.VMEM((LANES + reach, row_len), jnp.float32),
             pltpu.VMEM((LANES + reach, row_len), jnp.float32),
         ],
         compiler_params=pltpu.CompilerParams(vmem_limit_bytes=24 * 1024 * 1024),
         name="filter_sort",
-    )(scan, resp_rows, cycle, column, jnp.asarray(twiddle), jnp.asarray(forward), jnp.asarray(back))
+    )(*operands)
 
 
 def split2(x):
@@ -288,9 +312,9 @@
 
 
 def bin_kernel(
-    me_ref, recv_ref, pick_ref, table_hi, table_lo, map_ref, *refs, windows, rows, window_cycles
+    recv_ref, pick_ref, table_hi, table_lo, map_ref, send_ref, flag_ref,
+    left_a, left_b, right_a, right_b, acc_ref, *, windows, rows, window_cycles
 ):
-    send_refs, (blocks_ref, left_a, left_b, right_a, right_b, acc_ref) = refs[:-6], refs[-6:]
     left_refs, right_refs = (left_a, left_b), (right_a, right_b)
     sources = recv_ref.shape[0]
     row_len = recv_ref.shape[2]
@@ -367,22 +391,20 @@
     choose = jnp.where(choose, 1.0, 0.0).astype(jnp.bfloat16)
     moved = jnp.dot(pieces, choose, preferred_element_type=jnp.float32)
     moved = moved[:cycles] + moved[cycles:2 * cycles] + moved[2 * cycles:]
-    owners, group_rows, lanes = blocks_ref.shape
+    owners, group_rows, lanes = send_ref.shape
     groups = cycles // group_rows
     lane_group = lax.broadcasted_iota(jnp.int32, (group_rows, lanes), 1) // (lanes // groups)
     values = recv_ref[:, windows * rows:, :]
-    broken = jnp.max(jnp.where(values == values, 0.0, 1.0)) > 0.0
+    flag_ref[0] = (jnp.max(jnp.where(values == values, 0.0, 1.0)) > 0.0).astype(jnp.int32)
     for d in range(owners):
         block = moved[:, d * lanes:(d + 1) * lanes]
         out = block[:group_rows]
         for h in range(1, groups):
             out = jnp.where(lane_group == h, block[h * group_rows:(h + 1) * group_rows], out)
-        blocks_ref[d] = jnp.where(broken, jnp.nan, out)
-    for k in range(owners):
-        send_refs[k][...] = blocks_ref[me_ref[0] ^ k]
-
-
-def bin_and_modes(me, recv, order_slot, band_cycles):
+        send_ref[d] = out
+
+
+def bin_and_modes(recv, order_slot, band_cycles):
     sources, lines, row_len = recv.shape
     windows = WINDOWS
     rows = lines // (2 * windows)
@@ -402,11 +424,12 @@
         functools.partial(bin_kernel, windows=windows, rows=rows, window_cycles=cycles // windows),
         out_shape=(
             jax.ShapeDtypeStruct((cycles, NPHI), jnp.float32),
-        ) + (jax.ShapeDtypeStruct((cycles // groups, LANES), jnp.float32),) * sources,
-        in_specs=[pl.BlockSpec(memory_space=pltpu.SMEM)] + [vmem] * 4,
-        out_specs=(vmem,) * (sources + 1),
+            jax.ShapeDtypeStruct((sources, cycles // groups, LANES), jnp.float32),
+            jax.ShapeDtypeStruct((1,), jnp.int32),
+        ),
+        in_specs=[vmem] * 4,
+        out_specs=(vmem, vmem, pl.BlockSpec(memory_space=pltpu.SMEM)),
         scratch_shapes=[
-            pltpu.VMEM((sources, cycles // groups, LANES), jnp.float32),
             pltpu.VMEM((3 * area, depth), jnp.bfloat16),
             pltpu.VMEM((3 * area, depth), jnp.bfloat16),
             pltpu.VMEM((ROW, depth), jnp.bfloat16),
@@ -415,13 +438,11 @@
         ],
         compiler_params=pltpu.CompilerParams(vmem_limit_bytes=40 * 1024 * 1024),
         name="bin_modes",
-    )(me, recv, pick, jnp.asarray(high), jnp.asarray(low))
-
-
-def legendre_kernel(me_ref, *refs, sources, owners):
-    recv_refs, table_ref = refs[:sources], refs[sources]
-    out_refs = refs[sources + 1:sources + 1 + owners]
-    leg_ref, arrived, modes_ref, wide_ref, block_ref, sums_ref = refs[sources + 1 + owners:]
+    )(recv, pick, jnp.asarray(high), jnp.asarray(low))
+
+
+def legendre_kernel(me_ref, recv_ref, table_ref, *refs, owners):
+    out_refs, (leg_ref, arrived, modes_ref, wide_ref, sums_ref) = refs[:owners], refs[owners:]
     slots, band_cycles, degrees = table_ref.shape
 
     def load(slot):
@@ -432,18 +453,16 @@
         return carry
 
     lax.fori_loop(0, slots, start, 0)
-    group_rows, lanes = recv_refs[0].shape
+    sources, group_rows, lanes = recv_ref.shape
     groups = lanes // (2 * slots)
     width = out_refs[0].shape[1]
     tiles = degrees // LANES
-    cycles = group_rows * groups
-    for k in range(sources):
-        block = recv_refs[k][...]
+    for e in range(sources):
+        block = recv_ref[e]
         for h in range(groups):
+            at = (e * groups + h) * group_rows
             turned = block if h == 0 else pltpu.roll(block, lanes - h * 2 * slots, axis=1)
-            block_ref[h * group_rows:(h + 1) * group_rows, :] = turned
-        at = pl.multiple_of((me_ref[0] ^ k) * cycles, cycles)
-        modes_ref[pl.ds(at, cycles), :] = block_ref[...]
+            modes_ref[at:at + group_rows, :] = turned
 
     def widen(slot, half):
         turned = pltpu.roll(modes_ref[...], lax.rem(lanes - slot, lanes), axis=1)
@@ -474,28 +493,27 @@
 
     lax.fori_loop(0, slots, body, 0)
     for k in range(owners):
-        out_refs[k][...] = sums_ref[me_ref[1] ^ k]
+        out_refs[k][...] = sums_ref[me_ref[0] ^ k]
 
 
 def legendre_sums(me, recv, legendre, owners):
     slots, band_cycles, degrees = legendre.shape
     vmem = pl.BlockSpec(memory_space=pltpu.VMEM)
     return pl.pallas_call(
-        functools.partial(legendre_kernel, sources=len(recv), owners=owners),
+        functools.partial(legendre_kernel, owners=owners),
         out_shape=(jax.ShapeDtypeStruct((2 * slots, degrees // owners), jnp.float32),) * owners,
-        in_specs=[pl.BlockSpec(memory_space=pltpu.SMEM)] + [vmem] * len(recv) + [pl.BlockSpec(memory_space=pl.ANY)],
+        in_specs=[pl.BlockSpec(memory_space=pltpu.SMEM), vmem, pl.BlockSpec(memory_space=pl.ANY)],
         out_specs=(vmem,) * owners,
         scratch_shapes=[
             pltpu.VMEM(legendre.shape, jnp.float32),
             pltpu.SemaphoreType.DMA((slots,)),
             pltpu.VMEM((band_cycles, LANES), jnp.float32),
             pltpu.VMEM((2, 2, band_cycles, LANES), jnp.float32),
-            pltpu.VMEM((band_cycles // len(recv), LANES), jnp.float32),
             pltpu.VMEM((owners, 2 * slots, degrees // owners), jnp.float32),
         ],
         compiler_params=pltpu.CompilerParams(vmem_limit_bytes=44 * 1024 * 1024),
         name="legendre_sums",
-    )(me, *recv, legendre)
+    )(me, recv, legendre)
 
 
 def exchange_and_sum(x, axis, count):
@@ -503,8 +521,7 @@
     return jnp.sum(lax.all_to_all(parts, axis, split_axis=0, concat_axis=0, tiled=True), axis=0)
 
 
-def dense_path(filtered, cycle_offset, column, order_slot, legendre, det_count, band_count):
-    band_cycles = legendre.shape[1]
+def dense_path(filtered, cycle_offset, column, order_slot, band_cycles, det_count):
     flat_index = (cycle_offset * NPHI + column).reshape(-1)
     empty = jnp.zeros((band_cycles * NPHI,), jnp.float32)
     partial_value = empty.at[flat_index].add(filtered.reshape(-1)).reshape(band_cycles, NPHI)
@@ -514,21 +531,15 @@
     sky_map = summed / jnp.maximum(hit_total, 1.0)
     pixel_index = jnp.arange(NPHI, dtype=jnp.int32)[:, None]
     phases = 2.0 * jnp.pi / NPHI * (pixel_index * order_slot[None, :] % NPHI).astype(jnp.float32)
-    cycle_modes = jnp.stack([
+    modes = jnp.stack([
         jnp.dot(sky_map, jnp.cos(phases), precision=precise),
         -jnp.dot(sky_map, jnp.sin(phases), precision=precise),
     ])
-    slot_count, _, degrees = legendre.shape
-    local_orders = lax.dynamic_slice_in_dim(order_slot, lax.axis_index("det") * slot_count, slot_count, 0)
-    keep = jnp.arange(degrees, dtype=jnp.int32)[None, :] >= local_orders[:, None]
-    terms = jnp.einsum(
-        "crs,srl->csl",
-        lax.all_to_all(cycle_modes, "det", split_axis=2, concat_axis=1, tiled=True),
-        legendre,
-        precision=precise,
-    ) * keep.astype(jnp.float32)[None]
-    harmonics = exchange_and_sum(terms.transpose(2, 0, 1).reshape(degrees, -1), "band", band_count)
-    return harmonics.reshape(-1, 2, slot_count).transpose(1, 2, 0), sky_map
+    slots = order_slot.shape[0] // det_count
+    groups = LANES // (2 * slots)
+    blocks = modes.reshape(2, groups, -1, det_count, slots).transpose(3, 2, 1, 0, 4)
+    blocks = blocks.reshape(det_count, -1, LANES)
+    return sky_map, lax.all_to_all(blocks, "det", split_axis=0, concat_axis=0, tiled=True)
 
 
 def swap_blocks(blocks, axis):
@@ -543,25 +554,22 @@
     filtered, send = filter_and_sort(
         scan_lines, response, cycle_offset, column, det_count, band_cycles
     )
-    me = jnp.stack([lax.axis_index("det"), lax.axis_index("band")]).astype(jnp.int32)
     recv = lax.all_to_all(send, "det", split_axis=0, concat_axis=0, tiled=True)
-    sky_map, *modes = bin_and_modes(me, recv, order_slot, band_cycles)
-    modes = swap_blocks(modes, "det")
-    terms = swap_blocks(legendre_sums(me, modes, legendre, band_count), "band")
+    sky_map, modes, crowded = bin_and_modes(recv, order_slot, band_cycles)
+    modes = lax.all_to_all(modes, "det", split_axis=0, concat_axis=0, tiled=True)
+    sky_map, modes = lax.cond(
+        crowded[0] > 0,
+        lambda: dense_path(filtered, cycle_offset, column, order_slot, band_cycles, det_count),
+        lambda: (sky_map, modes),
+    )
+    band = lax.axis_index("band").astype(jnp.int32)
+    terms = swap_blocks(legendre_sums(band.reshape(1), modes, legendre, band_count), "band")
     sums = functools.reduce(jnp.add, terms)
-    crowded = jnp.isnan(sums[0, 0])
     local_orders = lax.dynamic_slice_in_dim(order_slot, lax.axis_index("det") * slots, slots, 0)
     width = degrees // band_count
-    degree = lax.axis_index("band") * width + jnp.arange(width, dtype=jnp.int32)
+    degree = band * width + jnp.arange(width, dtype=jnp.int32)
     keep = degree[None, None, :] >= local_orders[None, :, None]
-    harmonics = jnp.where(keep, sums.reshape(2, slots, width), 0.0)
-    return lax.cond(
-        crowded,
-        lambda: dense_path(
-            filtered, cycle_offset, column, order_slot, legendre, det_count, band_count
-        ),
-        lambda: (harmonics, sky_map),
-    )
+    return jnp.where(keep, sums.reshape(2, slots, width), 0.0), sky_map
 
 
 def solution(mesh):

time: 80.2 us -> 77.5 us (0.966)
  starting transfers between devices: 17.9 us -> 13.3 us
  waiting for transfers between devices: 17.3 us -> 19.8 us
  local copies, waits for them, and re-layouts: 6.46 us -> 4.37 us
  Pallas kernels: 34.8 us -> 36.7 us
    ppermute x10 -> x3, starting transfers between devices: 11.6 us -> 3.55 us  [swap_blocks(): lax.ppermute(blocks[k], axis, [(i, i ^ k) for i in range(count)])]
    all_to_all x0 -> x1, waiting for transfers between devices: none -> 5.11 us  [local(): lax.all_to_all(modes, 'det', split_axis=0, concat_axis=0, tiled=True)]
    all_to_all x0 -> x1, starting transfers between devices: none -> 3.36 us  [local(): lax.all_to_all(modes, 'det', split_axis=0, concat_axis=0, tiled=True)]
    pallas_call x1, Pallas kernels: 10.5 us -> 13.4 us  [filter_and_sort(): pl.pallas_call(body, out_shape=(jax.ShapeDtypeStruct((lines, length), jnp...]
    ppermute x10 -> x3, waiting for transfers between devices: 7.23 us -> 4.61 us  [swap_blocks(): lax.ppermute(blocks[k], axis, [(i, i ^ k) for i in range(count)])]
    unnamed x20 -> x16, local copies, waits for them, and re-layouts: 4.21 us -> 2.63 us
  transfers between devices with their start and end apart: 11 -> 5, of which waited for: 6 -> 5; matrix products, arithmetic and copies ran while one was open for 1% -> 2% of each run, Pallas kernels for 0% -> 0%
where the time goes in v4:
time: 77.5 us; the launch traced here: 77.1 us
  Pallas kernels  36.7 us (47%)
  waiting for transfers between devices  19.8 us (26%)
  starting transfers between devices  13.3 us (17%)
  local copies, waits for them, and re-layouts  4.37 us (6%)
  other arithmetic  1.49 us (2%)
  between operations  1.37 us (2%)
    pallas_call x1, Pallas kernels, filter_and_sort(): pl.pallas_call(body, out_shape=(jax.ShapeDtypeStruct((lines, length), jnp...  13.4 us
    pallas_call x1, Pallas kernels, bin_and_modes(): pl.pallas_call(functools.partial(bin_kernel, windows=windows, rows=rows,...  12.2 us
    pallas_call x1, Pallas kernels, legendre_sums(): pl.pallas_call(functools.partial(legendre_kernel, owners=owners), out_sha...  11.2 us
    all_to_all x1, waiting for transfers between devices, local(): recv = lax.all_to_all(send, 'det', split_axis=0, concat_axis=0, tiled=True)  10.1 us
    all_to_all x1, starting transfers between devices, local(): recv = lax.all_to_all(send, 'det', split_axis=0, concat_axis=0, tiled=True)  6.34 us
    all_to_all x1, waiting for transfers between devices, local(): lax.all_to_all(modes, 'det', split_axis=0, concat_axis=0, tiled=True)  5.11 us
    ppermute x3, waiting for transfers between devices, swap_blocks(): lax.ppermute(blocks[k], axis, [(i, i ^ k) for i in range(count)])  4.61 us
    ppermute x3, starting transfers between devices, swap_blocks(): lax.ppermute(blocks[k], axis, [(i, i ^ k) for i in range(count)])  3.55 us
  transfers between devices with their start and end apart: 5, of which 5 were waited for; matrix products, arithmetic and copies ran while one was open for 2% of the time, Pallas kernels for 0%

profile of v4, /device:TPU:0, one launch (start us, length us, event | category | flops | bytes accessed | tf_op | source)
XLA Modules:
  0.0 77.1 jit_solution(4745727948379214132)
XLA Ops:
  0.7 1.2 %reshape.147 = f32[8,128,32]{2,1,0:T(8,128)S(1)} reshape(f32[8,4096]{1,0:T(8,128)} %param.13) | data formatting | bytes 262144 | tf_op jit(solution)/shard_map/reshape | solution.py:283
  1.9 0.2 copy.17
  2.1 0.9 %copy-done.2 = f32[256,256]{1,0:T(8,128)S(1)} copy-done((f32[256,256]{1,0:T(8,128)S(1)}, f32[256,256]{1,0:T(8,128)}, u32[]{:S(2)}) %copy-start.2) | copy-done | bytes 262168
  3.0 0.9 %copy-done.3 = f32[8,4096]{1,0:T(8,128)S(1)} copy-done((f32[8,4096]{1,0:T(8,128)S(1)}, f32[8,4096]{1,0:T(8,128)}, u32[]{:S(2)}) %copy-start.3) | copy-done | bytes 131096
  3.9 0.8 copy-done.4
  4.7 13.4 %filter_sort.1 = (f32[8,4096]{1,0:T(8,128)S(1)}, f32[8,40,256]{2,1,0:T(8,128)}) custom-call(f32[8,4096]{1,0:T(8,128)S(1)} %copy-done.3, f32[256,128]{1,0:T(8,128)S(1)} %bitcast.17, s32[8,4096]{1,0:T(8,128)} %cycle_hbm.1, s32[8,4096]{1,0:T(8,128)} %column_hbm.1, f32[32,256]{1,0:T(8,128)S(1)} %copy-done.4, f32[256,256]{1,0:T(8,128)S(1)} %copy-done.2), custom_call_target="tpu_custom_call" | custom-call | tf_op jit(solution)/shard_map/filter_sort/pallas_call | solution.py:287
  18.1 6.3 %all-to-all-start.3 = ((f32[8,40,256]{2,1,0:T(8,128)}), f32[8,40,256]{2,1,0:T(8,128)S(1)}, u32[]{:S(2)}, u32[]{:S(2)}) async-start(f32[8,40,256]{2,1,0:T(8,128)} %get-tuple-element.29), calls=%async_computation.3 | async-start | bytes 655360 | tf_op jit(solution)/shard_map/all_to_all | solution.py:557
  24.4 0.7 and_multiply_fusion
  25.1 0.1 mul.51
  25.3 0.1 add_add_fusion.1
  25.4 0.1 reshape.149.pick_ref
  25.5 10.1 %all-to-all-done.3.recv_ref = f32[8,40,256]{2,1,0:T(8,128)S(1)} async-done(((f32[8,40,256]{2,1,0:T(8,128)}), f32[8,40,256]{2,1,0:T(8,128)S(1)}, u32[]{:S(2)}, u32[]{:S(2)}) %all-to-all-start.3) | async-done | bytes 327712 | tf_op jit(solution)/shard_map/all_to_all | solution.py:557
  35.6 12.2 %bin_modes.1 = (f32[32,2048]{1,0:T(8,128)}, f32[8,16,128]{2,1,0:T(8,128)}, s32[1]{0:T(128)}) custom-call(f32[8,40,256]{2,1,0:T(8,128)S(1)} %all-to-all-done.3.recv_ref, s32[1,1024]{1,0:T(1,128)S(1)} %reshape.149.pick_ref, bf16[2,1024,256]{2,1,0:T(8,128)(2,1)S(1)} %copy-done, bf16[2,1024,256]{2,1,0:T(8,128)(2,1)S(1)} %copy-done.1), custom_call_target="tpu_custom_call" | custom-call | tf_op jit(solution)/shard_map/bin_modes/pallas_call | solution.py:423
  47.8 3.4 %all-to-all-start.4 = ((f32[8,16,128]{2,1,0:T(8,128)}), f32[8,16,128]{2,1,0:T(8,128)S(1)}, u32[]{:S(2)}, u32[]{:S(2)}) async-start(f32[8,16,128]{2,1,0:T(8,128)} %get-tuple-element.32), calls=%async_computation.4 | async-start | bytes 131072 | tf_op jit(solution)/shard_map/all_to_all | solution.py:559
  51.1 0.1 dynamic_slice.3
  51.9 5.1 %all-to-all-done.4 = f32[8,16,128]{2,1,0:T(8,128)S(1)} async-done(((f32[8,16,128]{2,1,0:T(8,128)}), f32[8,16,128]{2,1,0:T(8,128)S(1)}, u32[]{:S(2)}, u32[]{:S(2)}) %all-to-all-start.4) | async-done | bytes 65568 | tf_op jit(solution)/shard_map/all_to_all | solution.py:559
  57.0 11.2 %legendre_sums.1 = (f32[64,256]{1,0:T(8,128)S(1)}, f32[64,256]{1,0:T(8,128)S(1)}, f32[64,256]{1,0:T(8,128)S(1)}, f32[64,256]{1,0:T(8,128)S(1)}) custom-call(s32[1]{0:T(128)} %bitcast.2.me_ref, f32[8,16,128]{2,1,0:T(8,128)S(1)} %get-tuple-element.34.recv_ref, f32[32,256,1024]{2,1,0:T(8,128)} %table_ref.1), custom_call_target="tpu_custom_call" | custom-call | tf_op jit(solution)/shard_map/legendre_sums/pallas_call | solution.py:502
  68.2 1.6 %collective-permute-start = (f32[64,256]{1,0:T(8,128)S(1)}, f32[64,256]{1,0:T(8,128)S(1)}, u32[]{:S(2)}, u32[]{:S(2)}) collective-permute-start(f32[64,256]{1,0:T(8,128)S(1)} %get-tuple-element.36), channel_id=1, source_target_pairs={{0,1},{1,0},{2,3},{3,2},{4,5},{5,4},{6,7},{7,6},{8,9},{9,8},{10,11... | collective-permute-start | bytes 196616 | tf_op jit(solution)/shard_map/ppermute | solution.py:548
  69.7 1.5 %collective-permute-start.1 = (f32[64,256]{1,0:T(8,128)S(1)}, f32[64,256]{1,0:T(8,128)S(1)}, u32[]{:S(2)}, u32[]{:S(2)}) collective-permute-start(f32[64,256]{1,0:T(8,128)S(1)} %get-tuple-element.37), channel_id=1, source_target_pairs={{0,2},{1,3},{2,0},{3,1},{4,6},{5,7},{6,4},{7,5},{8,10},{9,11},{10,... | collective-permute-start | bytes 196616 | tf_op jit(solution)/shard_map/ppermute | solution.py:548
  71.2 0.5 collective-permute-start.2
  71.8 0.7 collective-permute-done
  72.5 2.2 %collective-permute-done.1 = f32[64,256]{1,0:T(8,128)S(1)} collective-permute-done((f32[64,256]{1,0:T(8,128)S(1)}, f32[64,256]{1,0:T(8,128)S(1)}, u32[]{:S(2)}, u32[]{:S(2)}) %collective-permute-start.1) | collective-permute-done | bytes 65568 | tf_op jit(solution)/shard_map/ppermute | solution.py:548
  74.7 1.7 %collective-permute-done.2 = f32[64,256]{1,0:T(8,128)S(1)} collective-permute-done((f32[64,256]{1,0:T(8,128)S(1)}, f32[64,256]{1,0:T(8,128)S(1)}, u32[]{:S(2)}, u32[]{:S(2)}) %collective-permute-start.2) | collective-permute-done | bytes 65568 | tf_op jit(solution)/shard_map/ppermute | solution.py:548
  76.4 0.6 broadcast_select_fusion
  (20 shorter events, 0.2 us)
Async XLA Ops:
  0.6 35.0 %copy-start = (bf16[2,1024,256]{2,1,0:T(8,128)(2,1)S(1)}, bf16[2,1024,256]{2,1,0:T(8,128)(2,1)}, u32[]{:S(2)}) copy-start(bf16[2,1024,256]{2,1,0:T(8,128)(2,1)} %constant.61.clone.table_hi) | copy-start | bytes 3145732
  0.6 34.9 %copy-start.1 = (bf16[2,1024,256]{2,1,0:T(8,128)(2,1)S(1)}, bf16[2,1024,256]{2,1,0:T(8,128)(2,1)}, u32[]{:S(2)}) copy-start(bf16[2,1024,256]{2,1,0:T(8,128)(2,1)} %constant.62.clone.table_lo) | copy-start | bytes 3145732
  2.1 1.0 %copy-start.2 = (f32[256,256]{1,0:T(8,128)S(1)}, f32[256,256]{1,0:T(8,128)}, u32[]{:S(2)}) copy-start(f32[256,256]{1,0:T(8,128)} %constant.60.clone.forward_hbm) | copy-start | bytes 786436
  3.0 0.9 %copy-start.3 = (f32[8,4096]{1,0:T(8,128)S(1)}, f32[8,4096]{1,0:T(8,128)}, u32[]{:S(2)}) copy-start(f32[8,4096]{1,0:T(8,128)} %scan_hbm.1) | copy-start | bytes 393220
  3.9 0.8 copy-start.4
  4.7 46.4 %copy-start.7 = (s32[256]{0:T(256)S(1)}, s32[256]{0:T(256)}, u32[]{:S(2)}) copy-start(s32[256]{0:T(256)} %param.16) | copy-start | bytes 3076
  4.7 52.3 %copy-start.5 = (s32[8,4096]{1,0:T(8,128)S(1)}, s32[8,4096]{1,0:T(8,128)}, u32[]{:S(2)}) copy-start(s32[8,4096]{1,0:T(8,128)} %cycle_hbm.1) | copy-start | bytes 393220
  4.7 52.3 %copy-start.6 = (s32[8,4096]{1,0:T(8,128)S(1)}, s32[8,4096]{1,0:T(8,128)}, u32[]{:S(2)}) copy-start(s32[8,4096]{1,0:T(8,128)} %column_hbm.1) | copy-start | bytes 393220
  18.1 17.5 %all-to-all-start.3 = ((f32[8,40,256]{2,1,0:T(8,128)}), f32[8,40,256]{2,1,0:T(8,128)S(1)}, u32[]{:S(2)}, u32[]{:S(2)}) async-start(f32[8,40,256]{2,1,0:T(8,128)} %get-tuple-element.29), calls=%async_computation.3 | async-start | bytes 655360 | tf_op jit(solution)/shard_map/all_to_all | solution.py:557
  47.8 9.2 %all-to-all-start.4 = ((f32[8,16,128]{2,1,0:T(8,128)}), f32[8,16,128]{2,1,0:T(8,128)S(1)}, u32[]{:S(2)}, u32[]{:S(2)}) async-start(f32[8,16,128]{2,1,0:T(8,128)} %get-tuple-element.32), calls=%async_computation.4 | async-start | bytes 131072 | tf_op jit(solution)/shard_map/all_to_all | solution.py:559
  68.2 4.3 %collective-permute-start = (f32[64,256]{1,0:T(8,128)S(1)}, f32[64,256]{1,0:T(8,128)S(1)}, u32[]{:S(2)}, u32[]{:S(2)}) collective-permute-start(f32[64,256]{1,0:T(8,128)S(1)} %get-tuple-element.36), channel_id=1, source_target_pairs={{0,1},{1,0},{2,3},{3,2},{4,5},{5,4},{6,7},{7,6},{8,9},{9,8},{10,11... | collective-permute-start | bytes 196616 | tf_op jit(solution)/shard_map/ppermute | solution.py:548
  69.7 5.0 %collective-permute-start.1 = (f32[64,256]{1,0:T(8,128)S(1)}, f32[64,256]{1,0:T(8,128)S(1)}, u32[]{:S(2)}, u32[]{:S(2)}) collective-permute-start(f32[64,256]{1,0:T(8,128)S(1)} %get-tuple-element.37), channel_id=1, source_target_pairs={{0,2},{1,3},{2,0},{3,1},{4,6},{5,7},{6,4},{7,5},{8,10},{9,11},{10,... | collective-permute-start | bytes 196616 | tf_op jit(solution)/shard_map/ppermute | solution.py:548
  71.2 5.2 %collective-permute-start.2 = (f32[64,256]{1,0:T(8,128)S(1)}, f32[64,256]{1,0:T(8,128)S(1)}, u32[]{:S(2)}, u32[]{:S(2)}) collective-permute-start(f32[64,256]{1,0:T(8,128)S(1)} %get-tuple-element.38), channel_id=1, source_target_pairs={{0,3},{1,2},{2,1},{3,0},{4,7},{5,6},{6,5},{7,4},{8,11},{9,10},{10,... | collective-permute-start | bytes 196616 | tf_op jit(solution)/shard_map/ppermute | solution.py:548

commit v5 on v4

--- a/solution.py
+++ b/solution.py
@@ -116,83 +116,54 @@
 
 
 def exchange(keys, vals, a, b, down):
-    if down is True:
-        swap = keys[a] < keys[b]
-    else:
-        swap = keys[a] > keys[b]
-        if down is not False:
-            swap = jnp.logical_xor(swap, down)
-    keys[a], keys[b] = jnp.where(swap, keys[b], keys[a]), jnp.where(swap, keys[a], keys[b])
+    if down:
+        a, b = b, a
+    swap = keys[a] > keys[b]
+    keys[a], keys[b] = jnp.minimum(keys[a], keys[b]), jnp.maximum(keys[a], keys[b])
     vals[a], vals[b] = jnp.where(swap, vals[b], vals[a]), jnp.where(swap, vals[a], vals[b])
 
 
-def sort_inner(key_ref, val_ref, level, places, group):
-    pairs = key_ref.shape[0]
-    steps = []
-    down = places.mask(level) if level < places.total_bits else False
-    for bit in range(level - 1, places.tile_bits - 1, -1):
-        steps.append((places.mask(bit),) + places.axis_distance(bit))
+def sort_registers(keys, vals):
+    tiles = len(keys)
+    tile_bits = tiles.bit_length() - 1
+    places = Places(tile_bits, tile_bits + 10)
+
+    def flip(bit):
+        return jnp.where(places.mask(bit), -1.0, 1.0)
+
+    def trade_all(bit):
+        upper, (axis, distance) = places.mask(bit), places.axis_distance(bit)
         places.swap(bit)
-
-    def body(g, carry):
-        part = pl.ds(g * group, group)
-        keys = [key_ref[part, 0], key_ref[part, 1]]
-        vals = [val_ref[part, 0], val_ref[part, 1]]
-        for upper, axis, distance in steps:
-            keys = list(trade(*keys, upper, axis, distance))
-            vals = list(trade(*vals, upper, axis, distance))
-            exchange(keys, vals, 0, 1, down)
-        for i in range(2):
-            key_ref[part, i] = keys[i]
-            val_ref[part, i] = vals[i]
-        return carry
-
-    lax.fori_loop(0, pairs // group, body, 0)
-
-
-def sort_across(key_ref, val_ref, level, places):
-    tiles = 2 * key_ref.shape[0]
-    tile_bits = places.tile_bits
-    mask = places.mask(level) if tile_bits <= level < places.total_bits else None
-    back = None
-    if level > tile_bits:
-        back = (places.mask(0),) + places.axis_distance(0)
-        places.swap(0)
-    bits = list(range(min(level, tile_bits) - 1, -1, -1))
-    for chosen in [bits[:-3], bits[-3:]] if len(bits) > 3 else [bits]:
-        low = min(chosen)
-        members, stride = 1 << len(chosen), 1 << low
-        for g in range(tiles // members):
-            base = (g // stride) * (members * stride) + g % stride
-            spots = [divmod(base + i * stride, 2) for i in range(members)]
-            keys = [key_ref[spot] for spot in spots]
-            vals = [val_ref[spot] for spot in spots]
-            for bit in chosen:
-                step = 1 << (bit - low)
-                for i in range(members):
-                    if i & step:
-                        continue
-                    if bit == 0 and back is not None:
-                        keys[i], keys[i + 1] = trade(keys[i], keys[i + 1], *back)
-                        vals[i], vals[i + 1] = trade(vals[i], vals[i + 1], *back)
-                    down = mask
-                    if level >= places.total_bits:
-                        down = False
-                    elif level < tile_bits:
-                        down = ((base + i * stride) >> level) & 1 == 1
-                    exchange(keys, vals, i, i + step, down)
-            for spot, key, val in zip(spots, keys, vals):
-                key_ref[spot] = key
-                val_ref[spot] = val
+        for i in range(0, tiles, 2):
+            keys[i], keys[i + 1] = trade(keys[i], keys[i + 1], upper, axis, distance)
+            vals[i], vals[i + 1] = trade(vals[i], vals[i + 1], upper, axis, distance)
+
+    for level in range(1, places.total_bits + 1):
+        if level >= tile_bits:
+            sign = 1.0
+            if level > tile_bits:
+                sign = flip(level - 1)
+            if level < places.total_bits:
+                sign = sign * flip(level)
+            for i in range(tiles):
+                keys[i] = keys[i] * sign
+        for bit in range(level - 1, -1, -1):
+            if bit >= tile_bits or (bit == 0 and level > tile_bits):
+                trade_all(bit)
+            step = 1 << bit if bit < tile_bits else 1
+            for i in range(tiles):
+                if not i & step:
+                    exchange(keys, vals, i, i + step, level < tile_bits and (i >> level) & 1 == 1)
+    assert places.of == list(range(places.total_bits))
 
 
 def sort_kernel(
-    scan_hbm, resp_hbm, cycle_hbm, column_hbm, twiddle_hbm, forward_hbm,
-    filtered_ref, send_ref,
-    scan_ref, resp_ref, cycle_ref, column_ref, twiddle_ref, forward_ref, arrived,
-    key_ref, val_ref, spec_ref, key_rows, val_rows,
-    *, buckets, span, rows, windows,
+    me_ref, scan_hbm, resp_hbm, cycle_hbm, column_hbm, twiddle_hbm, forward_hbm, filtered_ref, *refs,
+    buckets, span, rows, windows,
 ):
+    send_refs, refs = refs[:buckets // windows], refs[buckets // windows:]
+    scan_ref, resp_ref, cycle_ref, column_ref, twiddle_ref, forward_ref, arrived = refs[:7]
+    key_ref, val_ref, spec_ref, key_rows, val_rows = refs[7:]
     lines, length = scan_ref.shape
     outer = length // LANES
     loads = [
@@ -228,49 +199,51 @@
         re.append(ur * c - ui * s)
         im.append(ui * c + ur * s)
     out, _ = small_fft(re, im, 1)
+    keys = []
     for n in range(outer):
         cols = slice(n * LANES, (n + 1) * LANES)
         filtered_ref[:, cols] = out[n]
-        val_ref[divmod(n, 2)] = out[n]
-        key_ref[divmod(n, 2)] = (cycle_ref[:, cols] * NPHI + column_ref[:, cols]).astype(jnp.float32)
-    tiles = outer
-    tile_bits = tiles.bit_length() - 1
-    places = Places(tile_bits, tile_bits + 10)
-    for level in range(1, places.total_bits + 1):
-        if level > tile_bits:
-            sort_inner(key_ref, val_ref, level, places, min(8, tiles // 2))
-        sort_across(key_ref, val_ref, level, places)
-    assert places.of == list(range(places.total_bits))
-    row_len = tiles * SUB
-    keys = key_ref[...].reshape(tiles, SUB, LANES)
-    last = jnp.max(jnp.max(keys, axis=0), axis=0, keepdims=True)
-    first = jnp.min(jnp.min(keys, axis=0), axis=0, keepdims=True)
-    key_rows[:LANES, :] = keys.reshape(row_len, LANES).T
-    val_rows[:LANES, :] = val_ref[...].reshape(row_len, LANES).T
+        keys.append((cycle_ref[:, cols] * NPHI + column_ref[:, cols]).astype(jnp.float32))
+    vals = list(out)
+    sort_registers(keys, vals)
+    row_len = outer * SUB
+    last = functools.reduce(jnp.maximum, keys)
+    first = functools.reduce(jnp.minimum, keys)
+    last = jnp.max(last, axis=0, keepdims=True)
+    first = jnp.min(first, axis=0, keepdims=True)
+    for i in range(outer):
+        key_ref[i * SUB:(i + 1) * SUB, :] = keys[i]
+        val_ref[i * SUB:(i + 1) * SUB, :] = vals[i]
+    key_rows[:LANES, :] = key_ref[...].T
+    val_rows[:LANES, :] = val_ref[...].T
     reach = key_rows.shape[0] - LANES
     key_rows[LANES:, :] = jnp.full((reach, row_len), 2.0 * buckets * span, jnp.float32)
     val_rows[LANES:, :] = jnp.zeros((reach, row_len), jnp.float32)
     over = jnp.int32(0)
-    for b in range(buckets):
-        begin = jnp.sum((last < float(b * span)).astype(jnp.float32)).astype(jnp.int32)
-        end = jnp.sum((first < float((b + 1) * span)).astype(jnp.float32)).astype(jnp.int32)
-        over = over + (end - begin > rows).astype(jnp.int32)
-        begin = jnp.minimum(begin, LANES)
-        aligned = pl.multiple_of((begin // SUB) * SUB, SUB)
-        back = lax.rem(reach - (begin - aligned), reach)
-        here = pl.ds(aligned, reach)
-        dest, w = divmod(b, windows)
-        taken = pltpu.roll(key_rows[here, :], back, axis=0)[:rows]
-        send_ref[dest, w * rows:(w + 1) * rows, :] = taken - float(b * span)
-        at = (windows + w) * rows
-        send_ref[dest, at:at + rows, :] = pltpu.roll(val_rows[here, :], back, axis=0)[:rows]
+    for k, send_ref in enumerate(send_refs):
+        for w in range(windows):
+            bucket = (me_ref[0] ^ k) * windows + w
+            low = (bucket * span).astype(jnp.float32)
+            high = low + float(span)
+            begin = jnp.sum((last < low).astype(jnp.float32)).astype(jnp.int32)
+            end = jnp.sum((first < high).astype(jnp.float32)).astype(jnp.int32)
+            over = over + (end - begin > rows).astype(jnp.int32)
+            begin = jnp.minimum(begin, LANES)
+            aligned = pl.multiple_of((begin // SUB) * SUB, SUB)
+            back = lax.rem(reach - (begin - aligned), reach)
+            here = pl.ds(aligned, reach)
+            taken = pltpu.roll(key_rows[here, :], back, axis=0)[:rows]
+            send_ref[w * rows:(w + 1) * rows, :] = taken - low
+            at = (windows + w) * rows
+            send_ref[at:at + rows, :] = pltpu.roll(val_rows[here, :], back, axis=0)[:rows]
 
     @pl.when(over > 0)
     def _():
-        send_ref[...] = jnp.full(send_ref.shape, jnp.nan, jnp.float32)
-
-
-def filter_and_sort(scan, resp, cycle, column, det_count, band_cycles):
+        for send_ref in send_refs:
+            send_ref[...] = jnp.full(send_ref.shape, jnp.nan, jnp.float32)
+
+
+def filter_and_sort(me, scan, resp, cycle, column, det_count, band_cycles):
     lines, length = scan.shape
     tiles = length // LANES
     windows = WINDOWS
@@ -288,21 +261,21 @@
         body,
         out_shape=(
             jax.ShapeDtypeStruct((lines, length), jnp.float32),
-            jax.ShapeDtypeStruct((det_count, 2 * windows * rows, row_len), jnp.float32),
-        ),
-        in_specs=[pl.BlockSpec(memory_space=pltpu.HBM)] * len(operands),
-        out_specs=(vmem, vmem),
+        ) + (jax.ShapeDtypeStruct((2 * windows * rows, row_len), jnp.float32),) * det_count,
+        in_specs=[pl.BlockSpec(memory_space=pltpu.SMEM)]
+        + [pl.BlockSpec(memory_space=pltpu.HBM)] * len(operands),
+        out_specs=(vmem,) * (1 + det_count),
         scratch_shapes=[pltpu.VMEM(x.shape, x.dtype) for x in operands] + [
             pltpu.SemaphoreType.DMA((len(operands),)),
-            pltpu.VMEM((tiles // 2, 2, SUB, LANES), jnp.float32),
-            pltpu.VMEM((tiles // 2, 2, SUB, LANES), jnp.float32),
+            pltpu.VMEM((row_len, LANES), jnp.float32),
+            pltpu.VMEM((row_len, LANES), jnp.float32),
             pltpu.VMEM((tiles * lines, 2 * LANES), jnp.float32),
             pltpu.VMEM((LANES + reach, row_len), jnp.float32),
             pltpu.VMEM((LANES + reach, row_len), jnp.float32),
         ],
-        compiler_params=pltpu.CompilerParams(vmem_limit_bytes=24 * 1024 * 1024),
+        compiler_params=pltpu.CompilerParams(vmem_limit_bytes=63 * 1024 * 1024),
         name="filter_sort",
-    )(*operands)
+    )(me, *operands)
 
 
 def split2(x):
@@ -312,11 +285,13 @@
 
 
 def bin_kernel(
-    recv_ref, pick_ref, table_hi, table_lo, map_ref, send_ref, flag_ref,
-    left_a, left_b, right_a, right_b, acc_ref, *, windows, rows, window_cycles
+    *refs, sources, windows, rows, window_cycles
 ):
+    recv_refs, (pick_ref, table_hi, table_lo, map_ref, send_ref, flag_ref) = refs[:sources], refs[sources:-6]
+    recv_ref, left_a, left_b, right_a, right_b, acc_ref = refs[-6:]
+    for e in range(sources):
+        recv_ref[e] = recv_refs[e][...]
     left_refs, right_refs = (left_a, left_b), (right_a, right_b)
-    sources = recv_ref.shape[0]
     row_len = recv_ref.shape[2]
     parts = NPHI // ROW
     area = parts * window_cycles
@@ -405,7 +380,8 @@
 
 
 def bin_and_modes(recv, order_slot, band_cycles):
-    sources, lines, row_len = recv.shape
+    sources = len(recv)
+    lines, row_len = recv[0].shape
     windows = WINDOWS
     rows = lines // (2 * windows)
     cycles = band_cycles // sources
@@ -421,15 +397,16 @@
     depth = rows * row_len
     vmem = pl.BlockSpec(memory_space=pltpu.VMEM)
     return pl.pallas_call(
-        functools.partial(bin_kernel, windows=windows, rows=rows, window_cycles=cycles // windows),
+        functools.partial(bin_kernel, sources=sources, windows=windows, rows=rows, window_cycles=cycles // windows),
         out_shape=(
             jax.ShapeDtypeStruct((cycles, NPHI), jnp.float32),
             jax.ShapeDtypeStruct((sources, cycles // groups, LANES), jnp.float32),
             jax.ShapeDtypeStruct((1,), jnp.int32),
         ),
-        in_specs=[vmem] * 4,
+        in_specs=[vmem] * (sources + 3),
         out_specs=(vmem, vmem, pl.BlockSpec(memory_space=pltpu.SMEM)),
         scratch_shapes=[
+            pltpu.VMEM((sources, lines, row_len), jnp.float32),
             pltpu.VMEM((3 * area, depth), jnp.bfloat16),
             pltpu.VMEM((3 * area, depth), jnp.bfloat16),
             pltpu.VMEM((ROW, depth), jnp.bfloat16),
@@ -438,7 +415,7 @@
         ],
         compiler_params=pltpu.CompilerParams(vmem_limit_bytes=40 * 1024 * 1024),
         name="bin_modes",
-    )(recv, pick, jnp.asarray(high), jnp.asarray(low))
+    )(*recv, pick, jnp.asarray(high), jnp.asarray(low))
 
 
 def legendre_kernel(me_ref, recv_ref, table_ref, *refs, owners):
@@ -551,10 +528,11 @@
 
 def local(scan_lines, response, cycle_offset, column, order_slot, legendre, *, det_count, band_count):
     slots, band_cycles, degrees = legendre.shape
-    filtered, send = filter_and_sort(
-        scan_lines, response, cycle_offset, column, det_count, band_cycles
+    me = lax.axis_index("det").astype(jnp.int32).reshape(1)
+    filtered, *send = filter_and_sort(
+        me, scan_lines, response, cycle_offset, column, det_count, band_cycles
     )
-    recv = lax.all_to_all(send, "det", split_axis=0, concat_axis=0, tiled=True)
+    recv = swap_blocks(send, "det")
     sky_map, modes, crowded = bin_and_modes(recv, order_slot, band_cycles)
     modes = lax.all_to_all(modes, "det", split_axis=0, concat_axis=0, tiled=True)
     sky_map, modes = lax.cond(

time: 77.5 us -> 71.6 us (0.924)
  Pallas kernels: 36.7 us -> 31.9 us
  waiting for transfers between devices: 19.8 us -> 15.1 us
  starting transfers between devices: 13.3 us -> 16.6 us
  local copies, waits for them, and re-layouts: 4.37 us -> 5.48 us
    all_to_all x1 -> x0, waiting for transfers between devices: 10.1 us -> none  [local(): recv = lax.all_to_all(send, 'det', split_axis=0, concat_axis=0, tiled=True)]
    ppermute x3 -> x10, starting transfers between devices: 3.55 us -> 13.3 us  [swap_blocks(): lax.ppermute(blocks[k], axis, [(i, i ^ k) for i in range(count)])]
    all_to_all x1 -> x0, starting transfers between devices: 6.34 us -> none  [local(): recv = lax.all_to_all(send, 'det', split_axis=0, concat_axis=0, tiled=True)]
    ppermute x3 -> x10, waiting for transfers between devices: 4.61 us -> 9.92 us  [swap_blocks(): lax.ppermute(blocks[k], axis, [(i, i ^ k) for i in range(count)])]
    pallas_call x1, Pallas kernels: 13.4 us -> 8.55 us  [filter_and_sort(): pl.pallas_call(body, out_shape=(jax.ShapeDtypeStruct((lines, length), jnp...]
    unnamed x16 -> x12, local copies, waits for them, and re-layouts: 2.63 us -> 3.24 us
  transfers between devices with their start and end apart: 5 -> 11, of which waited for: 5 -> 7; matrix products, arithmetic and copies ran while one was open for 2% -> 1% of each run, Pallas kernels for 0% -> 0%
where the time goes in v5:
time: 71.6 us; the launch traced here: 71.3 us
  Pallas kernels  31.9 us (45%)
  starting transfers between devices  16.6 us (23%)
  waiting for transfers between devices  15.1 us (21%)
  local copies, waits for them, and re-layouts  5.48 us (8%)
  between operations  1.29 us (2%)
  other arithmetic  0.81 us (1%)
    ppermute x10, starting transfers between devices, swap_blocks(): lax.ppermute(blocks[k], axis, [(i, i ^ k) for i in range(count)])  13.3 us
    pallas_call x1, Pallas kernels, bin_and_modes(): pl.pallas_call(functools.partial(bin_kernel, sources=sources, windows=win...  12.2 us
    pallas_call x1, Pallas kernels, legendre_sums(): pl.pallas_call(functools.partial(legendre_kernel, owners=owners), out_sha...  11.2 us
    ppermute x10, waiting for transfers between devices, swap_blocks(): lax.ppermute(blocks[k], axis, [(i, i ^ k) for i in range(count)])  9.92 us
    pallas_call x1, Pallas kernels, filter_and_sort(): pl.pallas_call(body, out_shape=(jax.ShapeDtypeStruct((lines, length), jnp...  8.55 us
    all_to_all x1, waiting for transfers between devices, local(): lax.all_to_all(modes, 'det', split_axis=0, concat_axis=0, tiled=True)  5.21 us
    all_to_all x1, starting transfers between devices, local(): lax.all_to_all(modes, 'det', split_axis=0, concat_axis=0, tiled=True)  3.36 us
    unnamed x12, local copies, waits for them, and re-layouts  3.24 us
  transfers between devices with their start and end apart: 11, of which 7 were waited for; matrix products, arithmetic and copies ran while one was open for 1% of the time, Pallas kernels for 0%

profile of v5, /device:TPU:0, one launch (start us, length us, event | category | flops | bytes accessed | tf_op | source)
XLA Modules:
  0.0 71.3 jit_solution(15251804247225724953)
XLA Ops:
  0.6 1.1 %reshape.151 = f32[8,128,32]{2,1,0:T(8,128)S(1)} reshape(f32[8,4096]{1,0:T(8,128)} %param.13) | data formatting | bytes 262144 | tf_op jit(solution)/shard_map/reshape | solution.py:256
  1.8 0.8 %copy.17 = f32[32,8,128]{2,1,0:T(8,128)} copy(f32[32,8,128]{0,2,1:T(8,128)S(1)} %bitcast.18) | data formatting | bytes 262144 | tf_op jit(solution)/shard_map/transpose | solution.py:256
  2.6 8.6 %filter_sort.1 = (f32[8,4096]{1,0:T(8,128)S(1)}, f32[40,256]{1,0:T(8,128)}, f32[40,256]{1,0:T(8,128)}, f32[40,256]{1,0:T(8,128)}, f32[40,256]{1,0:T(8,128)}, /*i...) custom-call(s32[1]{0:T(128)} %bitcast.3.me_ref, f32[8,4096]{1,0:T(8,128)} %scan_hbm.1, ...), custom_call_target="tpu_custom_call" | custom-call | tf_op jit(solution)/shard_map/filter_sort/pallas_call | solution.py:260
  11.1 0.5 collective-permute-start
  11.7 2.6 %collective-permute-start.1 = (f32[40,256]{1,0:T(8,128)}, f32[40,256]{1,0:T(8,128)S(1)}, u32[]{:S(2)}, u32[]{:S(2)}) collective-permute-start(f32[40,256]{1,0:T(8,128)} %get-tuple-element.38), channel_id=1, source_target_pairs={{0,8},{4,12},{8,0},{12,4},{16,24},{20,28},{24,16},{28,20},{1,9},{5... | collective-permute-start | bytes 122888 | tf_op jit(solution)/shard_map/ppermute | solution.py:525
  14.4 2.8 %collective-permute-start.3 = (f32[40,256]{1,0:T(8,128)}, f32[40,256]{1,0:T(8,128)S(1)}, u32[]{:S(2)}, u32[]{:S(2)}) collective-permute-start(f32[40,256]{1,0:T(8,128)} %get-tuple-element.40), channel_id=1, source_target_pairs={{0,16},{4,20},{8,24},{12,28},{16,0},{20,4},{24,8},{28,12},{1,17},{... | collective-permute-start | bytes 122888 | tf_op jit(solution)/shard_map/ppermute | solution.py:525
  17.3 3.6 %collective-permute-start.5 = (f32[40,256]{1,0:T(8,128)}, f32[40,256]{1,0:T(8,128)S(1)}, u32[]{:S(2)}, u32[]{:S(2)}) collective-permute-start(f32[40,256]{1,0:T(8,128)} %get-tuple-element.42), channel_id=1, source_target_pairs={{0,24},{4,28},{8,16},{12,20},{16,8},{20,12},{24,0},{28,4},{1,25},{... | collective-permute-start | bytes 122888 | tf_op jit(solution)/shard_map/ppermute | solution.py:525
  21.2 0.8 %collective-permute-done.4.refs_5_ = f32[40,256]{1,0:T(8,128)S(1)} collective-permute-done((f32[40,256]{1,0:T(8,128)}, f32[40,256]{1,0:T(8,128)S(1)}, u32[]{:S(2)}, u32[]{:S(2)}) %collective-permute-start.4) | collective-permute-done | bytes 40992 | tf_op jit(solution)/shard_map/ppermute | solution.py:525
  22.0 2.1 %collective-permute-done.5.refs_6_ = f32[40,256]{1,0:T(8,128)S(1)} collective-permute-done((f32[40,256]{1,0:T(8,128)}, f32[40,256]{1,0:T(8,128)S(1)}, u32[]{:S(2)}, u32[]{:S(2)}) %collective-permute-start.5) | collective-permute-done | bytes 40992 | tf_op jit(solution)/shard_map/ppermute | solution.py:525
  24.1 2.4 %collective-permute-done.6.refs_7_ = f32[40,256]{1,0:T(8,128)S(1)} collective-permute-done((f32[40,256]{1,0:T(8,128)}, f32[40,256]{1,0:T(8,128)S(1)}, u32[]{:S(2)}, u32[]{:S(2)}) %collective-permute-start.6) | collective-permute-done | bytes 40992 | tf_op jit(solution)/shard_map/ppermute | solution.py:525
  26.5 1.2 %copy-done = bf16[2,1024,256]{2,1,0:T(8,128)(2,1)S(1)} copy-done((bf16[2,1024,256]{2,1,0:T(8,128)(2,1)S(1)}, bf16[2,1024,256]{2,1,0:T(8,128)(2,1)}, u32[]{:S(2)}) %copy-start) | copy-done | bytes 1048600
  27.8 1.2 %copy-done.1 = bf16[2,1024,256]{2,1,0:T(8,128)(2,1)S(1)} copy-done((bf16[2,1024,256]{2,1,0:T(8,128)(2,1)S(1)}, bf16[2,1024,256]{2,1,0:T(8,128)(2,1)}, u32[]{:S(2)}) %copy-start.1) | copy-done | bytes 1048600
  29.0 0.8 %copy-done.2 = f32[40,256]{1,0:T(8,128)S(1)} copy-done((f32[40,256]{1,0:T(8,128)S(1)}, f32[40,256]{1,0:T(8,128)}, u32[]{:S(2)}) %copy-start.2) | copy-done | bytes 40984
  29.8 12.2 %bin_modes.1 = (f32[32,2048]{1,0:T(8,128)}, f32[8,16,128]{2,1,0:T(8,128)}, s32[1]{0:T(128)}) custom-call(f32[40,256]{1,0:T(8,128)S(1)} %copy-done.2, f32[40,256]{1,0:T(8,128)S(1)} %collective-permute-done.refs_1_, f32[40,256]{1,0:T(8,128)S(1)} %collective-permute-done.1.refs_2_, f32[40,256]{1,0:T(8,128)S(1)} %collective-permute-done.2.refs_3_, ...), custom_call_target="tpu_custom_call" | custom-call | tf_op jit(solution)/shard_map/bin_modes/pallas_call | solution.py:399
  41.9 3.4 %all-to-all-start.3 = ((f32[8,16,128]{2,1,0:T(8,128)}), f32[8,16,128]{2,1,0:T(8,128)S(1)}, u32[]{:S(2)}, u32[]{:S(2)}) async-start(f32[8,16,128]{2,1,0:T(8,128)} %get-tuple-element.46), calls=%async_computation.3 | async-start | bytes 131072 | tf_op jit(solution)/shard_map/all_to_all | solution.py:537
  46.0 5.2 %all-to-all-done.3 = f32[8,16,128]{2,1,0:T(8,128)S(1)} async-done(((f32[8,16,128]{2,1,0:T(8,128)}), f32[8,16,128]{2,1,0:T(8,128)S(1)}, u32[]{:S(2)}, u32[]{:S(2)}) %all-to-all-start.3) | async-done | bytes 65568 | tf_op jit(solution)/shard_map/all_to_all | solution.py:537
  51.2 11.2 %legendre_sums.1 = (f32[64,256]{1,0:T(8,128)S(1)}, f32[64,256]{1,0:T(8,128)S(1)}, f32[64,256]{1,0:T(8,128)S(1)}, f32[64,256]{1,0:T(8,128)S(1)}) custom-call(s32[1]{0:T(128)} %bitcast.2.me_ref, f32[8,16,128]{2,1,0:T(8,128)S(1)} %get-tuple-element.48.recv_ref, f32[32,256,1024]{2,1,0:T(8,128)} %table_ref.1), custom_call_target="tpu_custom_call" | custom-call | tf_op jit(solution)/shard_map/legendre_sums/pallas_call | solution.py:479
  62.4 1.6 %collective-permute-start.7 = (f32[64,256]{1,0:T(8,128)S(1)}, f32[64,256]{1,0:T(8,128)S(1)}, u32[]{:S(2)}, u32[]{:S(2)}) collective-permute-start(f32[64,256]{1,0:T(8,128)S(1)} %get-tuple-element.50), channel_id=1, source_target_pairs={{0,1},{1,0},{2,3},{3,2},{4,5},{5,4},{6,7},{7,6},{8,9},{9,8},{10,11... | collective-permute-start | bytes 196616 | tf_op jit(solution)/shard_map/ppermute | solution.py:525
  63.9 1.5 %collective-permute-start.8 = (f32[64,256]{1,0:T(8,128)S(1)}, f32[64,256]{1,0:T(8,128)S(1)}, u32[]{:S(2)}, u32[]{:S(2)}) collective-permute-start(f32[64,256]{1,0:T(8,128)S(1)} %get-tuple-element.51), channel_id=1, source_target_pairs={{0,2},{1,3},{2,0},{3,1},{4,6},{5,7},{6,4},{7,5},{8,10},{9,11},{10,... | collective-permute-start | bytes 196616 | tf_op jit(solution)/shard_map/ppermute | solution.py:525
  65.4 0.5 collective-permute-start.9
  66.0 0.7 collective-permute-done.7
  66.7 2.2 %collective-permute-done.8 = f32[64,256]{1,0:T(8,128)S(1)} collective-permute-done((f32[64,256]{1,0:T(8,128)S(1)}, f32[64,256]{1,0:T(8,128)S(1)}, u32[]{:S(2)}, u32[]{:S(2)}) %collective-permute-start.8) | collective-permute-done | bytes 65568 | tf_op jit(solution)/shard_map/ppermute | solution.py:525
  68.9 1.7 %collective-permute-done.9 = f32[64,256]{1,0:T(8,128)S(1)} collective-permute-done((f32[64,256]{1,0:T(8,128)S(1)}, f32[64,256]{1,0:T(8,128)S(1)}, u32[]{:S(2)}, u32[]{:S(2)}) %collective-permute-start.9) | collective-permute-done | bytes 65568 | tf_op jit(solution)/shard_map/ppermute | solution.py:525
  70.6 0.6 broadcast_select_fusion
  (28 shorter events, 0.7 us)
Async XLA Ops:
  0.6 16.5 %copy-start.5 = (s32[256]{0:T(256)S(1)}, s32[256]{0:T(256)}, u32[]{:S(2)}) copy-start(s32[256]{0:T(256)} %param.16) | copy-start | bytes 3076
  1.7 49.4 %copy-start.3 = (s32[8,4096]{1,0:T(8,128)S(1)}, s32[8,4096]{1,0:T(8,128)}, u32[]{:S(2)}) copy-start(s32[8,4096]{1,0:T(8,128)} %cycle_hbm.1) | copy-start | bytes 393220
  1.7 49.4 %copy-start.4 = (s32[8,4096]{1,0:T(8,128)S(1)}, s32[8,4096]{1,0:T(8,128)}, u32[]{:S(2)}) copy-start(s32[8,4096]{1,0:T(8,128)} %column_hbm.1) | copy-start | bytes 393220
  11.1 6.2 %collective-permute-start = (f32[40,256]{1,0:T(8,128)}, f32[40,256]{1,0:T(8,128)S(1)}, u32[]{:S(2)}, u32[]{:S(2)}) collective-permute-start(f32[40,256]{1,0:T(8,128)} %get-tuple-element.37), channel_id=1, source_target_pairs={{0,4},{4,0},{8,12},{12,8},{16,20},{20,16},{24,28},{28,24},{1,5},{5... | collective-permute-start | bytes 122888 | tf_op jit(solution)/shard_map/ppermute | solution.py:525
  11.7 9.2 %collective-permute-start.1 = (f32[40,256]{1,0:T(8,128)}, f32[40,256]{1,0:T(8,128)S(1)}, u32[]{:S(2)}, u32[]{:S(2)}) collective-permute-start(f32[40,256]{1,0:T(8,128)} %get-tuple-element.38), channel_id=1, source_target_pairs={{0,8},{4,12},{8,0},{12,4},{16,24},{20,28},{24,16},{28,20},{1,9},{5... | collective-permute-start | bytes 122888 | tf_op jit(solution)/shard_map/ppermute | solution.py:525
  14.3 6.9 %collective-permute-start.2 = (f32[40,256]{1,0:T(8,128)}, f32[40,256]{1,0:T(8,128)S(1)}, u32[]{:S(2)}, u32[]{:S(2)}) collective-permute-start(f32[40,256]{1,0:T(8,128)} %get-tuple-element.39), channel_id=1, source_target_pairs={{0,12},{4,8},{8,4},{12,0},{16,28},{20,24},{24,20},{28,16},{1,13},{... | collective-permute-start | bytes 122888 | tf_op jit(solution)/shard_map/ppermute | solution.py:525
  14.4 6.8 %collective-permute-start.3 = (f32[40,256]{1,0:T(8,128)}, f32[40,256]{1,0:T(8,128)S(1)}, u32[]{:S(2)}, u32[]{:S(2)}) collective-permute-start(f32[40,256]{1,0:T(8,128)} %get-tuple-element.40), channel_id=1, source_target_pairs={{0,16},{4,20},{8,24},{12,28},{16,0},{20,4},{24,8},{28,12},{1,17},{... | collective-permute-start | bytes 122888 | tf_op jit(solution)/shard_map/ppermute | solution.py:525
  17.1 4.9 %collective-permute-start.4 = (f32[40,256]{1,0:T(8,128)}, f32[40,256]{1,0:T(8,128)S(1)}, u32[]{:S(2)}, u32[]{:S(2)}) collective-permute-start(f32[40,256]{1,0:T(8,128)} %get-tuple-element.41), channel_id=1, source_target_pairs={{0,20},{4,16},{8,28},{12,24},{16,4},{20,0},{24,12},{28,8},{1,21},{... | collective-permute-start | bytes 122888 | tf_op jit(solution)/shard_map/ppermute | solution.py:525
  17.3 6.8 %collective-permute-start.5 = (f32[40,256]{1,0:T(8,128)}, f32[40,256]{1,0:T(8,128)S(1)}, u32[]{:S(2)}, u32[]{:S(2)}) collective-permute-start(f32[40,256]{1,0:T(8,128)} %get-tuple-element.42), channel_id=1, source_target_pairs={{0,24},{4,28},{8,16},{12,20},{16,8},{20,12},{24,0},{28,4},{1,25},{... | collective-permute-start | bytes 122888 | tf_op jit(solution)/shard_map/ppermute | solution.py:525
  20.9 5.6 %collective-permute-start.6 = (f32[40,256]{1,0:T(8,128)}, f32[40,256]{1,0:T(8,128)S(1)}, u32[]{:S(2)}, u32[]{:S(2)}) collective-permute-start(f32[40,256]{1,0:T(8,128)} %get-tuple-element.43), channel_id=1, source_target_pairs={{0,28},{4,24},{8,20},{12,16},{16,12},{20,8},{24,4},{28,0},{1,29},{... | collective-permute-start | bytes 122888 | tf_op jit(solution)/shard_map/ppermute | solution.py:525
  26.5 1.2 %copy-start = (bf16[2,1024,256]{2,1,0:T(8,128)(2,1)S(1)}, bf16[2,1024,256]{2,1,0:T(8,128)(2,1)}, u32[]{:S(2)}) copy-start(bf16[2,1024,256]{2,1,0:T(8,128)(2,1)} %constant.61.clone.refs_9_) | copy-start | bytes 3145732
  27.7 1.2 %copy-start.1 = (bf16[2,1024,256]{2,1,0:T(8,128)(2,1)S(1)}, bf16[2,1024,256]{2,1,0:T(8,128)(2,1)}, u32[]{:S(2)}) copy-start(bf16[2,1024,256]{2,1,0:T(8,128)(2,1)} %constant.62.clone.refs_10_) | copy-start | bytes 3145732
  29.0 0.8 %copy-start.2 = (f32[40,256]{1,0:T(8,128)S(1)}, f32[40,256]{1,0:T(8,128)}, u32[]{:S(2)}) copy-start(f32[40,256]{1,0:T(8,128)} %get-tuple-element.36.refs_0_) | copy-start | bytes 122884
  41.9 9.2 %all-to-all-start.3 = ((f32[8,16,128]{2,1,0:T(8,128)}), f32[8,16,128]{2,1,0:T(8,128)S(1)}, u32[]{:S(2)}, u32[]{:S(2)}) async-start(f32[8,16,128]{2,1,0:T(8,128)} %get-tuple-element.46), calls=%async_computation.3 | async-start | bytes 131072 | tf_op jit(solution)/shard_map/all_to_all | solution.py:537
  62.4 4.3 %collective-permute-start.7 = (f32[64,256]{1,0:T(8,128)S(1)}, f32[64,256]{1,0:T(8,128)S(1)}, u32[]{:S(2)}, u32[]{:S(2)}) collective-permute-start(f32[64,256]{1,0:T(8,128)S(1)} %get-tuple-element.50), channel_id=1, source_target_pairs={{0,1},{1,0},{2,3},{3,2},{4,5},{5,4},{6,7},{7,6},{8,9},{9,8},{10,11... | collective-permute-start | bytes 196616 | tf_op jit(solution)/shard_map/ppermute | solution.py:525
  63.9 5.0 %collective-permute-start.8 = (f32[64,256]{1,0:T(8,128)S(1)}, f32[64,256]{1,0:T(8,128)S(1)}, u32[]{:S(2)}, u32[]{:S(2)}) collective-permute-start(f32[64,256]{1,0:T(8,128)S(1)} %get-tuple-element.51), channel_id=1, source_target_pairs={{0,2},{1,3},{2,0},{3,1},{4,6},{5,7},{6,4},{7,5},{8,10},{9,11},{10,... | collective-permute-start | bytes 196616 | tf_op jit(solution)/shard_map/ppermute | solution.py:525
  65.4 5.2 %collective-permute-start.9 = (f32[64,256]{1,0:T(8,128)S(1)}, f32[64,256]{1,0:T(8,128)S(1)}, u32[]{:S(2)}, u32[]{:S(2)}) collective-permute-start(f32[64,256]{1,0:T(8,128)S(1)} %get-tuple-element.52), channel_id=1, source_target_pairs={{0,3},{1,2},{2,1},{3,0},{4,7},{5,6},{6,5},{7,4},{8,11},{9,10},{10,... | collective-permute-start | bytes 196616 | tf_op jit(solution)/shard_map/ppermute | solution.py:525

commit v6 on v5

--- a/solution.py
+++ b/solution.py
@@ -161,7 +161,8 @@
     me_ref, scan_hbm, resp_hbm, cycle_hbm, column_hbm, twiddle_hbm, forward_hbm, filtered_ref, *refs,
     buckets, span, rows, windows,
 ):
-    send_refs, refs = refs[:buckets // windows], refs[buckets // windows:]
+    chips = buckets // windows // 2
+    own_refs, pair_ref, refs = refs[:chips], refs[chips], refs[chips + 1:]
     scan_ref, resp_ref, cycle_ref, column_ref, twiddle_ref, forward_ref, arrived = refs[:7]
     key_ref, val_ref, spec_ref, key_rows, val_rows = refs[7:]
     lines, length = scan_ref.shape
@@ -220,9 +221,11 @@
     key_rows[LANES:, :] = jnp.full((reach, row_len), 2.0 * buckets * span, jnp.float32)
     val_rows[LANES:, :] = jnp.zeros((reach, row_len), jnp.float32)
     over = jnp.int32(0)
-    for k, send_ref in enumerate(send_refs):
+    depth = 2 * windows * rows
+    for j in range(len(own_refs) * 2):
+        send_ref, base = (pair_ref, j // 2 * depth) if j & 1 else (own_refs[j // 2], 0)
         for w in range(windows):
-            bucket = (me_ref[0] ^ k) * windows + w
+            bucket = (me_ref[0] ^ j) * windows + w
             low = (bucket * span).astype(jnp.float32)
             high = low + float(span)
             begin = jnp.sum((last < low).astype(jnp.float32)).astype(jnp.int32)
@@ -232,14 +235,14 @@
             aligned = pl.multiple_of((begin // SUB) * SUB, SUB)
             back = lax.rem(reach - (begin - aligned), reach)
             here = pl.ds(aligned, reach)
-            taken = pltpu.roll(key_rows[here, :], back, axis=0)[:rows]
-            send_ref[w * rows:(w + 1) * rows, :] = taken - low
-            at = (windows + w) * rows
+            at = base + w * rows
+            send_ref[at:at + rows, :] = pltpu.roll(key_rows[here, :], back, axis=0)[:rows] - low
+            at = base + (windows + w) * rows
             send_ref[at:at + rows, :] = pltpu.roll(val_rows[here, :], back, axis=0)[:rows]
 
     @pl.when(over > 0)
     def _():
-        for send_ref in send_refs:
+        for send_ref in own_refs + (pair_ref,):
             send_ref[...] = jnp.full(send_ref.shape, jnp.nan, jnp.float32)
 
 
@@ -252,6 +255,8 @@
     row_len = tiles * SUB
     rows = LANES // buckets + 2
     reach = (rows + 2 * SUB - 2) // SUB * SUB
+    chips = det_count // 2
+    depth = 2 * windows * rows
     twiddle, forward = filter_tables(length)
     resp_rows = resp.reshape(lines, LANES, tiles).transpose(2, 0, 1).reshape(tiles * lines, LANES)
     operands = [scan, resp_rows, cycle, column, jnp.asarray(twiddle), jnp.asarray(forward)]
@@ -261,10 +266,11 @@
         body,
         out_shape=(
             jax.ShapeDtypeStruct((lines, length), jnp.float32),
-        ) + (jax.ShapeDtypeStruct((2 * windows * rows, row_len), jnp.float32),) * det_count,
+        ) + (jax.ShapeDtypeStruct((depth, row_len), jnp.float32),) * chips
+        + (jax.ShapeDtypeStruct((chips * depth, row_len), jnp.float32),),
         in_specs=[pl.BlockSpec(memory_space=pltpu.SMEM)]
-        + [pl.BlockSpec(memory_space=pltpu.HBM)] * len(operands),
-        out_specs=(vmem,) * (1 + det_count),
+        + [pl.BlockSpec(memory_space=pl.ANY)] * len(operands),
+        out_specs=(vmem,) * (chips + 2),
         scratch_shapes=[pltpu.VMEM(x.shape, x.dtype) for x in operands] + [
             pltpu.SemaphoreType.DMA((len(operands),)),
             pltpu.VMEM((row_len, LANES), jnp.float32),
@@ -284,14 +290,24 @@
     return high, low
 
 
-def bin_kernel(
-    *refs, sources, windows, rows, window_cycles
-):
-    recv_refs, (pick_ref, table_hi, table_lo, map_ref, send_ref, flag_ref) = refs[:sources], refs[sources:-6]
-    recv_ref, left_a, left_b, right_a, right_b, acc_ref = refs[-6:]
-    for e in range(sources):
-        recv_ref[e] = recv_refs[e][...]
+def bin_kernel(me_ref, *refs, sources, windows, rows, window_cycles):
+    chips = sources // 2
+    recv_hbm, (pick_hbm, hi_hbm, lo_hbm) = refs[:chips + 1], refs[chips + 1:chips + 4]
+    map_ref, own_refs, pair_ref = refs[chips + 4], refs[chips + 5:2 * chips + 5], refs[2 * chips + 5]
+    flag_ref, recv_ref, left_a, left_b, right_a, right_b, acc_ref = refs[2 * chips + 6:2 * chips + 13]
+    pick_ref, table_hi, table_lo, blocks_ref, arrived = refs[2 * chips + 13:]
     left_refs, right_refs = (left_a, left_b), (right_a, right_b)
+    deep = 2 * windows * rows
+    parts = [(recv_hbm[0], recv_ref.at[0]), (recv_hbm[1].at[pl.ds(0, deep)], recv_ref.at[1])]
+    for k in range(1, chips):
+        for half in range(2):
+            parts.append((recv_hbm[k + 1].at[pl.ds(half * deep, deep)], recv_ref.at[2 * k + half]))
+    parts += [(pick_hbm, pick_ref), (hi_hbm, table_hi), (lo_hbm, table_lo)]
+    loads = [pltpu.make_async_copy(a, b, arrived.at[i]) for i, (a, b) in enumerate(parts)]
+    for load in loads:
+        load.start()
+    for load in loads[:sources]:
+        load.wait()
     row_len = recv_ref.shape[2]
     parts = NPHI // ROW
     area = parts * window_cycles
@@ -345,6 +361,8 @@
             map_ref[w * window_cycles:(w + 1) * window_cycles, c8 * ROW:(c8 + 1) * ROW] = (
                 sky[c8 * window_cycles:(c8 + 1) * window_cycles]
             )
+    for load in loads[sources:]:
+        load.wait()
     cycles = map_ref.shape[0]
     half = NPHI // 2
     modes = []
@@ -366,21 +384,25 @@
     choose = jnp.where(choose, 1.0, 0.0).astype(jnp.bfloat16)
     moved = jnp.dot(pieces, choose, preferred_element_type=jnp.float32)
     moved = moved[:cycles] + moved[cycles:2 * cycles] + moved[2 * cycles:]
-    owners, group_rows, lanes = send_ref.shape
+    group_rows, lanes = own_refs[0].shape
     groups = cycles // group_rows
     lane_group = lax.broadcasted_iota(jnp.int32, (group_rows, lanes), 1) // (lanes // groups)
     values = recv_ref[:, windows * rows:, :]
     flag_ref[0] = (jnp.max(jnp.where(values == values, 0.0, 1.0)) > 0.0).astype(jnp.int32)
-    for d in range(owners):
+    for d in range(sources):
         block = moved[:, d * lanes:(d + 1) * lanes]
         out = block[:group_rows]
         for h in range(1, groups):
             out = jnp.where(lane_group == h, block[h * group_rows:(h + 1) * group_rows], out)
-        send_ref[d] = out
-
-
-def bin_and_modes(recv, order_slot, band_cycles):
-    sources = len(recv)
+        blocks_ref[d] = out
+    for k in range(chips):
+        own_refs[k][...] = blocks_ref[me_ref[0] ^ (2 * k)]
+        pair_ref[k * group_rows:(k + 1) * group_rows, :] = blocks_ref[me_ref[0] ^ (2 * k + 1)]
+
+
+def bin_and_modes(me, recv, order_slot, band_cycles):
+    chips = len(recv) - 1
+    sources = 2 * chips
     lines, row_len = recv[0].shape
     windows = WINDOWS
     rows = lines // (2 * windows)
@@ -395,16 +417,20 @@
     pick = jnp.broadcast_to(pick, (sources, groups, 2, slots)).reshape(1, sources * LANES)
     area = cycles // windows * (NPHI // ROW)
     depth = rows * row_len
+    block = (cycles // groups, LANES)
     vmem = pl.BlockSpec(memory_space=pltpu.VMEM)
     return pl.pallas_call(
-        functools.partial(bin_kernel, sources=sources, windows=windows, rows=rows, window_cycles=cycles // windows),
-        out_shape=(
-            jax.ShapeDtypeStruct((cycles, NPHI), jnp.float32),
-            jax.ShapeDtypeStruct((sources, cycles // groups, LANES), jnp.float32),
+        functools.partial(
+            bin_kernel, sources=sources, windows=windows, rows=rows, window_cycles=cycles // windows
+        ),
+        out_shape=(jax.ShapeDtypeStruct((cycles, NPHI), jnp.float32),)
+        + (jax.ShapeDtypeStruct(block, jnp.float32),) * chips
+        + (
+            jax.ShapeDtypeStruct((chips * block[0], LANES), jnp.float32),
             jax.ShapeDtypeStruct((1,), jnp.int32),
         ),
-        in_specs=[vmem] * (sources + 3),
-        out_specs=(vmem, vmem, pl.BlockSpec(memory_space=pltpu.SMEM)),
+        in_specs=[pl.BlockSpec(memory_space=pltpu.SMEM)] + [pl.BlockSpec(memory_space=pl.ANY)] * (chips + 4),
+        out_specs=(vmem,) * (chips + 2) + (pl.BlockSpec(memory_space=pltpu.SMEM),),
         scratch_shapes=[
             pltpu.VMEM((sources, lines, row_len), jnp.float32),
             pltpu.VMEM((3 * area, depth), jnp.bfloat16),
@@ -412,13 +438,19 @@
             pltpu.VMEM((ROW, depth), jnp.bfloat16),
             pltpu.VMEM((ROW, depth), jnp.bfloat16),
             pltpu.VMEM((3 * area, ROW), jnp.float32),
+            pltpu.VMEM(pick.shape, jnp.int32),
+            pltpu.VMEM(high.shape, jnp.bfloat16),
+            pltpu.VMEM(low.shape, jnp.bfloat16),
+            pltpu.VMEM((sources,) + block, jnp.float32),
+            pltpu.SemaphoreType.DMA((sources + 3,)),
         ],
-        compiler_params=pltpu.CompilerParams(vmem_limit_bytes=40 * 1024 * 1024),
+        compiler_params=pltpu.CompilerParams(vmem_limit_bytes=63 * 1024 * 1024),
         name="bin_modes",
-    )(*recv, pick, jnp.asarray(high), jnp.asarray(low))
-
-
-def legendre_kernel(me_ref, recv_ref, table_ref, *refs, owners):
+    )(me, *recv, pick, jnp.asarray(high), jnp.asarray(low))
+
+
+def legendre_kernel(me_ref, *refs, chips, owners):
+    recv_refs, table_ref, refs = refs[:chips + 1], refs[chips + 1], refs[chips + 2:]
     out_refs, (leg_ref, arrived, modes_ref, wide_ref, sums_ref) = refs[:owners], refs[owners:]
     slots, band_cycles, degrees = table_ref.shape
 
@@ -430,16 +462,19 @@
         return carry
 
     lax.fori_loop(0, slots, start, 0)
-    sources, group_rows, lanes = recv_ref.shape
+    group_rows, lanes = recv_refs[0].shape
     groups = lanes // (2 * slots)
     width = out_refs[0].shape[1]
     tiles = degrees // LANES
-    for e in range(sources):
-        block = recv_ref[e]
-        for h in range(groups):
-            at = (e * groups + h) * group_rows
-            turned = block if h == 0 else pltpu.roll(block, lanes - h * 2 * slots, axis=1)
-            modes_ref[at:at + group_rows, :] = turned
+    cycles = group_rows * groups
+    for j in range(2 * chips):
+        if j < 2:
+            block = recv_refs[j][:group_rows, :]
+        else:
+            block = recv_refs[j // 2 + 1][j % 2 * group_rows:(j % 2 + 1) * group_rows, :]
+        turned = [block] + [pltpu.roll(block, lanes - h * 2 * slots, axis=1) for h in range(1, groups)]
+        at = pl.multiple_of((me_ref[0] ^ j) * cycles, cycles)
+        modes_ref[pl.ds(at, cycles), :] = jnp.concatenate(turned, axis=0)
 
     def widen(slot, half):
         turned = pltpu.roll(modes_ref[...], lax.rem(lanes - slot, lanes), axis=1)
@@ -470,16 +505,16 @@
 
     lax.fori_loop(0, slots, body, 0)
     for k in range(owners):
-        out_refs[k][...] = sums_ref[me_ref[0] ^ k]
+        out_refs[k][...] = sums_ref[me_ref[1] ^ k]
 
 
 def legendre_sums(me, recv, legendre, owners):
     slots, band_cycles, degrees = legendre.shape
     vmem = pl.BlockSpec(memory_space=pltpu.VMEM)
     return pl.pallas_call(
-        functools.partial(legendre_kernel, owners=owners),
+        functools.partial(legendre_kernel, chips=len(recv) - 1, owners=owners),
         out_shape=(jax.ShapeDtypeStruct((2 * slots, degrees // owners), jnp.float32),) * owners,
-        in_specs=[pl.BlockSpec(memory_space=pltpu.SMEM), vmem, pl.BlockSpec(memory_space=pl.ANY)],
+        in_specs=[pl.BlockSpec(memory_space=pltpu.SMEM)] + [vmem] * len(recv) + [pl.BlockSpec(memory_space=pl.ANY)],
         out_specs=(vmem,) * owners,
         scratch_shapes=[
             pltpu.VMEM(legendre.shape, jnp.float32),
@@ -490,7 +525,7 @@
         ],
         compiler_params=pltpu.CompilerParams(vmem_limit_bytes=44 * 1024 * 1024),
         name="legendre_sums",
-    )(me, recv, legendre)
+    )(me, *recv, legendre)
 
 
 def exchange_and_sum(x, axis, count):
@@ -516,7 +551,22 @@
     groups = LANES // (2 * slots)
     blocks = modes.reshape(2, groups, -1, det_count, slots).transpose(3, 2, 1, 0, 4)
     blocks = blocks.reshape(det_count, -1, LANES)
-    return sky_map, lax.all_to_all(blocks, "det", split_axis=0, concat_axis=0, tiled=True)
+    me = lax.axis_index("det")
+    mine = [lax.dynamic_index_in_dim(blocks, me ^ j, 0, keepdims=False) for j in range(det_count)]
+    return (sky_map, *two_level_swap(mine[0::2], jnp.concatenate(mine[1::2]), "det"))
+
+
+def two_level_swap(own, pair, axis):
+    chips, rows = len(own), own[0].shape[0]
+    pair = lax.ppermute(pair, axis, [(i, i ^ 1) for i in range(2 * chips)])
+    both = {}
+    for k in range(chips - 1, 0, -1):
+        both[k] = lax.ppermute(
+            jnp.concatenate([own[k], pair[k * rows:(k + 1) * rows]]),
+            axis,
+            [(i, i ^ (2 * k)) for i in range(2 * chips)],
+        )
+    return [own[0], pair] + [both[k] for k in range(1, chips)]
 
 
 def swap_blocks(blocks, axis):
@@ -528,20 +578,20 @@
 
 def local(scan_lines, response, cycle_offset, column, order_slot, legendre, *, det_count, band_count):
     slots, band_cycles, degrees = legendre.shape
-    me = lax.axis_index("det").astype(jnp.int32).reshape(1)
-    filtered, *send = filter_and_sort(
+    band = lax.axis_index("band").astype(jnp.int32)
+    me = jnp.stack([lax.axis_index("det").astype(jnp.int32), band])
+    filtered, *own, pair = filter_and_sort(
         me, scan_lines, response, cycle_offset, column, det_count, band_cycles
     )
-    recv = swap_blocks(send, "det")
-    sky_map, modes, crowded = bin_and_modes(recv, order_slot, band_cycles)
-    modes = lax.all_to_all(modes, "det", split_axis=0, concat_axis=0, tiled=True)
-    sky_map, modes = lax.cond(
+    recv = two_level_swap(own, pair, "det")
+    sky_map, *own, pair, crowded = bin_and_modes(me, recv, order_slot, band_cycles)
+    modes = two_level_swap(own, pair, "det")
+    sky_map, *modes = lax.cond(
         crowded[0] > 0,
         lambda: dense_path(filtered, cycle_offset, column, order_slot, band_cycles, det_count),
-        lambda: (sky_map, modes),
+        lambda: (sky_map, *modes),
     )
-    band = lax.axis_index("band").astype(jnp.int32)
-    terms = swap_blocks(legendre_sums(band.reshape(1), modes, legendre, band_count), "band")
+    terms = swap_blocks(legendre_sums(me, modes, legendre, band_count), "band")
     sums = functools.reduce(jnp.add, terms)
     local_orders = lax.dynamic_slice_in_dim(order_slot, lax.axis_index("det") * slots, slots, 0)
     width = degrees // band_count

time: 71.6 us -> 77.5 us (1.082)
  other arithmetic: 0.81 us -> 5.89 us
  Pallas kernels: 31.9 us -> 35.4 us
  starting transfers between devices: 16.6 us -> 14.1 us
  local copies, waits for them, and re-layouts: 5.48 us -> 4.54 us
    ppermute x0 -> x8, waiting for transfers between devices: none -> 11.6 us  [the longest x6 8.98 us: two_level_swap(): lax.ppermute(jnp.concatenate([own[k], pair[k * rows:(k + 1) * rows]]), ax...]
    ppermute x0 -> x8, starting transfers between devices: none -> 10.5 us  [the longest x6 9.92 us: two_level_swap(): lax.ppermute(jnp.concatenate([own[k], pair[k * rows:(k + 1) * rows]]), ax...]
    ppermute x10 -> x3, starting transfers between devices: 13.3 us -> 3.55 us  [swap_blocks(): lax.ppermute(blocks[k], axis, [(i, i ^ k) for i in range(count)])]
    ppermute x10 -> x3, waiting for transfers between devices: 9.92 us -> 3.66 us  [swap_blocks(): lax.ppermute(blocks[k], axis, [(i, i ^ k) for i in range(count)])]
    all_to_all x1 -> x0, waiting for transfers between devices: 5.21 us -> none  [local(): lax.all_to_all(modes, 'det', split_axis=0, concat_axis=0, tiled=True)]
    concatenate x0 -> x6, other arithmetic: none -> 4.5 us  [two_level_swap(): jnp.concatenate([own[k], pair[k * rows:(k + 1) * rows]])]
    all_to_all x1 -> x0, starting transfers between devices: 3.36 us -> none  [local(): lax.all_to_all(modes, 'det', split_axis=0, concat_axis=0, tiled=True)]
    unnamed x12 -> x16, local copies, waits for them, and re-layouts: 3.24 us -> 0.98 us
  transfers between devices with their start and end apart: 11 -> 11, of which waited for: 7 -> 9; matrix products, arithmetic and copies ran while one was open for 1% -> 5% of each run, Pallas kernels for 0% -> 0%
where the time goes in v6:
time: 77.5 us; the launch traced here: 76.8 us
  Pallas kernels  35.4 us (46%)
  waiting for transfers between devices  15.2 us (20%)
  starting transfers between devices  14.1 us (18%)
  other arithmetic  5.89 us (8%)
  local copies, waits for them, and re-layouts  4.54 us (6%)
  between operations  1.42 us (2%)
    pallas_call x1, Pallas kernels, bin_and_modes(): pl.pallas_call(functools.partial(bin_kernel, sources=sources, windows=win...  14 us
    pallas_call x1, Pallas kernels, legendre_sums(): pl.pallas_call(functools.partial(legendre_kernel, chips=len(recv) - 1, ow...  12 us
    ppermute x6, starting transfers between devices, two_level_swap(): lax.ppermute(jnp.concatenate([own[k], pair[k * rows:(k + 1) * rows]]), ax...  9.92 us
    pallas_call x1, Pallas kernels, filter_and_sort(): pl.pallas_call(body, out_shape=(jax.ShapeDtypeStruct((lines, length), jnp...  9.37 us
    ppermute x6, waiting for transfers between devices, two_level_swap(): lax.ppermute(jnp.concatenate([own[k], pair[k * rows:(k + 1) * rows]]), ax...  8.98 us
    concatenate x6, other arithmetic, two_level_swap(): jnp.concatenate([own[k], pair[k * rows:(k + 1) * rows]])  4.5 us
    ppermute x3, waiting for transfers between devices, swap_blocks(): lax.ppermute(blocks[k], axis, [(i, i ^ k) for i in range(count)])  3.66 us
    ppermute x3, starting transfers between devices, swap_blocks(): lax.ppermute(blocks[k], axis, [(i, i ^ k) for i in range(count)])  3.55 us
  transfers between devices with their start and end apart: 11, of which 9 were waited for; matrix products, arithmetic and copies ran while one was open for 5% of the time, Pallas kernels for 0%

profile of v6, /device:TPU:0, one launch (start us, length us, event | category | flops | bytes accessed | tf_op | source)
XLA Modules:
  0.0 76.8 jit_solution(8452395659878072364)
XLA Ops:
  0.6 1.1 %reshape.143 = f32[8,128,32]{2,1,0:T(8,128)S(1)} reshape(f32[8,4096]{1,0:T(8,128)} %param.13) | data formatting | bytes 262144 | tf_op jit(solution)/shard_map/reshape | solution.py:261
  1.7 0.8 %copy.18 = f32[32,8,128]{2,1,0:T(8,128)} copy(f32[32,8,128]{0,2,1:T(8,128)S(1)} %bitcast.34) | data formatting | bytes 262144 | tf_op jit(solution)/shard_map/transpose | solution.py:261
  3.1 9.4 %filter_sort.1 = (f32[8,4096]{1,0:T(8,128)S(1)}, f32[40,256]{1,0:T(8,128)}, f32[40,256]{1,0:T(8,128)}, f32[40,256]{1,0:T(8,128)}, f32[40,256]{1,0:T(8,128)}, /*index=5*/f32[160,256]{1,0:T(8,128)}) custom-call(s32[2]{0:T(128)} %pad_add_fusion.me_ref, f32[8,4096]{1,0:T(8,128)} %scan_hbm.1, f32[256,128]{1,0:T(8,128)} %bitcast.35, s32[8,4096]{1,0:T(8,128)} %cycle_hbm.1, ...), custom_call_target="tpu_custom_call" | custom-call | tf_op jit(solution)/shard_map/filter_sort/pallas_call | solution.py:265
  13.2 1.1 %collective-permute-done.4.refs_1_ = f32[160,256]{1,0:T(8,128)S(1)} collective-permute-done((f32[160,256]{1,0:T(8,128)}, f32[160,256]{1,0:T(8,128)S(1)}, u32[]{:S(2)}, u32[]{:S(2)}) %collective-permute-start.4) | collective-permute-done | bytes 163872 | tf_op jit(solution)/shard_map/ppermute | solution.py:561
  14.3 0.8 %pad_maximum_fusion.4 = f32[80,256]{1,0:T(8,128)S(1)} fusion(f32[40,256]{1,0:T(8,128)S(1)} %get-tuple-element.85, f32[40,256]{1,0:T(8,128)} %get-tuple-element.51), kind=kLoop, calls=%fused_computation.44 | loop fusion | flops 20480 | bytes 163840 | tf_op jit(solution)/shard_map/concatenate | solution.py:565
  15.1 2.9 %collective-permute-start.5 = (f32[80,256]{1,0:T(8,128)S(1)}, f32[80,256]{1,0:T(8,128)S(1)}, u32[]{:S(2)}, u32[]{:S(2)}) collective-permute-start(f32[80,256]{1,0:T(8,128)S(1)} %pad_maximum_fusion.4), channel_id=1, source_target_pairs={{0,8},{4,12},{8,0},{12,4},{16,24},{20,28},{24,16},{28,20},{1,9},{5... | collective-permute-start | bytes 245768 | tf_op jit(solution)/shard_map/ppermute | solution.py:564
  18.1 0.8 %pad_maximum_fusion.5 = f32[80,256]{1,0:T(8,128)S(1)} fusion(f32[40,256]{1,0:T(8,128)S(1)} %get-tuple-element.84, f32[40,256]{1,0:T(8,128)} %get-tuple-element.52), kind=kLoop, calls=%fused_computation.45 | loop fusion | flops 20480 | bytes 163840 | tf_op jit(solution)/shard_map/concatenate | solution.py:565
  18.9 2.6 %collective-permute-start.6 = (f32[80,256]{1,0:T(8,128)S(1)}, f32[80,256]{1,0:T(8,128)S(1)}, u32[]{:S(2)}, u32[]{:S(2)}) collective-permute-start(f32[80,256]{1,0:T(8,128)S(1)} %pad_maximum_fusion.5), channel_id=1, source_target_pairs={{0,16},{4,20},{8,24},{12,28},{16,0},{20,4},{24,8},{28,12},{1,17},{... | collective-permute-start | bytes 245768 | tf_op jit(solution)/shard_map/ppermute | solution.py:564
  21.4 0.8 %pad_maximum_fusion.6 = f32[80,256]{1,0:T(8,128)S(1)} fusion(f32[40,256]{1,0:T(8,128)S(1)} %get-tuple-element.83, f32[40,256]{1,0:T(8,128)} %get-tuple-element.53), kind=kLoop, calls=%fused_computation.46 | loop fusion | flops 20480 | bytes 163840 | tf_op jit(solution)/shard_map/concatenate | solution.py:565
  23.0 3.3 %collective-permute-done.6.refs_3_ = f32[80,256]{1,0:T(8,128)S(1)} collective-permute-done((f32[80,256]{1,0:T(8,128)S(1)}, f32[80,256]{1,0:T(8,128)S(1)}, u32[]{:S(2)}, u32[]{:S(2)}) %collective-permute-start.6) | collective-permute-done | bytes 81952 | tf_op jit(solution)/shard_map/ppermute | solution.py:564
  26.3 2.2 %collective-permute-done.7.refs_4_ = f32[80,256]{1,0:T(8,128)S(1)} collective-permute-done((f32[80,256]{1,0:T(8,128)S(1)}, f32[80,256]{1,0:T(8,128)S(1)}, u32[]{:S(2)}, u32[]{:S(2)}) %collective-permute-start.7) | collective-permute-done | bytes 81952 | tf_op jit(solution)/shard_map/ppermute | solution.py:564
  29.2 14.0 %bin_modes.1 = (f32[32,2048]{1,0:T(8,128)}, f32[16,128]{1,0:T(8,128)S(1)}, f32[16,128]{1,0:T(8,128)}, f32[16,128]{1,0:T(8,128)}, f32[16,128]{1,0:T(8,128)}, /*index=5*/f32[64,128]{1,0:T(8,128)}, s32[1]{0:T(128)}) custom-call(s32[2]{0:T(128)} %pad_add_fusion.me_ref, f32[40,256]{1,0:T(8,128)} %get-tuple-element.49.refs_0_, f32[160,256]{1,0:T(8,128)} %copy-done.3, ...), custom_call_target="tpu_custom_call" | custom-call | tf_op jit(solution)/shard_map/bin_modes/pallas_call | solution.py:422
  43.3 1.5 %collective-permute-done.8 = f32[64,128]{1,0:T(8,128)} collective-permute-done((f32[64,128]{1,0:T(8,128)}, f32[64,128]{1,0:T(8,128)}, u32[]{:S(2)}, u32[]{:S(2)}) %collective-permute-start.8) | collective-permute-done | bytes 32800 | tf_op jit(solution)/shard_map/ppermute | solution.py:561
  44.8 0.7 fusion.29
  45.5 0.7 pad_maximum_fusion.7
  46.2 1.3 %collective-permute-start.9 = (f32[32,128]{1,0:T(8,128)S(1)}, f32[32,128]{1,0:T(8,128)}, u32[]{:S(2)}, u32[]{:S(2)}) collective-permute-start(f32[32,128]{1,0:T(8,128)S(1)} %pad_maximum_fusion.7), channel_id=1, source_target_pairs={{0,8},{4,12},{8,0},{12,4},{16,24},{20,28},{24,16},{28,20},{1,9},{5... | collective-permute-start | bytes 49160 | tf_op jit(solution)/shard_map/ppermute | solution.py:564
  47.5 0.7 pad_maximum_fusion.8
  48.2 1.7 %collective-permute-start.10 = (f32[32,128]{1,0:T(8,128)S(1)}, f32[32,128]{1,0:T(8,128)}, u32[]{:S(2)}, u32[]{:S(2)}) collective-permute-start(f32[32,128]{1,0:T(8,128)S(1)} %pad_maximum_fusion.8), channel_id=1, source_target_pairs={{0,16},{4,20},{8,24},{12,28},{16,0},{20,4},{24,8},{28,12},{1,17},{... | collective-permute-start | bytes 49160 | tf_op jit(solution)/shard_map/ppermute | solution.py:564
  50.6 1.4 %collective-permute-start.11 = (f32[32,128]{1,0:T(8,128)S(1)}, f32[32,128]{1,0:T(8,128)}, u32[]{:S(2)}, u32[]{:S(2)}) collective-permute-start(f32[32,128]{1,0:T(8,128)S(1)} %pad_maximum_fusion.9), channel_id=1, source_target_pairs={{0,24},{4,28},{8,16},{12,20},{16,8},{20,12},{24,0},{28,4},{1,25},{... | collective-permute-start | bytes 49160 | tf_op jit(solution)/shard_map/ppermute | solution.py:564
  52.9 3.3 %collective-permute-done.11 = f32[32,128]{1,0:T(8,128)} collective-permute-done((f32[32,128]{1,0:T(8,128)S(1)}, f32[32,128]{1,0:T(8,128)}, u32[]{:S(2)}, u32[]{:S(2)}) %collective-permute-start.11) | collective-permute-done | bytes 16416 | tf_op jit(solution)/shard_map/ppermute | solution.py:564
  56.9 12.0 %legendre_sums.1 = (f32[64,256]{1,0:T(8,128)S(1)}, f32[64,256]{1,0:T(8,128)S(1)}, f32[64,256]{1,0:T(8,128)S(1)}, f32[64,256]{1,0:T(8,128)S(1)}) custom-call(s32[2]{0:T(128)S(1)} %copy-done, f32[16,128]{1,0:T(8,128)S(1)} %get-tuple-element.62.refs_0_, f32[64,128]{1,0:T(8,128)} %get-tuple-element.63.refs_1_, f32[32,128]{1,0:T(8,128)} %get-tuple-element.64.refs_2_, ...), custom_call_target="tpu_custom_call" | custom-call | tf_op jit(solution)/shard_map/legendre_sums/pallas_call | solution.py:514
  68.8 2.5 %collective-permute-start.14 = (f32[64,256]{1,0:T(8,128)S(1)}, f32[64,256]{1,0:T(8,128)S(1)}, u32[]{:S(2)}, u32[]{:S(2)}) collective-permute-start(f32[64,256]{1,0:T(8,128)S(1)} %get-tuple-element.70), channel_id=1, source_target_pairs={{0,3},{1,2},{2,1},{3,0},{4,7},{5,6},{6,5},{7,4},{8,11},{9,10},{10,... | collective-permute-start | bytes 196616 | tf_op jit(solution)/shard_map/ppermute | solution.py:575
  72.5 2.2 %collective-permute-done.14 = f32[64,256]{1,0:T(8,128)S(1)} collective-permute-done((f32[64,256]{1,0:T(8,128)S(1)}, f32[64,256]{1,0:T(8,128)S(1)}, u32[]{:S(2)}, u32[]{:S(2)}) %collective-permute-start.14) | collective-permute-done | bytes 65568 | tf_op jit(solution)/shard_map/ppermute | solution.py:575
  74.7 0.9 %collective-permute-done.13 = f32[64,256]{1,0:T(8,128)S(1)} collective-permute-done((f32[64,256]{1,0:T(8,128)S(1)}, f32[64,256]{1,0:T(8,128)S(1)}, u32[]{:S(2)}, u32[]{:S(2)}) %collective-permute-start.13) | collective-permute-done | bytes 65568 | tf_op jit(solution)/shard_map/ppermute | solution.py:575
  (41 shorter events, 6.6 us)
Async XLA Ops:
  0.6 12.4 %copy-start.7 = (s32[256]{0:T(256)S(1)}, s32[256]{0:T(256)}, u32[]{:S(2)}) copy-start(s32[256]{0:T(256)} %param.16) | copy-start | bytes 3076
  3.1 53.1 %copy-start.1 = (s32[8,4096]{1,0:T(8,128)S(1)}, s32[8,4096]{1,0:T(8,128)}, u32[]{:S(2)}) copy-start(s32[8,4096]{1,0:T(8,128)} %cycle_hbm.1) | copy-start | bytes 393220
  3.1 53.1 %copy-start.2 = (s32[8,4096]{1,0:T(8,128)S(1)}, s32[8,4096]{1,0:T(8,128)}, u32[]{:S(2)}) copy-start(s32[8,4096]{1,0:T(8,128)} %column_hbm.1) | copy-start | bytes 393220
  12.5 1.8 %collective-permute-start.4 = (f32[160,256]{1,0:T(8,128)}, f32[160,256]{1,0:T(8,128)S(1)}, u32[]{:S(2)}, u32[]{:S(2)}) collective-permute-start(f32[160,256]{1,0:T(8,128)} %get-tuple-element.50), channel_id=1, source_target_pairs={{0,4},{4,0},{8,12},{12,8},{16,20},{20,16},{24,28},{28,24},{1,5},{5... | collective-permute-start | bytes 491528 | tf_op jit(solution)/shard_map/ppermute | solution.py:561
  14.3 14.2 %copy-start.3 = (f32[160,256]{1,0:T(8,128)}, f32[160,256]{1,0:T(8,128)S(1)}, u32[]{:S(2)}) copy-start(f32[160,256]{1,0:T(8,128)S(1)} %collective-permute-done.4.refs_1_) | copy-start | bytes 491524
  15.1 7.9 %collective-permute-start.5 = (f32[80,256]{1,0:T(8,128)S(1)}, f32[80,256]{1,0:T(8,128)S(1)}, u32[]{:S(2)}, u32[]{:S(2)}) collective-permute-start(f32[80,256]{1,0:T(8,128)S(1)} %pad_maximum_fusion.4), channel_id=1, source_target_pairs={{0,8},{4,12},{8,0},{12,4},{16,24},{20,28},{24,16},{28,20},{1,9},{5... | collective-permute-start | bytes 245768 | tf_op jit(solution)/shard_map/ppermute | solution.py:564
  18.9 7.4 %collective-permute-start.6 = (f32[80,256]{1,0:T(8,128)S(1)}, f32[80,256]{1,0:T(8,128)S(1)}, u32[]{:S(2)}, u32[]{:S(2)}) collective-permute-start(f32[80,256]{1,0:T(8,128)S(1)} %pad_maximum_fusion.5), channel_id=1, source_target_pairs={{0,16},{4,20},{8,24},{12,28},{16,0},{20,4},{24,8},{28,12},{1,17},{... | collective-permute-start | bytes 245768 | tf_op jit(solution)/shard_map/ppermute | solution.py:564
  22.2 6.3 %collective-permute-start.7 = (f32[80,256]{1,0:T(8,128)S(1)}, f32[80,256]{1,0:T(8,128)S(1)}, u32[]{:S(2)}, u32[]{:S(2)}) collective-permute-start(f32[80,256]{1,0:T(8,128)S(1)} %pad_maximum_fusion.6), channel_id=1, source_target_pairs={{0,24},{4,28},{8,16},{12,20},{16,8},{20,12},{24,0},{28,4},{1,25},{... | collective-permute-start | bytes 245768 | tf_op jit(solution)/shard_map/ppermute | solution.py:564
  23.0 5.5 %copy-start.4 = (f32[80,256]{1,0:T(8,128)}, f32[80,256]{1,0:T(8,128)S(1)}, u32[]{:S(2)}) copy-start(f32[80,256]{1,0:T(8,128)S(1)} %collective-permute-done.5.refs_2_) | copy-start | bytes 245764
  26.3 2.2 %copy-start.5 = (f32[80,256]{1,0:T(8,128)}, f32[80,256]{1,0:T(8,128)S(1)}, u32[]{:S(2)}) copy-start(f32[80,256]{1,0:T(8,128)S(1)} %collective-permute-done.6.refs_3_) | copy-start | bytes 245764
  28.5 0.6 copy-start.6
  43.2 1.6 %collective-permute-start.8 = (f32[64,128]{1,0:T(8,128)}, f32[64,128]{1,0:T(8,128)}, u32[]{:S(2)}, u32[]{:S(2)}) collective-permute-start(f32[64,128]{1,0:T(8,128)} %get-tuple-element.57), channel_id=1, source_target_pairs={{0,4},{4,0},{8,12},{12,8},{16,20},{20,16},{24,28},{28,24},{1,5},{5... | collective-permute-start | bytes 98312 | tf_op jit(solution)/shard_map/ppermute | solution.py:561
  46.2 6.5 %collective-permute-start.9 = (f32[32,128]{1,0:T(8,128)S(1)}, f32[32,128]{1,0:T(8,128)}, u32[]{:S(2)}, u32[]{:S(2)}) collective-permute-start(f32[32,128]{1,0:T(8,128)S(1)} %pad_maximum_fusion.7), channel_id=1, source_target_pairs={{0,8},{4,12},{8,0},{12,4},{16,24},{20,28},{24,16},{28,20},{1,9},{5... | collective-permute-start | bytes 49160 | tf_op jit(solution)/shard_map/ppermute | solution.py:564
  48.2 4.7 %collective-permute-start.10 = (f32[32,128]{1,0:T(8,128)S(1)}, f32[32,128]{1,0:T(8,128)}, u32[]{:S(2)}, u32[]{:S(2)}) collective-permute-start(f32[32,128]{1,0:T(8,128)S(1)} %pad_maximum_fusion.8), channel_id=1, source_target_pairs={{0,16},{4,20},{8,24},{12,28},{16,0},{20,4},{24,8},{28,12},{1,17},{... | collective-permute-start | bytes 49160 | tf_op jit(solution)/shard_map/ppermute | solution.py:564
  50.6 5.6 %collective-permute-start.11 = (f32[32,128]{1,0:T(8,128)S(1)}, f32[32,128]{1,0:T(8,128)}, u32[]{:S(2)}, u32[]{:S(2)}) collective-permute-start(f32[32,128]{1,0:T(8,128)S(1)} %pad_maximum_fusion.9), channel_id=1, source_target_pairs={{0,24},{4,28},{8,16},{12,20},{16,8},{20,12},{24,0},{28,4},{1,25},{... | collective-permute-start | bytes 49160 | tf_op jit(solution)/shard_map/ppermute | solution.py:564
  56.2 0.6 copy-start
  68.8 5.9 %collective-permute-start.14 = (f32[64,256]{1,0:T(8,128)S(1)}, f32[64,256]{1,0:T(8,128)S(1)}, u32[]{:S(2)}, u32[]{:S(2)}) collective-permute-start(f32[64,256]{1,0:T(8,128)S(1)} %get-tuple-element.70), channel_id=1, source_target_pairs={{0,3},{1,2},{2,1},{3,0},{4,7},{5,6},{6,5},{7,4},{8,11},{9,10},{10,... | collective-permute-start | bytes 196616 | tf_op jit(solution)/shard_map/ppermute | solution.py:575
  71.4 4.3 %collective-permute-start.13 = (f32[64,256]{1,0:T(8,128)S(1)}, f32[64,256]{1,0:T(8,128)S(1)}, u32[]{:S(2)}, u32[]{:S(2)}) collective-permute-start(f32[64,256]{1,0:T(8,128)S(1)} %get-tuple-element.69), channel_id=1, source_target_pairs={{0,2},{1,3},{2,0},{3,1},{4,6},{5,7},{6,4},{7,5},{8,10},{9,11},{10,... | collective-permute-start | bytes 196616 | tf_op jit(solution)/shard_map/ppermute | solution.py:575
  71.9 4.3 %collective-permute-start.12 = (f32[64,256]{1,0:T(8,128)S(1)}, f32[64,256]{1,0:T(8,128)S(1)}, u32[]{:S(2)}, u32[]{:S(2)}) collective-permute-start(f32[64,256]{1,0:T(8,128)S(1)} %get-tuple-element.68), channel_id=1, source_target_pairs={{0,1},{1,0},{2,3},{3,2},{4,5},{5,4},{6,7},{7,6},{8,9},{9,8},{10,11... | collective-permute-start | bytes 196616 | tf_op jit(solution)/shard_map/ppermute | solution.py:575

commit v7 on v5

--- a/solution.py
+++ b/solution.py
@@ -27,6 +27,8 @@
     a = np.arange(LANES)
     angle = 2.0 * np.pi * (np.outer(a, a) % LANES) / LANES
     c, s = np.cos(angle), np.sin(angle)
+    order = (a % outer) * (LANES // outer) + a // outer
+    c, s = c[:, order], s[:, order]
     forward = np.block([[c, -s], [s, c]])
     return twiddle.astype(np.float32), forward.astype(np.float32)
 
@@ -42,7 +44,7 @@
     table = np.stack(out).astype(np.float32)
     high = table.astype(jnp.bfloat16)
     low = (table - high.astype(np.float32)).astype(jnp.bfloat16)
-    return high, low
+    return np.stack([high, low])
 
 
 def small_fft(re, im, sign):
@@ -186,7 +188,15 @@
     for load in loads[2:]:
         load.wait()
     spec = jnp.dot(spec_ref[...], forward_ref[...], precision=precise, preferred_element_type=jnp.float32)
-    resp = resp_ref[...] * (1.0 / length)
+    resp = [resp_ref[:, n * LANES:(n + 1) * LANES] * (1.0 / length) for n in range(outer)]
+    step = 1
+    while step < outer:
+        upper = (lax.broadcasted_iota(jnp.int32, (lines, LANES), 1) & step) != 0
+        for n in range(outer):
+            if not n & step:
+                resp[n], resp[n + step] = trade(resp[n], resp[n + step], upper, 1, step)
+        step *= 2
+    resp = jnp.concatenate(resp, axis=0)
     spec = spec * jnp.concatenate([resp, resp], axis=1)
     spec_ref[...] = lax.dot_general(
         spec, forward_ref[...], NT, precision=precise, preferred_element_type=jnp.float32
@@ -253,8 +263,7 @@
     rows = LANES // buckets + 2
     reach = (rows + 2 * SUB - 2) // SUB * SUB
     twiddle, forward = filter_tables(length)
-    resp_rows = resp.reshape(lines, LANES, tiles).transpose(2, 0, 1).reshape(tiles * lines, LANES)
-    operands = [scan, resp_rows, cycle, column, jnp.asarray(twiddle), jnp.asarray(forward)]
+    operands = [scan, resp, cycle, column, jnp.asarray(twiddle), jnp.asarray(forward)]
     body = functools.partial(sort_kernel, buckets=buckets, span=span, rows=rows, windows=windows)
     vmem = pl.BlockSpec(memory_space=pltpu.VMEM)
     return pl.pallas_call(
@@ -263,7 +272,7 @@
             jax.ShapeDtypeStruct((lines, length), jnp.float32),
         ) + (jax.ShapeDtypeStruct((2 * windows * rows, row_len), jnp.float32),) * det_count,
         in_specs=[pl.BlockSpec(memory_space=pltpu.SMEM)]
-        + [pl.BlockSpec(memory_space=pltpu.HBM)] * len(operands),
+        + [pl.BlockSpec(memory_space=pl.ANY)] * len(operands),
         out_specs=(vmem,) * (1 + det_count),
         scratch_shapes=[pltpu.VMEM(x.shape, x.dtype) for x in operands] + [
             pltpu.SemaphoreType.DMA((len(operands),)),
@@ -287,16 +296,24 @@
 def bin_kernel(
     *refs, sources, windows, rows, window_cycles
 ):
-    recv_refs, (pick_ref, table_hi, table_lo, map_ref, send_ref, flag_ref) = refs[:sources], refs[sources:-6]
-    recv_ref, left_a, left_b, right_a, right_b, acc_ref = refs[-6:]
+    recv_refs, (pick_ref, table_hbm, map_ref, send_ref, flag_ref) = refs[:sources], refs[sources:-9]
+    recv_ref, column_ref, left_a, left_b, right_a, right_b, acc_ref, table_ref, arrived = refs[-9:]
+    load = pltpu.make_async_copy(table_hbm, table_ref, arrived)
+    load.start()
+    wide_rows = column_ref.shape[2]
     for e in range(sources):
-        recv_ref[e] = recv_refs[e][...]
+        block = recv_refs[e][...]
+        recv_ref[e] = block
+        column_ref[e] = (block[:wide_rows].astype(jnp.int32) & (ROW - 1)).astype(jnp.float32).T
     left_refs, right_refs = (left_a, left_b), (right_a, right_b)
     row_len = recv_ref.shape[2]
     parts = NPHI // ROW
     area = parts * window_cycles
     a_iota = lax.broadcasted_iota(jnp.int32, (area, row_len), 0).astype(jnp.float32).astype(jnp.bfloat16)
-    b_iota = lax.broadcasted_iota(jnp.int32, (ROW, row_len), 0).astype(jnp.float32).astype(jnp.bfloat16)
+    b_iota = [
+        (lax.broadcasted_iota(jnp.int32, (row_len, LANES), 1) + first).astype(jnp.float32).astype(jnp.bfloat16)
+        for first in range(0, ROW, LANES)
+    ]
     zero, one = jnp.zeros((), jnp.bfloat16), jnp.ones((), jnp.bfloat16)
 
     def build(e, w, slot):
@@ -309,18 +326,18 @@
             inside = (q >= 0) & (cycle < window_cycles)
             a = jnp.where(inside, ((q >> 8) & (parts - 1)) * window_cycles + cycle, -1)
             a = a.astype(jnp.float32).astype(jnp.bfloat16)
-            b = (q & (ROW - 1)).astype(jnp.float32).astype(jnp.bfloat16)
+            at = w * rows + r
+            b = jnp.broadcast_to(column_ref[e, :, at:at + 1], (row_len, LANES)).astype(jnp.bfloat16)
             cols = slice(r * row_len, (r + 1) * row_len)
             hit = a_iota == a
             left[:area, cols] = jnp.where(hit, high, zero)
             left[area:2 * area, cols] = jnp.where(hit, low, zero)
             left[2 * area:, cols] = jnp.where(hit, one, zero)
-            right[:, cols] = jnp.where(b_iota == b, one, zero)
+            for i, iota in enumerate(b_iota):
+                right[cols, i * LANES:(i + 1) * LANES] = jnp.where(iota == b, one, zero)
 
     def multiply(slot):
-        acc_ref[...] += lax.dot_general(
-            left_refs[slot][...], right_refs[slot][...], NT, preferred_element_type=jnp.float32
-        )
+        acc_ref[...] += jnp.dot(left_refs[slot][...], right_refs[slot][...], preferred_element_type=jnp.float32)
 
     build(0, 0, 0)
     for w in range(windows):
@@ -345,14 +362,15 @@
             map_ref[w * window_cycles:(w + 1) * window_cycles, c8 * ROW:(c8 + 1) * ROW] = (
                 sky[c8 * window_cycles:(c8 + 1) * window_cycles]
             )
+    load.wait()
     cycles = map_ref.shape[0]
     half = NPHI // 2
     modes = []
     for parity in (0, 1):
         a, b = map_ref[:, :half], map_ref[:, half:]
         high, low = split2(a + b if parity == 0 else a - b)
-        first = jnp.dot(jnp.concatenate([high, low], axis=0), table_hi[parity], preferred_element_type=jnp.float32)
-        second = jnp.dot(high, table_lo[parity], preferred_element_type=jnp.float32)
+        first = jnp.dot(jnp.concatenate([high, low], axis=0), table_ref[0, parity], preferred_element_type=jnp.float32)
+        second = jnp.dot(high, table_ref[1, parity], preferred_element_type=jnp.float32)
         modes.append(first[:cycles] + first[cycles:] + second)
     modes = jnp.concatenate(modes, axis=1)
     count = modes.shape[1]
@@ -388,7 +406,7 @@
     count = order_slot.shape[0]
     slots = count // sources
     groups = LANES // (2 * slots)
-    high, low = mode_tables(count)
+    tables = jnp.asarray(mode_tables(count))
     m = order_slot.reshape(sources, 1, 1, slots)
     part = jnp.arange(2, dtype=jnp.int32).reshape(1, 1, 2, 1)
     pick = (m & 1) * count + part * (count // 2) + (m >> 1)
@@ -403,19 +421,22 @@
             jax.ShapeDtypeStruct((sources, cycles // groups, LANES), jnp.float32),
             jax.ShapeDtypeStruct((1,), jnp.int32),
         ),
-        in_specs=[vmem] * (sources + 3),
+        in_specs=[vmem] * (sources + 1) + [pl.BlockSpec(memory_space=pl.ANY)],
         out_specs=(vmem, vmem, pl.BlockSpec(memory_space=pltpu.SMEM)),
         scratch_shapes=[
             pltpu.VMEM((sources, lines, row_len), jnp.float32),
+            pltpu.VMEM((sources, row_len, -(-windows * rows // SUB) * SUB), jnp.float32),
             pltpu.VMEM((3 * area, depth), jnp.bfloat16),
             pltpu.VMEM((3 * area, depth), jnp.bfloat16),
-            pltpu.VMEM((ROW, depth), jnp.bfloat16),
-            pltpu.VMEM((ROW, depth), jnp.bfloat16),
+            pltpu.VMEM((depth, ROW), jnp.bfloat16),
+            pltpu.VMEM((depth, ROW), jnp.bfloat16),
             pltpu.VMEM((3 * area, ROW), jnp.float32),
+            pltpu.VMEM(tables.shape, jnp.bfloat16),
+            pltpu.SemaphoreType.DMA,
         ],
-        compiler_params=pltpu.CompilerParams(vmem_limit_bytes=40 * 1024 * 1024),
+        compiler_params=pltpu.CompilerParams(vmem_limit_bytes=48 * 1024 * 1024),
         name="bin_modes",
-    )(*recv, pick, jnp.asarray(high), jnp.asarray(low))
+    )(*recv, pick, tables)
 
 
 def legendre_kernel(me_ref, recv_ref, table_ref, *refs, owners):
@@ -521,9 +542,10 @@
 
 def swap_blocks(blocks, axis):
     count = len(blocks)
-    return [blocks[0]] + [
-        lax.ppermute(blocks[k], axis, [(i, i ^ k) for i in range(count)]) for k in range(1, count)
-    ]
+    out = list(blocks)
+    for k in range(count - 1, 0, -1):
+        out[k] = lax.ppermute(blocks[k], axis, [(i, i ^ k) for i in range(count)])
+    return out
 
 
 def local(scan_lines, response, cycle_offset, column, order_slot, legendre, *, det_count, band_count):

time: 71.6 us -> 71 us (level)
  local copies, waits for them, and re-layouts: 5.48 us -> 2.72 us
  Pallas kernels: 31.9 us -> 33.5 us
    pallas_call x1, Pallas kernels: 12.2 us -> 13.5 us  [bin_and_modes(): pl.pallas_call(functools.partial(bin_kernel, sources=sources, windows=win...]
    reshape x1 -> x0, local copies, waits for them, and re-layouts: 1.07 us -> none  [filter_and_sort(): resp.reshape(lines, LANES, tiles).transpose(2, 0, 1)]
    unnamed x12 -> x10, local copies, waits for them, and re-layouts: 3.24 us -> 2.38 us
    transpose x1 -> x0, local copies, waits for them, and re-layouts: 0.83 us -> none  [filter_and_sort(): resp.reshape(lines, LANES, tiles).transpose(2, 0, 1)]
  transfers between devices with their start and end apart: 11 -> 11, of which waited for: 7 -> 7; matrix products, arithmetic and copies ran while one was open for 1% -> 2% of each run, Pallas kernels for 0% -> 0%
where the time goes in v7:
time: 71 us; the launch traced here: 70.7 us
  Pallas kernels  33.5 us (47%)
  starting transfers between devices  16.6 us (23%)
  waiting for transfers between devices  15 us (21%)
  local copies, waits for them, and re-layouts  2.72 us (4%)
  other arithmetic  1.49 us (2%)
  between operations  1.37 us (2%)
    pallas_call x1, Pallas kernels, bin_and_modes(): pl.pallas_call(functools.partial(bin_kernel, sources=sources, windows=win...  13.5 us
    ppermute x10, starting transfers between devices, swap_blocks(): out[k] = lax.ppermute(blocks[k], axis, [(i, i ^ k) for i in range(count)])  13.3 us
    pallas_call x1, Pallas kernels, legendre_sums(): pl.pallas_call(functools.partial(legendre_kernel, owners=owners), out_sha...  11.2 us
    ppermute x10, waiting for transfers between devices, swap_blocks(): out[k] = lax.ppermute(blocks[k], axis, [(i, i ^ k) for i in range(count)])  9.92 us
    pallas_call x1, Pallas kernels, filter_and_sort(): pl.pallas_call(body, out_shape=(jax.ShapeDtypeStruct((lines, length), jnp...  8.75 us
    all_to_all x1, waiting for transfers between devices, local(): lax.all_to_all(modes, 'det', split_axis=0, concat_axis=0, tiled=True)  5.11 us
    all_to_all x1, starting transfers between devices, local(): lax.all_to_all(modes, 'det', split_axis=0, concat_axis=0, tiled=True)  3.36 us
    unnamed x10, local copies, waits for them, and re-layouts  2.38 us
  transfers between devices with their start and end apart: 11, of which 7 were waited for; matrix products, arithmetic and copies ran while one was open for 2% of the time, Pallas kernels for 0%

profile of v7, /device:TPU:0, one launch (start us, length us, event | category | flops | bytes accessed | tf_op | source)
XLA Modules:
  0.0 70.7 jit_solution(15200102119120598940)
XLA Ops:
  0.7 8.8 %filter_sort.1 = (f32[8,4096]{1,0:T(8,128)S(1)}, f32[40,256]{1,0:T(8,128)}, f32[40,256]{1,0:T(8,128)}, f32[40,256]{1,0:T(8,128)}, f32[40,256]{1,0:T(8,128)}, /*i...) custom-call(s32[1]{0:T(128)} %bitcast.3.me_ref, f32[8,4096]{1,0:T(8,128)} %scan_hbm.1, ...), custom_call_target="tpu_custom_call" | custom-call | tf_op jit(solution)/shard_map/filter_sort/pallas_call | solution.py:269
  9.4 0.5 collective-permute-start
  9.9 2.6 %collective-permute-start.1 = (f32[40,256]{1,0:T(8,128)}, f32[40,256]{1,0:T(8,128)S(1)}, u32[]{:S(2)}, u32[]{:S(2)}) collective-permute-start(f32[40,256]{1,0:T(8,128)} %get-tuple-element.38), channel_id=1, source_target_pairs={{0,8},{4,12},{8,0},{12,4},{16,24},{20,28},{24,16},{28,20},{1,9},{5... | collective-permute-start | bytes 122888 | tf_op jit(solution)/shard_map/ppermute | solution.py:547
  12.7 2.8 %collective-permute-start.3 = (f32[40,256]{1,0:T(8,128)}, f32[40,256]{1,0:T(8,128)S(1)}, u32[]{:S(2)}, u32[]{:S(2)}) collective-permute-start(f32[40,256]{1,0:T(8,128)} %get-tuple-element.40), channel_id=1, source_target_pairs={{0,16},{4,20},{8,24},{12,28},{16,0},{20,4},{24,8},{28,12},{1,17},{... | collective-permute-start | bytes 122888 | tf_op jit(solution)/shard_map/ppermute | solution.py:547
  15.4 0.7 and_multiply_fusion
  16.3 3.6 %collective-permute-start.5 = (f32[40,256]{1,0:T(8,128)}, f32[40,256]{1,0:T(8,128)S(1)}, u32[]{:S(2)}, u32[]{:S(2)}) collective-permute-start(f32[40,256]{1,0:T(8,128)} %get-tuple-element.42), channel_id=1, source_target_pairs={{0,24},{4,28},{8,16},{12,20},{16,8},{20,12},{24,0},{28,4},{1,25},{... | collective-permute-start | bytes 122888 | tf_op jit(solution)/shard_map/ppermute | solution.py:547
  19.9 0.1 collective-permute-start.6
  20.1 0.1 reshape.145.refs_8_
  20.2 0.1 collective-permute-done.4.refs_5_
  20.3 2.1 %collective-permute-done.5.refs_6_ = f32[40,256]{1,0:T(8,128)S(1)} collective-permute-done((f32[40,256]{1,0:T(8,128)}, f32[40,256]{1,0:T(8,128)S(1)}, u32[]{:S(2)}, u32[]{:S(2)}) %collective-permute-start.5) | collective-permute-done | bytes 40992 | tf_op jit(solution)/shard_map/ppermute | solution.py:547
  22.4 3.1 %collective-permute-done.6.refs_7_ = f32[40,256]{1,0:T(8,128)S(1)} collective-permute-done((f32[40,256]{1,0:T(8,128)}, f32[40,256]{1,0:T(8,128)S(1)}, u32[]{:S(2)}, u32[]{:S(2)}) %collective-permute-start.6) | collective-permute-done | bytes 40992 | tf_op jit(solution)/shard_map/ppermute | solution.py:547
  25.5 1.6 %copy-done = bf16[2,2,1024,256]{3,2,1,0:T(8,128)(2,1)S(1)} copy-done((bf16[2,2,1024,256]{3,2,1,0:T(8,128)(2,1)S(1)}, bf16[2,2,1024,256]{3,2,1,0:T(8,128)(2,1)}, u32[]{:S(2)}) %copy-start) | copy-done | bytes 2097176
  27.1 0.8 %copy-done.1 = f32[40,256]{1,0:T(8,128)S(1)} copy-done((f32[40,256]{1,0:T(8,128)S(1)}, f32[40,256]{1,0:T(8,128)}, u32[]{:S(2)}) %copy-start.1) | copy-done | bytes 40984
  27.8 13.5 %bin_modes.1 = (f32[32,2048]{1,0:T(8,128)}, f32[8,16,128]{2,1,0:T(8,128)}, s32[1]{0:T(128)}) custom-call(f32[40,256]{1,0:T(8,128)S(1)} %copy-done.1, f32[40,256]{1,0:T(8,128)S(1)} %collective-permute-done.refs_1_, f32[40,256]{1,0:T(8,128)S(1)} %collective-permute-done.1.refs_2_, f32[40,256]{1,0:T(8,128)S(1)} %collective-permute-done.2.refs_3_, ...), custom_call_target="tpu_custom_call" | custom-call | tf_op jit(solution)/shard_map/bin_modes/pallas_call | solution.py:417
  41.4 3.4 %all-to-all-start.3 = ((f32[8,16,128]{2,1,0:T(8,128)}), f32[8,16,128]{2,1,0:T(8,128)S(1)}, u32[]{:S(2)}, u32[]{:S(2)}) async-start(f32[8,16,128]{2,1,0:T(8,128)} %get-tuple-element.46), calls=%async_computation.3 | async-start | bytes 131072 | tf_op jit(solution)/shard_map/all_to_all | solution.py:559
  45.5 5.1 %all-to-all-done.3 = f32[8,16,128]{2,1,0:T(8,128)S(1)} async-done(((f32[8,16,128]{2,1,0:T(8,128)}), f32[8,16,128]{2,1,0:T(8,128)S(1)}, u32[]{:S(2)}, u32[]{:S(2)}) %all-to-all-start.3) | async-done | bytes 65568 | tf_op jit(solution)/shard_map/all_to_all | solution.py:559
  50.6 11.2 %legendre_sums.1 = (f32[64,256]{1,0:T(8,128)S(1)}, f32[64,256]{1,0:T(8,128)S(1)}, f32[64,256]{1,0:T(8,128)S(1)}, f32[64,256]{1,0:T(8,128)S(1)}) custom-call(s32[1]{0:T(128)} %bitcast.2.me_ref, f32[8,16,128]{2,1,0:T(8,128)S(1)} %get-tuple-element.48.recv_ref, f32[32,256,1024]{2,1,0:T(8,128)} %table_ref.1), custom_call_target="tpu_custom_call" | custom-call | tf_op jit(solution)/shard_map/legendre_sums/pallas_call | solution.py:500
  61.8 1.6 %collective-permute-start.7 = (f32[64,256]{1,0:T(8,128)S(1)}, f32[64,256]{1,0:T(8,128)S(1)}, u32[]{:S(2)}, u32[]{:S(2)}) collective-permute-start(f32[64,256]{1,0:T(8,128)S(1)} %get-tuple-element.50), channel_id=1, source_target_pairs={{0,1},{1,0},{2,3},{3,2},{4,5},{5,4},{6,7},{7,6},{8,9},{9,8},{10,11... | collective-permute-start | bytes 196616 | tf_op jit(solution)/shard_map/ppermute | solution.py:547
  63.4 1.5 %collective-permute-start.8 = (f32[64,256]{1,0:T(8,128)S(1)}, f32[64,256]{1,0:T(8,128)S(1)}, u32[]{:S(2)}, u32[]{:S(2)}) collective-permute-start(f32[64,256]{1,0:T(8,128)S(1)} %get-tuple-element.51), channel_id=1, source_target_pairs={{0,2},{1,3},{2,0},{3,1},{4,6},{5,7},{6,4},{7,5},{8,10},{9,11},{10,... | collective-permute-start | bytes 196616 | tf_op jit(solution)/shard_map/ppermute | solution.py:547
  64.9 0.5 collective-permute-start.9
  65.4 0.7 collective-permute-done.7
  66.1 2.2 %collective-permute-done.8 = f32[64,256]{1,0:T(8,128)S(1)} collective-permute-done((f32[64,256]{1,0:T(8,128)S(1)}, f32[64,256]{1,0:T(8,128)S(1)}, u32[]{:S(2)}, u32[]{:S(2)}) %collective-permute-start.8) | collective-permute-done | bytes 65568 | tf_op jit(solution)/shard_map/ppermute | solution.py:547
  68.3 1.7 %collective-permute-done.9 = f32[64,256]{1,0:T(8,128)S(1)} collective-permute-done((f32[64,256]{1,0:T(8,128)S(1)}, f32[64,256]{1,0:T(8,128)S(1)}, u32[]{:S(2)}, u32[]{:S(2)}) %collective-permute-start.9) | collective-permute-done | bytes 65568 | tf_op jit(solution)/shard_map/ppermute | solution.py:547
  70.1 0.6 broadcast_select_fusion
  (24 shorter events, 0.5 us)
Async XLA Ops:
  0.6 50.0 %copy-start.2 = (s32[8,4096]{1,0:T(8,128)S(1)}, s32[8,4096]{1,0:T(8,128)}, u32[]{:S(2)}) copy-start(s32[8,4096]{1,0:T(8,128)} %cycle_hbm.1) | copy-start | bytes 393220
  0.6 50.0 %copy-start.3 = (s32[8,4096]{1,0:T(8,128)S(1)}, s32[8,4096]{1,0:T(8,128)}, u32[]{:S(2)}) copy-start(s32[8,4096]{1,0:T(8,128)} %column_hbm.1) | copy-start | bytes 393220
  0.7 44.1 %copy-start.4 = (s32[256]{0:T(256)S(1)}, s32[256]{0:T(256)}, u32[]{:S(2)}) copy-start(s32[256]{0:T(256)} %param.15) | copy-start | bytes 3076
  9.4 6.8 %collective-permute-start = (f32[40,256]{1,0:T(8,128)}, f32[40,256]{1,0:T(8,128)S(1)}, u32[]{:S(2)}, u32[]{:S(2)}) collective-permute-start(f32[40,256]{1,0:T(8,128)} %get-tuple-element.37), channel_id=1, source_target_pairs={{0,4},{4,0},{8,12},{12,8},{16,20},{20,16},{24,28},{28,24},{1,5},{5... | collective-permute-start | bytes 122888 | tf_op jit(solution)/shard_map/ppermute | solution.py:547
  9.9 9.9 %collective-permute-start.1 = (f32[40,256]{1,0:T(8,128)}, f32[40,256]{1,0:T(8,128)S(1)}, u32[]{:S(2)}, u32[]{:S(2)}) collective-permute-start(f32[40,256]{1,0:T(8,128)} %get-tuple-element.38), channel_id=1, source_target_pairs={{0,8},{4,12},{8,0},{12,4},{16,24},{20,28},{24,16},{28,20},{1,9},{5... | collective-permute-start | bytes 122888 | tf_op jit(solution)/shard_map/ppermute | solution.py:547
  12.6 7.6 %collective-permute-start.2 = (f32[40,256]{1,0:T(8,128)}, f32[40,256]{1,0:T(8,128)S(1)}, u32[]{:S(2)}, u32[]{:S(2)}) collective-permute-start(f32[40,256]{1,0:T(8,128)} %get-tuple-element.39), channel_id=1, source_target_pairs={{0,12},{4,8},{8,4},{12,0},{16,28},{20,24},{24,20},{28,16},{1,13},{... | collective-permute-start | bytes 122888 | tf_op jit(solution)/shard_map/ppermute | solution.py:547
  12.7 7.5 %collective-permute-start.3 = (f32[40,256]{1,0:T(8,128)}, f32[40,256]{1,0:T(8,128)S(1)}, u32[]{:S(2)}, u32[]{:S(2)}) collective-permute-start(f32[40,256]{1,0:T(8,128)} %get-tuple-element.40), channel_id=1, source_target_pairs={{0,16},{4,20},{8,24},{12,28},{16,0},{20,4},{24,8},{28,12},{1,17},{... | collective-permute-start | bytes 122888 | tf_op jit(solution)/shard_map/ppermute | solution.py:547
  15.4 4.9 %collective-permute-start.4 = (f32[40,256]{1,0:T(8,128)}, f32[40,256]{1,0:T(8,128)S(1)}, u32[]{:S(2)}, u32[]{:S(2)}) collective-permute-start(f32[40,256]{1,0:T(8,128)} %get-tuple-element.41), channel_id=1, source_target_pairs={{0,20},{4,16},{8,28},{12,24},{16,4},{20,0},{24,12},{28,8},{1,21},{... | collective-permute-start | bytes 122888 | tf_op jit(solution)/shard_map/ppermute | solution.py:547
  16.3 6.1 %collective-permute-start.5 = (f32[40,256]{1,0:T(8,128)}, f32[40,256]{1,0:T(8,128)S(1)}, u32[]{:S(2)}, u32[]{:S(2)}) collective-permute-start(f32[40,256]{1,0:T(8,128)} %get-tuple-element.42), channel_id=1, source_target_pairs={{0,24},{4,28},{8,16},{12,20},{16,8},{20,12},{24,0},{28,4},{1,25},{... | collective-permute-start | bytes 122888 | tf_op jit(solution)/shard_map/ppermute | solution.py:547
  19.9 5.6 %collective-permute-start.6 = (f32[40,256]{1,0:T(8,128)}, f32[40,256]{1,0:T(8,128)S(1)}, u32[]{:S(2)}, u32[]{:S(2)}) collective-permute-start(f32[40,256]{1,0:T(8,128)} %get-tuple-element.43), channel_id=1, source_target_pairs={{0,28},{4,24},{8,20},{12,16},{16,12},{20,8},{24,4},{28,0},{1,29},{... | collective-permute-start | bytes 122888 | tf_op jit(solution)/shard_map/ppermute | solution.py:547
  25.5 1.6 %copy-start = (bf16[2,2,1024,256]{3,2,1,0:T(8,128)(2,1)S(1)}, bf16[2,2,1024,256]{3,2,1,0:T(8,128)(2,1)}, u32[]{:S(2)}) copy-start(bf16[2,2,1024,256]{3,2,1,0:T(8,128)(2,1)} %constant.59.clone.refs_9_) | copy-start | bytes 6291460
  27.1 0.8 %copy-start.1 = (f32[40,256]{1,0:T(8,128)S(1)}, f32[40,256]{1,0:T(8,128)}, u32[]{:S(2)}) copy-start(f32[40,256]{1,0:T(8,128)} %get-tuple-element.36.refs_0_) | copy-start | bytes 122884
  41.4 9.2 %all-to-all-start.3 = ((f32[8,16,128]{2,1,0:T(8,128)}), f32[8,16,128]{2,1,0:T(8,128)S(1)}, u32[]{:S(2)}, u32[]{:S(2)}) async-start(f32[8,16,128]{2,1,0:T(8,128)} %get-tuple-element.46), calls=%async_computation.3 | async-start | bytes 131072 | tf_op jit(solution)/shard_map/all_to_all | solution.py:559
  61.8 4.3 %collective-permute-start.7 = (f32[64,256]{1,0:T(8,128)S(1)}, f32[64,256]{1,0:T(8,128)S(1)}, u32[]{:S(2)}, u32[]{:S(2)}) collective-permute-start(f32[64,256]{1,0:T(8,128)S(1)} %get-tuple-element.50), channel_id=1, source_target_pairs={{0,1},{1,0},{2,3},{3,2},{4,5},{5,4},{6,7},{7,6},{8,9},{9,8},{10,11... | collective-permute-start | bytes 196616 | tf_op jit(solution)/shard_map/ppermute | solution.py:547
  63.4 5.0 %collective-permute-start.8 = (f32[64,256]{1,0:T(8,128)S(1)}, f32[64,256]{1,0:T(8,128)S(1)}, u32[]{:S(2)}, u32[]{:S(2)}) collective-permute-start(f32[64,256]{1,0:T(8,128)S(1)} %get-tuple-element.51), channel_id=1, source_target_pairs={{0,2},{1,3},{2,0},{3,1},{4,6},{5,7},{6,4},{7,5},{8,10},{9,11},{10,... | collective-permute-start | bytes 196616 | tf_op jit(solution)/shard_map/ppermute | solution.py:547
  64.9 5.2 %collective-permute-start.9 = (f32[64,256]{1,0:T(8,128)S(1)}, f32[64,256]{1,0:T(8,128)S(1)}, u32[]{:S(2)}, u32[]{:S(2)}) collective-permute-start(f32[64,256]{1,0:T(8,128)S(1)} %get-tuple-element.52), channel_id=1, source_target_pairs={{0,3},{1,2},{2,1},{3,0},{4,7},{5,6},{6,5},{7,4},{8,11},{9,10},{10,... | collective-permute-start | bytes 196616 | tf_op jit(solution)/shard_map/ppermute | solution.py:547

commit v8 on v5

--- a/solution.py
+++ b/solution.py
@@ -13,6 +13,7 @@
 SUB = 8
 WINDOWS = 2
 ROW = 256
+PIECE, PIECES, STEP, TOP = jnp.float8_e4m3fn, 3, 32.0, 224.0
 
 precise = lax.Precision.HIGHEST
 NT = (((1,), (1,)), ((), ()))
@@ -27,8 +28,10 @@
     a = np.arange(LANES)
     angle = 2.0 * np.pi * (np.outer(a, a) % LANES) / LANES
     c, s = np.cos(angle), np.sin(angle)
+    order = (a % outer) * (LANES // outer) + a // outer
+    c, s = c[:, order], s[:, order]
     forward = np.block([[c, -s], [s, c]])
-    return twiddle.astype(np.float32), forward.astype(np.float32)
+    return np.concatenate([forward, twiddle]).astype(np.float32)
 
 
 def mode_tables(count):
@@ -158,42 +161,55 @@
 
 
 def sort_kernel(
-    me_ref, scan_hbm, resp_hbm, cycle_hbm, column_hbm, twiddle_hbm, forward_hbm, filtered_ref, *refs,
+    me_ref, scan_hbm, resp_hbm, cycle_hbm, column_hbm, table_hbm, *refs,
     buckets, span, rows, windows,
 ):
     send_refs, refs = refs[:buckets // windows], refs[buckets // windows:]
-    scan_ref, resp_ref, cycle_ref, column_ref, twiddle_ref, forward_ref, arrived = refs[:7]
-    key_ref, val_ref, spec_ref, key_rows, val_rows = refs[7:]
+    scan_ref, resp_ref, cycle_ref, column_ref, table_ref, arrived = refs[:6]
+    key_ref, val_ref, spec_ref, key_rows, val_rows = refs[6:]
     lines, length = scan_ref.shape
     outer = length // LANES
     loads = [
         pltpu.make_async_copy(source, place, arrived.at[i])
         for i, (source, place) in enumerate([
-            (scan_hbm, scan_ref), (twiddle_hbm, twiddle_ref), (forward_hbm, forward_ref),
-            (resp_hbm, resp_ref), (cycle_hbm, cycle_ref), (column_hbm, column_ref),
+            (scan_hbm, scan_ref), (table_hbm, table_ref), (resp_hbm, resp_ref),
+            (cycle_hbm, cycle_ref), (column_hbm, column_ref),
         ])
     ]
     for load in loads:
         load.start()
+    def twiddle_row(k):
+        at = 2 * LANES + k
+        return table_ref[at:at + 1, :LANES], table_ref[at:at + 1, LANES:]
+
     loads[0].wait()
     re, im = small_fft([scan_ref[:, n * LANES:(n + 1) * LANES] for n in range(outer)], None, -1)
     loads[1].wait()
+    forward = table_ref[:2 * LANES, :]
     for k in range(outer):
-        c, s = twiddle_ref[k:k + 1, :LANES], twiddle_ref[k:k + 1, LANES:]
+        c, s = twiddle_row(k)
         here = pl.ds(k * lines, lines)
         spec_ref[here, :LANES] = re[k] * c + im[k] * s
         spec_ref[here, LANES:] = im[k] * c - re[k] * s
     for load in loads[2:]:
         load.wait()
-    spec = jnp.dot(spec_ref[...], forward_ref[...], precision=precise, preferred_element_type=jnp.float32)
-    resp = resp_ref[...] * (1.0 / length)
+    spec = jnp.dot(spec_ref[...], forward, precision=precise, preferred_element_type=jnp.float32)
+    resp = [resp_ref[:, n * LANES:(n + 1) * LANES] * (1.0 / length) for n in range(outer)]
+    step = 1
+    while step < outer:
+        upper = (lax.broadcasted_iota(jnp.int32, (lines, LANES), 1) & step) != 0
+        for n in range(outer):
+            if not n & step:
+                resp[n], resp[n + step] = trade(resp[n], resp[n + step], upper, 1, step)
+        step *= 2
+    resp = jnp.concatenate(resp, axis=0)
     spec = spec * jnp.concatenate([resp, resp], axis=1)
     spec_ref[...] = lax.dot_general(
-        spec, forward_ref[...], NT, precision=precise, preferred_element_type=jnp.float32
+        spec, forward, NT, precision=precise, preferred_element_type=jnp.float32
     )
     re, im = [], []
     for k in range(outer):
-        c, s = twiddle_ref[k:k + 1, :LANES], twiddle_ref[k:k + 1, LANES:]
+        c, s = twiddle_row(k)
         here = pl.ds(k * lines, lines)
         ur, ui = spec_ref[here, :LANES], spec_ref[here, LANES:]
         re.append(ur * c - ui * s)
@@ -202,7 +218,6 @@
     keys = []
     for n in range(outer):
         cols = slice(n * LANES, (n + 1) * LANES)
-        filtered_ref[:, cols] = out[n]
         keys.append((cycle_ref[:, cols] * NPHI + column_ref[:, cols]).astype(jnp.float32))
     vals = list(out)
     sort_registers(keys, vals)
@@ -243,7 +258,7 @@
             send_ref[...] = jnp.full(send_ref.shape, jnp.nan, jnp.float32)
 
 
-def filter_and_sort(me, scan, resp, cycle, column, det_count, band_cycles):
+def filter_and_sort(me, table, scan, resp, cycle, column, det_count, band_cycles):
     lines, length = scan.shape
     tiles = length // LANES
     windows = WINDOWS
@@ -252,19 +267,15 @@
     row_len = tiles * SUB
     rows = LANES // buckets + 2
     reach = (rows + 2 * SUB - 2) // SUB * SUB
-    twiddle, forward = filter_tables(length)
-    resp_rows = resp.reshape(lines, LANES, tiles).transpose(2, 0, 1).reshape(tiles * lines, LANES)
-    operands = [scan, resp_rows, cycle, column, jnp.asarray(twiddle), jnp.asarray(forward)]
+    operands = [scan, resp, cycle, column, table]
     body = functools.partial(sort_kernel, buckets=buckets, span=span, rows=rows, windows=windows)
     vmem = pl.BlockSpec(memory_space=pltpu.VMEM)
     return pl.pallas_call(
         body,
-        out_shape=(
-            jax.ShapeDtypeStruct((lines, length), jnp.float32),
-        ) + (jax.ShapeDtypeStruct((2 * windows * rows, row_len), jnp.float32),) * det_count,
+        out_shape=(jax.ShapeDtypeStruct((2 * windows * rows, row_len), jnp.float32),) * det_count,
         in_specs=[pl.BlockSpec(memory_space=pltpu.SMEM)]
-        + [pl.BlockSpec(memory_space=pltpu.HBM)] * len(operands),
-        out_specs=(vmem,) * (1 + det_count),
+        + [pl.BlockSpec(memory_space=pl.ANY)] * len(operands),
+        out_specs=(vmem,) * det_count,
         scratch_shapes=[pltpu.VMEM(x.shape, x.dtype) for x in operands] + [
             pltpu.SemaphoreType.DMA((len(operands),)),
             pltpu.VMEM((row_len, LANES), jnp.float32),
@@ -273,7 +284,7 @@
             pltpu.VMEM((LANES + reach, row_len), jnp.float32),
             pltpu.VMEM((LANES + reach, row_len), jnp.float32),
         ],
-        compiler_params=pltpu.CompilerParams(vmem_limit_bytes=63 * 1024 * 1024),
+        compiler_params=pltpu.CompilerParams(vmem_limit_bytes=24 * 1024 * 1024),
         name="filter_sort",
     )(me, *operands)
 
@@ -295,26 +306,29 @@
     row_len = recv_ref.shape[2]
     parts = NPHI // ROW
     area = parts * window_cycles
-    a_iota = lax.broadcasted_iota(jnp.int32, (area, row_len), 0).astype(jnp.float32).astype(jnp.bfloat16)
-    b_iota = lax.broadcasted_iota(jnp.int32, (ROW, row_len), 0).astype(jnp.float32).astype(jnp.bfloat16)
-    zero, one = jnp.zeros((), jnp.bfloat16), jnp.ones((), jnp.bfloat16)
+    a_iota = lax.broadcasted_iota(jnp.int32, (area, row_len), 0).astype(jnp.int8)
+    b_iota = (lax.broadcasted_iota(jnp.int32, (ROW, row_len), 0) - ROW // 2).astype(jnp.int8)
+    zero, one = jnp.zeros((), PIECE), jnp.ones((), PIECE)
+    values = recv_ref[:, windows * rows:, :]
+    largest = jnp.max(jnp.max(jnp.abs(values), axis=0), axis=(0, 1), keepdims=True)
+    scale = jnp.where(largest > 0.0, TOP / largest, 1.0)
 
     def build(e, w, slot):
         left, right = left_refs[slot], right_refs[slot]
         for r in range(rows):
             q = recv_ref[e, w * rows + r:w * rows + r + 1, :].astype(jnp.int32)
-            v = recv_ref[e, (windows + w) * rows + r:(windows + w) * rows + r + 1, :]
-            high, low = split2(v)
+            rest = recv_ref[e, (windows + w) * rows + r:(windows + w) * rows + r + 1, :] * scale
             cycle = q >> 11
             inside = (q >= 0) & (cycle < window_cycles)
-            a = jnp.where(inside, ((q >> 8) & (parts - 1)) * window_cycles + cycle, -1)
-            a = a.astype(jnp.float32).astype(jnp.bfloat16)
-            b = (q & (ROW - 1)).astype(jnp.float32).astype(jnp.bfloat16)
+            a = jnp.where(inside, ((q >> 8) & (parts - 1)) * window_cycles + cycle, -1).astype(jnp.int8)
+            b = ((q & (ROW - 1)) - ROW // 2).astype(jnp.int8)
             cols = slice(r * row_len, (r + 1) * row_len)
             hit = a_iota == a
-            left[:area, cols] = jnp.where(hit, high, zero)
-            left[area:2 * area, cols] = jnp.where(hit, low, zero)
-            left[2 * area:, cols] = jnp.where(hit, one, zero)
+            for p in range(PIECES):
+                piece = rest.astype(PIECE)
+                rest = (rest - piece.astype(jnp.float32)) * STEP
+                left[p * area:(p + 1) * area, cols] = jnp.where(hit, piece, zero)
+            left[PIECES * area:, cols] = jnp.where(hit, one, zero)
             right[:, cols] = jnp.where(b_iota == b, one, zero)
 
     def multiply(slot):
@@ -340,7 +354,10 @@
             build(0, w + 1, 0)
         multiply(1)
         acc = acc_ref[...]
-        sky = (acc[:area] + acc[area:2 * area]) / jnp.maximum(acc[2 * area:], 1.0)
+        total = acc[(PIECES - 1) * area:PIECES * area]
+        for p in range(PIECES - 2, -1, -1):
+            total = acc[p * area:(p + 1) * area] + total * (1.0 / STEP)
+        sky = total / scale / jnp.maximum(acc[PIECES * area:], 1.0)
         for c8 in range(parts):
             map_ref[w * window_cycles:(w + 1) * window_cycles, c8 * ROW:(c8 + 1) * ROW] = (
                 sky[c8 * window_cycles:(c8 + 1) * window_cycles]
@@ -369,7 +386,6 @@
     owners, group_rows, lanes = send_ref.shape
     groups = cycles // group_rows
     lane_group = lax.broadcasted_iota(jnp.int32, (group_rows, lanes), 1) // (lanes // groups)
-    values = recv_ref[:, windows * rows:, :]
     flag_ref[0] = (jnp.max(jnp.where(values == values, 0.0, 1.0)) > 0.0).astype(jnp.int32)
     for d in range(owners):
         block = moved[:, d * lanes:(d + 1) * lanes]
@@ -407,11 +423,11 @@
         out_specs=(vmem, vmem, pl.BlockSpec(memory_space=pltpu.SMEM)),
         scratch_shapes=[
             pltpu.VMEM((sources, lines, row_len), jnp.float32),
-            pltpu.VMEM((3 * area, depth), jnp.bfloat16),
-            pltpu.VMEM((3 * area, depth), jnp.bfloat16),
-            pltpu.VMEM((ROW, depth), jnp.bfloat16),
-            pltpu.VMEM((ROW, depth), jnp.bfloat16),
-            pltpu.VMEM((3 * area, ROW), jnp.float32),
+            pltpu.VMEM(((PIECES + 1) * area, depth), PIECE),
+            pltpu.VMEM(((PIECES + 1) * area, depth), PIECE),
+            pltpu.VMEM((ROW, depth), PIECE),
+            pltpu.VMEM((ROW, depth), PIECE),
+            pltpu.VMEM(((PIECES + 1) * area, ROW), jnp.float32),
         ],
         compiler_params=pltpu.CompilerParams(vmem_limit_bytes=40 * 1024 * 1024),
         name="bin_modes",
@@ -498,7 +514,30 @@
     return jnp.sum(lax.all_to_all(parts, axis, split_axis=0, concat_axis=0, tiled=True), axis=0)
 
 
-def dense_path(filtered, cycle_offset, column, order_slot, band_cycles, det_count):
+def dense_filter(table, scan, resp):
+    lines, length = scan.shape
+    outer = length // LANES
+    forward = table[:2 * LANES]
+    c, s = table[2 * LANES:, :LANES], table[2 * LANES:, LANES:]
+    k = jnp.arange(outer, dtype=jnp.int32)
+    angle = 2.0 * jnp.pi / outer * (k[:, None] * k[None, :] % outer).astype(jnp.float32)
+    x = scan.reshape(lines, outer, LANES)
+    re = jnp.einsum("lna,nk->lka", x, jnp.cos(angle), precision=precise)
+    im = -jnp.einsum("lna,nk->lka", x, jnp.sin(angle), precision=precise)
+    spec = jnp.concatenate([re * c + im * s, im * c - re * s], axis=-1)
+    spec = jnp.einsum("lki,ij->lkj", spec, forward, precision=precise)
+    split = LANES // outer
+    weight = resp.reshape(lines, outer, split, outer).transpose(0, 3, 2, 1).reshape(lines, outer, LANES)
+    spec = spec * jnp.concatenate([weight, weight], axis=-1)
+    spec = jnp.einsum("lki,ji->lkj", spec, forward, precision=precise)
+    ur, ui = spec[..., :LANES], spec[..., LANES:]
+    out = jnp.einsum("lka,kn->lna", ur * c - ui * s, jnp.cos(angle), precision=precise)
+    out = out - jnp.einsum("lka,kn->lna", ui * c + ur * s, jnp.sin(angle), precision=precise)
+    return (out / length).reshape(lines, length)
+
+
+def dense_path(table, scan_lines, response, cycle_offset, column, order_slot, band_cycles, det_count):
+    filtered = dense_filter(table, scan_lines, response)
     flat_index = (cycle_offset * NPHI + column).reshape(-1)
     empty = jnp.zeros((band_cycles * NPHI,), jnp.float32)
     partial_value = empty.at[flat_index].add(filtered.reshape(-1)).reshape(band_cycles, NPHI)
@@ -521,23 +560,27 @@
 
 def swap_blocks(blocks, axis):
     count = len(blocks)
-    return [blocks[0]] + [
-        lax.ppermute(blocks[k], axis, [(i, i ^ k) for i in range(count)]) for k in range(1, count)
-    ]
+    out = list(blocks)
+    for k in range(count - 1, 0, -1):
+        out[k] = lax.ppermute(blocks[k], axis, [(i, i ^ k) for i in range(count)])
+    return out
 
 
 def local(scan_lines, response, cycle_offset, column, order_slot, legendre, *, det_count, band_count):
     slots, band_cycles, degrees = legendre.shape
     me = lax.axis_index("det").astype(jnp.int32).reshape(1)
-    filtered, *send = filter_and_sort(
-        me, scan_lines, response, cycle_offset, column, det_count, band_cycles
+    table = jnp.asarray(filter_tables(scan_lines.shape[1]))
+    send = filter_and_sort(
+        me, table, scan_lines, response, cycle_offset, column, det_count, band_cycles
     )
     recv = swap_blocks(send, "det")
-    sky_map, modes, crowded = bin_and_modes(recv, order_slot, band_cycles)
+    sky_map, modes, crowded = bin_and_modes(recv[::-1], order_slot, band_cycles)
     modes = lax.all_to_all(modes, "det", split_axis=0, concat_axis=0, tiled=True)
     sky_map, modes = lax.cond(
         crowded[0] > 0,
-        lambda: dense_path(filtered, cycle_offset, column, order_slot, band_cycles, det_count),
+        lambda: dense_path(
+            table, scan_lines, response, cycle_offset, column, order_slot, band_cycles, det_count
+        ),
         lambda: (sky_map, modes),
     )
     band = lax.axis_index("band").astype(jnp.int32)

time: 71.6 us -> 65.2 us (0.911)
  Pallas kernels: 31.9 us -> 28.4 us
  local copies, waits for them, and re-layouts: 5.48 us -> 2.81 us
  waiting for transfers between devices: 15.1 us -> 13.1 us
  starting transfers between devices: 16.6 us -> 17.4 us
    pallas_call x1, Pallas kernels: 12.2 us -> 9.48 us  [bin_and_modes(): pl.pallas_call(functools.partial(bin_kernel, sources=sources, windows=win...]
    ppermute x10, waiting for transfers between devices: 9.92 us -> 7.91 us  [swap_blocks(): out[k] = lax.ppermute(blocks[k], axis, [(i, i ^ k) for i in range(count)])]
    reshape x1 -> x0, local copies, waits for them, and re-layouts: 1.07 us -> none  [filter_and_sort(): resp.reshape(lines, LANES, tiles).transpose(2, 0, 1)]
    all_to_all x1, starting transfers between devices: 3.36 us -> 4.3 us  [local(): lax.all_to_all(modes, 'det', split_axis=0, concat_axis=0, tiled=True)]
    transpose x1 -> x0, local copies, waits for them, and re-layouts: 0.83 us -> none  [filter_and_sort(): resp.reshape(lines, LANES, tiles).transpose(2, 0, 1)]
    pallas_call x1, Pallas kernels: 8.55 us -> 7.77 us  [filter_and_sort(): pl.pallas_call(body, out_shape=(jax.ShapeDtypeStruct((2 * windows * rows,...]
    unnamed x12 -> x16, local copies, waits for them, and re-layouts: 3.24 us -> 2.48 us
  transfers between devices with their start and end apart: 11 -> 11, of which waited for: 7 -> 8; matrix products, arithmetic and copies ran while one was open for 1% -> 2% of each run, Pallas kernels for 0% -> 0%
where the time goes in v8:
time: 65.2 us; the launch traced here: 64.9 us
  Pallas kernels  28.4 us (44%)
  starting transfers between devices  17.4 us (27%)
  waiting for transfers between devices  13.1 us (20%)
  local copies, waits for them, and re-layouts  2.81 us (4%)
  other arithmetic  1.49 us (2%)
  between operations  1.4 us (2%)
    ppermute x10, starting transfers between devices, swap_blocks(): out[k] = lax.ppermute(blocks[k], axis, [(i, i ^ k) for i in range(count)])  13.1 us
    pallas_call x1, Pallas kernels, legendre_sums(): pl.pallas_call(functools.partial(legendre_kernel, owners=owners), out_sha...  11.2 us
    pallas_call x1, Pallas kernels, bin_and_modes(): pl.pallas_call(functools.partial(bin_kernel, sources=sources, windows=win...  9.48 us
    ppermute x10, waiting for transfers between devices, swap_blocks(): out[k] = lax.ppermute(blocks[k], axis, [(i, i ^ k) for i in range(count)])  7.91 us
    pallas_call x1, Pallas kernels, filter_and_sort(): pl.pallas_call(body, out_shape=(jax.ShapeDtypeStruct((2 * windows * rows,...  7.77 us
    all_to_all x1, waiting for transfers between devices, local(): lax.all_to_all(modes, 'det', split_axis=0, concat_axis=0, tiled=True)  5.19 us
    all_to_all x1, starting transfers between devices, local(): lax.all_to_all(modes, 'det', split_axis=0, concat_axis=0, tiled=True)  4.3 us
    unnamed x16, local copies, waits for them, and re-layouts  2.48 us
  transfers between devices with their start and end apart: 11, of which 8 were waited for; matrix products, arithmetic and copies ran while one was open for 2% of the time, Pallas kernels for 0%

profile of v8, /device:TPU:0, one launch (start us, length us, event | category | flops | bytes accessed | tf_op | source)
XLA Modules:
  0.0 64.9 jit_solution(4231165589325552075)
XLA Ops:
  0.7 7.8 %filter_sort.1 = (f32[40,256]{1,0:T(8,128)S(1)}, f32[40,256]{1,0:T(8,128)S(1)}, f32[40,256]{1,0:T(8,128)S(1)}, f32[40,256]{1,0:T(8,128)S(1)}, f32[40,256]{1,0:T(...) custom-call(s32[1]{0:T(128)} %bitcast.12.me_ref, f32[8,4096]{1,0:T(8,128)} %scan_hbm.1, ...), custom_call_target="tpu_custom_call" | custom-call | tf_op jit(solution)/shard_map/filter_sort/pallas_call | solution.py:273
  8.5 4.6 %collective-permute-start = (f32[40,256]{1,0:T(8,128)S(1)}, f32[40,256]{1,0:T(8,128)S(1)}, u32[]{:S(2)}, u32[]{:S(2)}) collective-permute-start(f32[40,256]{1,0:T(8,128)S(1)} %get-tuple-element.41), channel_id=1, source_target_pairs={{0,28},{4,24},{8,20},{12,16},{16,12},{20,8},{24,4},{28,0},{1,29},{... | collective-permute-start | bytes 122888 | tf_op jit(solution)/shard_map/ppermute | solution.py:565
  13.0 0.6 collective-permute-start.1
  14.1 2.2 %collective-permute-start.3 = (f32[40,256]{1,0:T(8,128)S(1)}, f32[40,256]{1,0:T(8,128)S(1)}, u32[]{:S(2)}, u32[]{:S(2)}) collective-permute-start(f32[40,256]{1,0:T(8,128)S(1)} %get-tuple-element.44), channel_id=1, source_target_pairs={{0,16},{4,20},{8,24},{12,28},{16,0},{20,4},{24,8},{28,12},{1,17},{... | collective-permute-start | bytes 122888 | tf_op jit(solution)/shard_map/ppermute | solution.py:565
  16.2 1.0 %collective-permute-start.4 = (f32[40,256]{1,0:T(8,128)S(1)}, f32[40,256]{1,0:T(8,128)S(1)}, u32[]{:S(2)}, u32[]{:S(2)}) collective-permute-start(f32[40,256]{1,0:T(8,128)S(1)} %get-tuple-element.45), channel_id=1, source_target_pairs={{0,12},{4,8},{8,4},{12,0},{16,28},{20,24},{24,20},{28,16},{1,13},{... | collective-permute-start | bytes 122888 | tf_op jit(solution)/shard_map/ppermute | solution.py:565
  17.2 0.7 %and_multiply_fusion = (s32[256]{0:T(256)S(1)}, s32[256]{0:T(256)S(1)}) fusion(s32[256]{0:T(256)} %param.15), kind=kLoop, calls=%fused_computation.100 | loop fusion | flops 768 | bytes 3072 | tf_op jit(solution)/shard_map/mul | solution.py:410
  18.0 0.9 %collective-permute-start.5 = (f32[40,256]{1,0:T(8,128)S(1)}, f32[40,256]{1,0:T(8,128)S(1)}, u32[]{:S(2)}, u32[]{:S(2)}) collective-permute-start(f32[40,256]{1,0:T(8,128)S(1)} %get-tuple-element.46), channel_id=1, source_target_pairs={{0,8},{4,12},{8,0},{12,4},{16,24},{20,28},{24,16},{28,20},{1,9},{5... | collective-permute-start | bytes 122888 | tf_op jit(solution)/shard_map/ppermute | solution.py:565
  18.9 0.5 collective-permute-done.1.refs_1_
  19.6 0.5 collective-permute-done.2.refs_2_
  20.1 1.9 %collective-permute-done.3.refs_3_ = f32[40,256]{1,0:T(8,128)S(1)} collective-permute-done((f32[40,256]{1,0:T(8,128)S(1)}, f32[40,256]{1,0:T(8,128)S(1)}, u32[]{:S(2)}, u32[]{:S(2)}) %collective-permute-start.3) | collective-permute-done | bytes 40992 | tf_op jit(solution)/shard_map/ppermute | solution.py:565
  22.0 0.4 collective-permute-done.5.refs_5_
  22.4 1.2 %copy-done = bf16[2,1024,256]{2,1,0:T(8,128)(2,1)S(1)} copy-done((bf16[2,1024,256]{2,1,0:T(8,128)(2,1)S(1)}, bf16[2,1024,256]{2,1,0:T(8,128)(2,1)}, u32[]{:S(2)}) %copy-start) | copy-done | bytes 1048600
  23.6 1.2 %copy-done.1 = bf16[2,1024,256]{2,1,0:T(8,128)(2,1)S(1)} copy-done((bf16[2,1024,256]{2,1,0:T(8,128)(2,1)S(1)}, bf16[2,1024,256]{2,1,0:T(8,128)(2,1)}, u32[]{:S(2)}) %copy-start.1) | copy-done | bytes 1048600
  24.8 9.5 %bin_modes.1 = (f32[32,2048]{1,0:T(8,128)}, f32[8,16,128]{2,1,0:T(8,128)}, s32[1]{0:T(128)}) custom-call(f32[40,256]{1,0:T(8,128)S(1)} %collective-permute-done.refs_0_, f32[40,256]{1,0:T(8,128)S(1)} %collective-permute-done.1.refs_1_, f32[40,256]{1,0:T(8,128)S(1)} %collective-permute-done.2.refs_2_, f32[40,256]{1,0:T(8,128)S(1)} %collective-permute-done.3.refs_3_, ...), custom_call_target="tpu_custom_call" | custom-call | tf_op jit(solution)/shard_map/bin_modes/pallas_call | solution.py:415
  34.3 4.3 %all-to-all-start.3 = ((f32[8,16,128]{2,1,0:T(8,128)}), f32[8,16,128]{2,1,0:T(8,128)S(1)}, u32[]{:S(2)}, u32[]{:S(2)}) async-start(f32[8,16,128]{2,1,0:T(8,128)} %get-tuple-element.51), calls=%async_computation.3 | async-start | bytes 131072 | tf_op jit(solution)/shard_map/all_to_all | solution.py:578
  39.4 5.2 %all-to-all-done.3 = f32[8,16,128]{2,1,0:T(8,128)S(1)} async-done(((f32[8,16,128]{2,1,0:T(8,128)}), f32[8,16,128]{2,1,0:T(8,128)S(1)}, u32[]{:S(2)}, u32[]{:S(2)}) %all-to-all-start.3) | async-done | bytes 65568 | tf_op jit(solution)/shard_map/all_to_all | solution.py:578
  44.8 11.2 %legendre_sums.1 = (f32[64,256]{1,0:T(8,128)S(1)}, f32[64,256]{1,0:T(8,128)S(1)}, f32[64,256]{1,0:T(8,128)S(1)}, f32[64,256]{1,0:T(8,128)S(1)}) custom-call(s32[1]{0:T(128)} %bitcast.11.me_ref, f32[8,16,128]{2,1,0:T(8,128)S(1)} %get-tuple-element.52.recv_ref, f32[32,256,1024]{2,1,0:T(8,128)} %table_ref.1), custom_call_target="tpu_custom_call" | custom-call | tf_op jit(solution)/shard_map/legendre_sums/pallas_call | solution.py:495
  56.0 1.6 %collective-permute-start.7 = (f32[64,256]{1,0:T(8,128)S(1)}, f32[64,256]{1,0:T(8,128)S(1)}, u32[]{:S(2)}, u32[]{:S(2)}) collective-permute-start(f32[64,256]{1,0:T(8,128)S(1)} %get-tuple-element.54), channel_id=1, source_target_pairs={{0,1},{1,0},{2,3},{3,2},{4,5},{5,4},{6,7},{7,6},{8,9},{9,8},{10,11... | collective-permute-start | bytes 196616 | tf_op jit(solution)/shard_map/ppermute | solution.py:565
  57.6 1.5 %collective-permute-start.8 = (f32[64,256]{1,0:T(8,128)S(1)}, f32[64,256]{1,0:T(8,128)S(1)}, u32[]{:S(2)}, u32[]{:S(2)}) collective-permute-start(f32[64,256]{1,0:T(8,128)S(1)} %get-tuple-element.55), channel_id=1, source_target_pairs={{0,2},{1,3},{2,0},{3,1},{4,6},{5,7},{6,4},{7,5},{8,10},{9,11},{10,... | collective-permute-start | bytes 196616 | tf_op jit(solution)/shard_map/ppermute | solution.py:565
  59.1 0.5 collective-permute-start.9
  59.6 0.7 %collective-permute-done.7 = f32[64,256]{1,0:T(8,128)S(1)} collective-permute-done((f32[64,256]{1,0:T(8,128)S(1)}, f32[64,256]{1,0:T(8,128)S(1)}, u32[]{:S(2)}, u32[]{:S(2)}) %collective-permute-start.7) | collective-permute-done | bytes 65568 | tf_op jit(solution)/shard_map/ppermute | solution.py:565
  60.3 2.2 %collective-permute-done.8 = f32[64,256]{1,0:T(8,128)S(1)} collective-permute-done((f32[64,256]{1,0:T(8,128)S(1)}, f32[64,256]{1,0:T(8,128)S(1)}, u32[]{:S(2)}, u32[]{:S(2)}) %collective-permute-start.8) | collective-permute-done | bytes 65568 | tf_op jit(solution)/shard_map/ppermute | solution.py:565
  62.5 1.7 %collective-permute-done.9 = f32[64,256]{1,0:T(8,128)S(1)} collective-permute-done((f32[64,256]{1,0:T(8,128)S(1)}, f32[64,256]{1,0:T(8,128)S(1)}, u32[]{:S(2)}, u32[]{:S(2)}) %collective-permute-start.9) | collective-permute-done | bytes 65568 | tf_op jit(solution)/shard_map/ppermute | solution.py:565
  64.3 0.6 broadcast_select_fusion
  (30 shorter events, 1.2 us)
Async XLA Ops:
  0.6 43.9 %copy-start.2 = (f32[288,256]{1,0:T(8,128)S(1)}, f32[288,256]{1,0:T(8,128)}, u32[]{:S(2)}) copy-start(f32[288,256]{1,0:T(8,128)} %constant.76.clone.table_hbm) | copy-start | bytes 884740
  0.6 43.9 %copy-start.3 = (f32[8,4096]{1,0:T(8,128)S(1)}, f32[8,4096]{1,0:T(8,128)}, u32[]{:S(2)}) copy-start(f32[8,4096]{1,0:T(8,128)} %scan_hbm.1) | copy-start | bytes 393220
  0.7 43.9 %copy-start.4 = (f32[8,4096]{1,0:T(8,128)S(1)}, f32[8,4096]{1,0:T(8,128)}, u32[]{:S(2)}) copy-start(f32[8,4096]{1,0:T(8,128)} %resp_hbm.1) | copy-start | bytes 393220
  0.7 43.9 %copy-start.5 = (s32[8,4096]{1,0:T(8,128)S(1)}, s32[8,4096]{1,0:T(8,128)}, u32[]{:S(2)}) copy-start(s32[8,4096]{1,0:T(8,128)} %cycle_hbm.1) | copy-start | bytes 393220
  0.7 43.9 %copy-start.6 = (s32[8,4096]{1,0:T(8,128)S(1)}, s32[8,4096]{1,0:T(8,128)}, u32[]{:S(2)}) copy-start(s32[8,4096]{1,0:T(8,128)} %column_hbm.1) | copy-start | bytes 393220
  0.7 38.0 %copy-start.7 = (s32[256]{0:T(256)S(1)}, s32[256]{0:T(256)}, u32[]{:S(2)}) copy-start(s32[256]{0:T(256)} %param.15) | copy-start | bytes 3076
  8.5 9.6 %collective-permute-start = (f32[40,256]{1,0:T(8,128)S(1)}, f32[40,256]{1,0:T(8,128)S(1)}, u32[]{:S(2)}, u32[]{:S(2)}) collective-permute-start(f32[40,256]{1,0:T(8,128)S(1)} %get-tuple-element.41), channel_id=1, source_target_pairs={{0,28},{4,24},{8,20},{12,16},{16,12},{20,8},{24,4},{28,0},{1,29},{... | collective-permute-start | bytes 122888 | tf_op jit(solution)/shard_map/ppermute | solution.py:565
  13.0 6.3 %collective-permute-start.1 = (f32[40,256]{1,0:T(8,128)S(1)}, f32[40,256]{1,0:T(8,128)S(1)}, u32[]{:S(2)}, u32[]{:S(2)}) collective-permute-start(f32[40,256]{1,0:T(8,128)S(1)} %get-tuple-element.42), channel_id=1, source_target_pairs={{0,24},{4,28},{8,16},{12,20},{16,8},{20,12},{24,0},{28,4},{1,25},{... | collective-permute-start | bytes 122888 | tf_op jit(solution)/shard_map/ppermute | solution.py:565
  13.7 6.4 %collective-permute-start.2 = (f32[40,256]{1,0:T(8,128)S(1)}, f32[40,256]{1,0:T(8,128)S(1)}, u32[]{:S(2)}, u32[]{:S(2)}) collective-permute-start(f32[40,256]{1,0:T(8,128)S(1)} %get-tuple-element.43), channel_id=1, source_target_pairs={{0,20},{4,16},{8,28},{12,24},{16,4},{20,0},{24,12},{28,8},{1,21},{... | collective-permute-start | bytes 122888 | tf_op jit(solution)/shard_map/ppermute | solution.py:565
  14.1 7.9 %collective-permute-start.3 = (f32[40,256]{1,0:T(8,128)S(1)}, f32[40,256]{1,0:T(8,128)S(1)}, u32[]{:S(2)}, u32[]{:S(2)}) collective-permute-start(f32[40,256]{1,0:T(8,128)S(1)} %get-tuple-element.44), channel_id=1, source_target_pairs={{0,16},{4,20},{8,24},{12,28},{16,0},{20,4},{24,8},{28,12},{1,17},{... | collective-permute-start | bytes 122888 | tf_op jit(solution)/shard_map/ppermute | solution.py:565
  16.2 5.7 %collective-permute-start.4 = (f32[40,256]{1,0:T(8,128)S(1)}, f32[40,256]{1,0:T(8,128)S(1)}, u32[]{:S(2)}, u32[]{:S(2)}) collective-permute-start(f32[40,256]{1,0:T(8,128)S(1)} %get-tuple-element.45), channel_id=1, source_target_pairs={{0,12},{4,8},{8,4},{12,0},{16,28},{20,24},{24,20},{28,16},{1,13},{... | collective-permute-start | bytes 122888 | tf_op jit(solution)/shard_map/ppermute | solution.py:565
  18.0 4.4 %collective-permute-start.5 = (f32[40,256]{1,0:T(8,128)S(1)}, f32[40,256]{1,0:T(8,128)S(1)}, u32[]{:S(2)}, u32[]{:S(2)}) collective-permute-start(f32[40,256]{1,0:T(8,128)S(1)} %get-tuple-element.46), channel_id=1, source_target_pairs={{0,8},{4,12},{8,0},{12,4},{16,24},{20,28},{24,16},{28,20},{1,9},{5... | collective-permute-start | bytes 122888 | tf_op jit(solution)/shard_map/ppermute | solution.py:565
  19.4 3.0 %collective-permute-start.6 = (f32[40,256]{1,0:T(8,128)S(1)}, f32[40,256]{1,0:T(8,128)S(1)}, u32[]{:S(2)}, u32[]{:S(2)}) collective-permute-start(f32[40,256]{1,0:T(8,128)S(1)} %get-tuple-element.47), channel_id=1, source_target_pairs={{0,4},{4,0},{8,12},{12,8},{16,20},{20,16},{24,28},{28,24},{1,5},{5... | collective-permute-start | bytes 122888 | tf_op jit(solution)/shard_map/ppermute | solution.py:565
  22.4 1.2 %copy-start = (bf16[2,1024,256]{2,1,0:T(8,128)(2,1)S(1)}, bf16[2,1024,256]{2,1,0:T(8,128)(2,1)}, u32[]{:S(2)}) copy-start(bf16[2,1024,256]{2,1,0:T(8,128)(2,1)} %constant.77.clone.refs_9_) | copy-start | bytes 3145732
  23.6 1.2 %copy-start.1 = (bf16[2,1024,256]{2,1,0:T(8,128)(2,1)S(1)}, bf16[2,1024,256]{2,1,0:T(8,128)(2,1)}, u32[]{:S(2)}) copy-start(bf16[2,1024,256]{2,1,0:T(8,128)(2,1)} %constant.78.clone.refs_10_) | copy-start | bytes 3145732
  34.3 10.2 %all-to-all-start.3 = ((f32[8,16,128]{2,1,0:T(8,128)}), f32[8,16,128]{2,1,0:T(8,128)S(1)}, u32[]{:S(2)}, u32[]{:S(2)}) async-start(f32[8,16,128]{2,1,0:T(8,128)} %get-tuple-element.51), calls=%async_computation.3 | async-start | bytes 131072 | tf_op jit(solution)/shard_map/all_to_all | solution.py:578
  56.0 4.3 %collective-permute-start.7 = (f32[64,256]{1,0:T(8,128)S(1)}, f32[64,256]{1,0:T(8,128)S(1)}, u32[]{:S(2)}, u32[]{:S(2)}) collective-permute-start(f32[64,256]{1,0:T(8,128)S(1)} %get-tuple-element.54), channel_id=1, source_target_pairs={{0,1},{1,0},{2,3},{3,2},{4,5},{5,4},{6,7},{7,6},{8,9},{9,8},{10,11... | collective-permute-start | bytes 196616 | tf_op jit(solution)/shard_map/ppermute | solution.py:565
  57.6 5.0 %collective-permute-start.8 = (f32[64,256]{1,0:T(8,128)S(1)}, f32[64,256]{1,0:T(8,128)S(1)}, u32[]{:S(2)}, u32[]{:S(2)}) collective-permute-start(f32[64,256]{1,0:T(8,128)S(1)} %get-tuple-element.55), channel_id=1, source_target_pairs={{0,2},{1,3},{2,0},{3,1},{4,6},{5,7},{6,4},{7,5},{8,10},{9,11},{10,... | collective-permute-start | bytes 196616 | tf_op jit(solution)/shard_map/ppermute | solution.py:565
  59.1 5.2 %collective-permute-start.9 = (f32[64,256]{1,0:T(8,128)S(1)}, f32[64,256]{1,0:T(8,128)S(1)}, u32[]{:S(2)}, u32[]{:S(2)}) collective-permute-start(f32[64,256]{1,0:T(8,128)S(1)} %get-tuple-element.56), channel_id=1, source_target_pairs={{0,3},{1,2},{2,1},{3,0},{4,7},{5,6},{6,5},{7,4},{8,11},{9,10},{10,... | collective-permute-start | bytes 196616 | tf_op jit(solution)/shard_map/ppermute | solution.py:565

commit v9 on v8

--- a/solution.py
+++ b/solution.py
@@ -14,6 +14,7 @@
 WINDOWS = 2
 ROW = 256
 PIECE, PIECES, STEP, TOP = jnp.float8_e4m3fn, 3, 32.0, 224.0
+KEEP = 2.0**20 + 1.0
 
 precise = lax.Precision.HIGHEST
 NT = (((1,), (1,)), ((), ()))
@@ -45,7 +46,7 @@
     table = np.stack(out).astype(np.float32)
     high = table.astype(jnp.bfloat16)
     low = (table - high.astype(np.float32)).astype(jnp.bfloat16)
-    return high, low
+    return np.stack([high, low])
 
 
 def small_fft(re, im, sign):
@@ -161,10 +162,11 @@
 
 
 def sort_kernel(
-    me_ref, scan_hbm, resp_hbm, cycle_hbm, column_hbm, table_hbm, *refs,
+    me_ref, scan_hbm, resp_hbm, cycle_hbm, column_hbm, table_hbm, modes_hbm, *refs,
     buckets, span, rows, windows,
 ):
     send_refs, refs = refs[:buckets // windows], refs[buckets // windows:]
+    modes_ref, refs = refs[0], refs[1:]
     scan_ref, resp_ref, cycle_ref, column_ref, table_ref, arrived = refs[:6]
     key_ref, val_ref, spec_ref, key_rows, val_rows = refs[6:]
     lines, length = scan_ref.shape
@@ -173,7 +175,7 @@
         pltpu.make_async_copy(source, place, arrived.at[i])
         for i, (source, place) in enumerate([
             (scan_hbm, scan_ref), (table_hbm, table_ref), (resp_hbm, resp_ref),
-            (cycle_hbm, cycle_ref), (column_hbm, column_ref),
+            (cycle_hbm, cycle_ref), (column_hbm, column_ref), (modes_hbm, modes_ref),
         ])
     ]
     for load in loads:
@@ -191,7 +193,7 @@
         here = pl.ds(k * lines, lines)
         spec_ref[here, :LANES] = re[k] * c + im[k] * s
         spec_ref[here, LANES:] = im[k] * c - re[k] * s
-    for load in loads[2:]:
+    for load in loads[2:-1]:
         load.wait()
     spec = jnp.dot(spec_ref[...], forward, precision=precise, preferred_element_type=jnp.float32)
     resp = [resp_ref[:, n * LANES:(n + 1) * LANES] * (1.0 / length) for n in range(outer)]
@@ -257,8 +259,10 @@
         for send_ref in send_refs:
             send_ref[...] = jnp.full(send_ref.shape, jnp.nan, jnp.float32)
 
-
-def filter_and_sort(me, table, scan, resp, cycle, column, det_count, band_cycles):
+    loads[-1].wait()
+
+
+def filter_and_sort(me, table, mode_table, scan, resp, cycle, column, det_count, band_cycles):
     lines, length = scan.shape
     tiles = length // LANES
     windows = WINDOWS
@@ -272,12 +276,13 @@
     vmem = pl.BlockSpec(memory_space=pltpu.VMEM)
     return pl.pallas_call(
         body,
-        out_shape=(jax.ShapeDtypeStruct((2 * windows * rows, row_len), jnp.float32),) * det_count,
+        out_shape=(jax.ShapeDtypeStruct((2 * windows * rows, row_len), jnp.float32),) * det_count
+        + (jax.ShapeDtypeStruct(mode_table.shape, mode_table.dtype),),
         in_specs=[pl.BlockSpec(memory_space=pltpu.SMEM)]
-        + [pl.BlockSpec(memory_space=pl.ANY)] * len(operands),
-        out_specs=(vmem,) * det_count,
+        + [pl.BlockSpec(memory_space=pl.ANY)] * (len(operands) + 1),
+        out_specs=(vmem,) * (det_count + 1),
         scratch_shapes=[pltpu.VMEM(x.shape, x.dtype) for x in operands] + [
-            pltpu.SemaphoreType.DMA((len(operands),)),
+            pltpu.SemaphoreType.DMA((len(operands) + 1,)),
             pltpu.VMEM((row_len, LANES), jnp.float32),
             pltpu.VMEM((row_len, LANES), jnp.float32),
             pltpu.VMEM((tiles * lines, 2 * LANES), jnp.float32),
@@ -286,7 +291,7 @@
         ],
         compiler_params=pltpu.CompilerParams(vmem_limit_bytes=24 * 1024 * 1024),
         name="filter_sort",
-    )(me, *operands)
+    )(me, *operands, mode_table)
 
 
 def split2(x):
@@ -298,7 +303,7 @@
 def bin_kernel(
     *refs, sources, windows, rows, window_cycles
 ):
-    recv_refs, (pick_ref, table_hi, table_lo, map_ref, send_ref, flag_ref) = refs[:sources], refs[sources:-6]
+    recv_refs, (pick_ref, table_ref, map_ref, send_ref, flag_ref) = refs[:sources], refs[sources:-6]
     recv_ref, left_a, left_b, right_a, right_b, acc_ref = refs[-6:]
     for e in range(sources):
         recv_ref[e] = recv_refs[e][...]
@@ -325,7 +330,8 @@
             cols = slice(r * row_len, (r + 1) * row_len)
             hit = a_iota == a
             for p in range(PIECES):
-                piece = rest.astype(PIECE)
+                spread = rest * KEEP
+                piece = (spread - (spread - rest)).astype(PIECE)
                 rest = (rest - piece.astype(jnp.float32)) * STEP
                 left[p * area:(p + 1) * area, cols] = jnp.where(hit, piece, zero)
             left[PIECES * area:, cols] = jnp.where(hit, one, zero)
@@ -368,8 +374,8 @@
     for parity in (0, 1):
         a, b = map_ref[:, :half], map_ref[:, half:]
         high, low = split2(a + b if parity == 0 else a - b)
-        first = jnp.dot(jnp.concatenate([high, low], axis=0), table_hi[parity], preferred_element_type=jnp.float32)
-        second = jnp.dot(high, table_lo[parity], preferred_element_type=jnp.float32)
+        first = jnp.dot(jnp.concatenate([high, low], axis=0), table_ref[0, parity], preferred_element_type=jnp.float32)
+        second = jnp.dot(high, table_ref[1, parity], preferred_element_type=jnp.float32)
         modes.append(first[:cycles] + first[cycles:] + second)
     modes = jnp.concatenate(modes, axis=1)
     count = modes.shape[1]
@@ -395,7 +401,7 @@
         send_ref[d] = out
 
 
-def bin_and_modes(recv, order_slot, band_cycles):
+def bin_and_modes(mode_table, recv, order_slot, band_cycles):
     sources = len(recv)
     lines, row_len = recv[0].shape
     windows = WINDOWS
@@ -404,7 +410,6 @@
     count = order_slot.shape[0]
     slots = count // sources
     groups = LANES // (2 * slots)
-    high, low = mode_tables(count)
     m = order_slot.reshape(sources, 1, 1, slots)
     part = jnp.arange(2, dtype=jnp.int32).reshape(1, 1, 2, 1)
     pick = (m & 1) * count + part * (count // 2) + (m >> 1)
@@ -419,7 +424,7 @@
             jax.ShapeDtypeStruct((sources, cycles // groups, LANES), jnp.float32),
             jax.ShapeDtypeStruct((1,), jnp.int32),
         ),
-        in_specs=[vmem] * (sources + 3),
+        in_specs=[vmem] * (sources + 2),
         out_specs=(vmem, vmem, pl.BlockSpec(memory_space=pltpu.SMEM)),
         scratch_shapes=[
             pltpu.VMEM((sources, lines, row_len), jnp.float32),
@@ -431,18 +436,29 @@
         ],
         compiler_params=pltpu.CompilerParams(vmem_limit_bytes=40 * 1024 * 1024),
         name="bin_modes",
-    )(*recv, pick, jnp.asarray(high), jnp.asarray(low))
-
-
-def legendre_kernel(me_ref, recv_ref, table_ref, *refs, owners):
+    )(*recv, pick, mode_table)
+
+
+def legendre_kernel(me_ref, order_ref, recv_ref, table_ref, *refs, owners):
     out_refs, (leg_ref, arrived, modes_ref, wide_ref, sums_ref) = refs[:owners], refs[owners:]
     slots, band_cycles, degrees = table_ref.shape
 
-    def load(slot):
-        return pltpu.make_async_copy(table_ref.at[slot], leg_ref.at[slot], arrived.at[slot])
+    def load(slot, act):
+        skip = order_ref[slot] >= LANES
+
+        @pl.when(skip)
+        def _():
+            upper = pl.ds(LANES, degrees - LANES)
+            act(pltpu.make_async_copy(
+                table_ref.at[slot, :, upper], leg_ref.at[slot, :, upper], arrived.at[slot]
+            ))
+
+        @pl.when(jnp.logical_not(skip))
+        def _():
+            act(pltpu.make_async_copy(table_ref.at[slot], leg_ref.at[slot], arrived.at[slot]))
 
     def start(slot, carry):
-        load(slot).start()
+        load(slot, lambda copy: copy.start())
         return carry
 
     lax.fori_loop(0, slots, start, 0)
@@ -467,7 +483,7 @@
 
     def body(slot, carry):
         half = slot & 1
-        load(slot).wait()
+        load(slot, lambda copy: copy.wait())
         sums = [[jnp.zeros((SUB, LANES), jnp.float32) for _ in range(tiles)] for _ in range(2)]
         for r in range(0, band_cycles, SUB):
             factor = [wide_ref[half, c, r:r + SUB, :] for c in range(2)]
@@ -489,13 +505,13 @@
         out_refs[k][...] = sums_ref[me_ref[0] ^ k]
 
 
-def legendre_sums(me, recv, legendre, owners):
+def legendre_sums(me, orders, recv, legendre, owners):
     slots, band_cycles, degrees = legendre.shape
     vmem = pl.BlockSpec(memory_space=pltpu.VMEM)
     return pl.pallas_call(
         functools.partial(legendre_kernel, owners=owners),
         out_shape=(jax.ShapeDtypeStruct((2 * slots, degrees // owners), jnp.float32),) * owners,
-        in_specs=[pl.BlockSpec(memory_space=pltpu.SMEM), vmem, pl.BlockSpec(memory_space=pl.ANY)],
+        in_specs=[pl.BlockSpec(memory_space=pltpu.SMEM)] * 2 + [vmem, pl.BlockSpec(memory_space=pl.ANY)],
         out_specs=(vmem,) * owners,
         scratch_shapes=[
             pltpu.VMEM(legendre.shape, jnp.float32),
@@ -506,7 +522,7 @@
         ],
         compiler_params=pltpu.CompilerParams(vmem_limit_bytes=44 * 1024 * 1024),
         name="legendre_sums",
-    )(me, recv, legendre)
+    )(me, orders, recv, legendre)
 
 
 def exchange_and_sum(x, axis, count):
@@ -536,7 +552,7 @@
     return (out / length).reshape(lines, length)
 
 
-def dense_path(table, scan_lines, response, cycle_offset, column, order_slot, band_cycles, det_count):
+def dense_path(table, mode_table, scan_lines, response, cycle_offset, column, order_slot, band_cycles, det_count):
     filtered = dense_filter(table, scan_lines, response)
     flat_index = (cycle_offset * NPHI + column).reshape(-1)
     empty = jnp.zeros((band_cycles * NPHI,), jnp.float32)
@@ -545,12 +561,15 @@
     summed = exchange_and_sum(partial_value, "det", det_count)
     hit_total = exchange_and_sum(counts, "det", det_count)
     sky_map = summed / jnp.maximum(hit_total, 1.0)
-    pixel_index = jnp.arange(NPHI, dtype=jnp.int32)[:, None]
-    phases = 2.0 * jnp.pi / NPHI * (pixel_index * order_slot[None, :] % NPHI).astype(jnp.float32)
-    modes = jnp.stack([
-        jnp.dot(sky_map, jnp.cos(phases), precision=precise),
-        -jnp.dot(sky_map, jnp.sin(phases), precision=precise),
-    ])
+    count, half = order_slot.shape[0], NPHI // 2
+    tables = jnp.sum(mode_table.astype(jnp.float32), axis=0)
+    first, second = sky_map[:, :half], sky_map[:, half:]
+    modes = jnp.concatenate([
+        jnp.dot(first + second, tables[0], precision=precise),
+        jnp.dot(first - second, tables[1], precision=precise),
+    ], axis=1)
+    part = jnp.arange(2, dtype=jnp.int32)[:, None] * (count // 2)
+    modes = modes[:, (order_slot & 1) * count + part + (order_slot >> 1)].transpose(1, 0, 2)
     slots = order_slot.shape[0] // det_count
     groups = LANES // (2 * slots)
     blocks = modes.reshape(2, groups, -1, det_count, slots).transpose(3, 2, 1, 0, 4)
@@ -570,23 +589,24 @@
     slots, band_cycles, degrees = legendre.shape
     me = lax.axis_index("det").astype(jnp.int32).reshape(1)
     table = jnp.asarray(filter_tables(scan_lines.shape[1]))
-    send = filter_and_sort(
-        me, table, scan_lines, response, cycle_offset, column, det_count, band_cycles
+    mode_table = jnp.asarray(mode_tables(order_slot.shape[0]))
+    *send, mode_copy = filter_and_sort(
+        me, table, mode_table, scan_lines, response, cycle_offset, column, det_count, band_cycles
     )
     recv = swap_blocks(send, "det")
-    sky_map, modes, crowded = bin_and_modes(recv[::-1], order_slot, band_cycles)
+    sky_map, modes, crowded = bin_and_modes(mode_copy, recv[::-1], order_slot, band_cycles)
     modes = lax.all_to_all(modes, "det", split_axis=0, concat_axis=0, tiled=True)
     sky_map, modes = lax.cond(
         crowded[0] > 0,
         lambda: dense_path(
-            table, scan_lines, response, cycle_offset, column, order_slot, band_cycles, det_count
+            table, mode_table, scan_lines, response, cycle_offset, column, order_slot, band_cycles, det_count
         ),
         lambda: (sky_map, modes),
     )
     band = lax.axis_index("band").astype(jnp.int32)
-    terms = swap_blocks(legendre_sums(band.reshape(1), modes, legendre, band_count), "band")
-    sums = functools.reduce(jnp.add, terms)
     local_orders = lax.dynamic_slice_in_dim(order_slot, lax.axis_index("det") * slots, slots, 0)
+    terms = swap_blocks(legendre_sums(band.reshape(1), local_orders, modes, legendre, band_count), "band")
+    sums = functools.reduce(jnp.add, terms[::-1])
     width = degrees // band_count
     degree = band * width + jnp.arange(width, dtype=jnp.int32)
     keep = degree[None, None, :] >= local_orders[None, :, None]

time: 65.2 us -> 61.9 us (0.949)
  local copies, waits for them, and re-layouts: 2.81 us -> 0.36 us
  other arithmetic: 1.49 us -> 0.81 us
    unnamed x16 -> x12, local copies, waits for them, and re-layouts: 2.48 us -> 0.03 us
    mul x2, other arithmetic: 0.68 us -> 0.01 us  [bin_and_modes(): pick = (m & 1) * count + part * (count // 2) + (m >> 1)]
  transfers between devices with their start and end apart: 11 -> 11, of which waited for: 8 -> 8; matrix products, arithmetic and copies ran while one was open for 2% -> 1% of each run, Pallas kernels for 0% -> 0%
where the time goes in v9:
time: 61.9 us; the launch traced here: 61.7 us
  Pallas kernels  28.6 us (46%)
  starting transfers between devices  17.7 us (29%)
  waiting for transfers between devices  12.6 us (20%)
  between operations  1.46 us (2%)
  other arithmetic  0.81 us (1%)
    ppermute x10, starting transfers between devices, swap_blocks(): out[k] = lax.ppermute(blocks[k], axis, [(i, i ^ k) for i in range(count)])  13.1 us
    pallas_call x1, Pallas kernels, legendre_sums(): pl.pallas_call(functools.partial(legendre_kernel, owners=owners), out_sha...  11.2 us
    pallas_call x1, Pallas kernels, bin_and_modes(): pl.pallas_call(functools.partial(bin_kernel, sources=sources, windows=win...  9.66 us
    pallas_call x1, Pallas kernels, filter_and_sort(): pl.pallas_call(body, out_shape=(jax.ShapeDtypeStruct((2 * windows * rows,...  7.78 us
    ppermute x10, waiting for transfers between devices, swap_blocks(): out[k] = lax.ppermute(blocks[k], axis, [(i, i ^ k) for i in range(count)])  7.41 us
    all_to_all x1, waiting for transfers between devices, local(): lax.all_to_all(modes, 'det', split_axis=0, concat_axis=0, tiled=True)  5.14 us
    all_to_all x1, starting transfers between devices, local(): lax.all_to_all(modes, 'det', split_axis=0, concat_axis=0, tiled=True)  4.51 us
  transfers between devices with their start and end apart: 11, of which 8 were waited for; matrix products, arithmetic and copies ran while one was open for 1% of the time, Pallas kernels for 0%

profile of v9, /device:TPU:0, one launch (start us, length us, event | category | flops | bytes accessed | tf_op | source)
XLA Modules:
  0.0 61.7 jit_solution(15572045311254455794)
XLA Ops:
  0.7 7.8 %filter_sort.1 = (f32[40,256]{1,0:T(8,128)S(1)}, f32[40,256]{1,0:T(8,128)S(1)}, f32[40,256]{1,0:T(8,128)S(1)}, f32[40,256]{1,0:T(8,128)S(1)}, f32[40,256]{1,0:T(...) custom-call(s32[1]{0:T(128)} %bitcast.16.me_ref, ...), custom_call_target="tpu_custom_call" | custom-call | tf_op jit(solution)/shard_map/filter_sort/pallas_call | solution.py:277
  8.5 4.6 %collective-permute-start = (f32[40,256]{1,0:T(8,128)S(1)}, f32[40,256]{1,0:T(8,128)S(1)}, u32[]{:S(2)}, u32[]{:S(2)}) collective-permute-start(f32[40,256]{1,0:T(8,128)S(1)} %get-tuple-element.45), channel_id=1, source_target_pairs={{0,28},{4,24},{8,20},{12,16},{16,12},{20,8},{24,4},{28,0},{1,29},{... | collective-permute-start | bytes 122888 | tf_op jit(solution)/shard_map/ppermute | solution.py:584
  13.0 0.6 %collective-permute-start.1 = (f32[40,256]{1,0:T(8,128)S(1)}, f32[40,256]{1,0:T(8,128)S(1)}, u32[]{:S(2)}, u32[]{:S(2)}) collective-permute-start(f32[40,256]{1,0:T(8,128)S(1)} %get-tuple-element.46), channel_id=1, source_target_pairs={{0,24},{4,28},{8,16},{12,20},{16,8},{20,12},{24,0},{28,4},{1,25},{... | collective-permute-start | bytes 122888 | tf_op jit(solution)/shard_map/ppermute | solution.py:584
  13.7 0.4 collective-permute-start.2
  14.1 2.2 %collective-permute-start.3 = (f32[40,256]{1,0:T(8,128)S(1)}, f32[40,256]{1,0:T(8,128)S(1)}, u32[]{:S(2)}, u32[]{:S(2)}) collective-permute-start(f32[40,256]{1,0:T(8,128)S(1)} %get-tuple-element.48), channel_id=1, source_target_pairs={{0,16},{4,20},{8,24},{12,28},{16,0},{20,4},{24,8},{28,12},{1,17},{... | collective-permute-start | bytes 122888 | tf_op jit(solution)/shard_map/ppermute | solution.py:584
  16.3 1.0 %collective-permute-start.4 = (f32[40,256]{1,0:T(8,128)S(1)}, f32[40,256]{1,0:T(8,128)S(1)}, u32[]{:S(2)}, u32[]{:S(2)}) collective-permute-start(f32[40,256]{1,0:T(8,128)S(1)} %get-tuple-element.49), channel_id=1, source_target_pairs={{0,12},{4,8},{8,4},{12,0},{16,28},{20,24},{24,20},{28,16},{1,13},{... | collective-permute-start | bytes 122888 | tf_op jit(solution)/shard_map/ppermute | solution.py:584
  17.4 0.9 %collective-permute-start.5 = (f32[40,256]{1,0:T(8,128)S(1)}, f32[40,256]{1,0:T(8,128)S(1)}, u32[]{:S(2)}, u32[]{:S(2)}) collective-permute-start(f32[40,256]{1,0:T(8,128)S(1)} %get-tuple-element.50), channel_id=1, source_target_pairs={{0,8},{4,12},{8,0},{12,4},{16,24},{20,28},{24,16},{28,20},{1,9},{5... | collective-permute-start | bytes 122888 | tf_op jit(solution)/shard_map/ppermute | solution.py:584
  18.2 1.1 %collective-permute-done.1.refs_1_ = f32[40,256]{1,0:T(8,128)S(1)} collective-permute-done((f32[40,256]{1,0:T(8,128)S(1)}, f32[40,256]{1,0:T(8,128)S(1)}, u32[]{:S(2)}, u32[]{:S(2)}) %collective-permute-start.1) | collective-permute-done | bytes 40992 | tf_op jit(solution)/shard_map/ppermute | solution.py:584
  19.5 0.1 reshape.230.refs_8_
  19.6 0.5 collective-permute-done.2.refs_2_
  20.1 1.9 %collective-permute-done.3.refs_3_ = f32[40,256]{1,0:T(8,128)S(1)} collective-permute-done((f32[40,256]{1,0:T(8,128)S(1)}, f32[40,256]{1,0:T(8,128)S(1)}, u32[]{:S(2)}, u32[]{:S(2)}) %collective-permute-start.3) | collective-permute-done | bytes 40992 | tf_op jit(solution)/shard_map/ppermute | solution.py:584
  22.0 0.2 collective-permute-done.5.refs_5_
  22.2 9.7 %bin_modes.1 = (f32[32,2048]{1,0:T(8,128)}, f32[8,16,128]{2,1,0:T(8,128)}, s32[1]{0:T(128)}) custom-call(f32[40,256]{1,0:T(8,128)S(1)} %collective-permute-done.refs_0_, f32[40,256]{1,0:T(8,128)S(1)} %collective-permute-done.1.refs_1_, f32[40,256]{1,0:T(8,128)S(1)} %collective-permute-done.2.refs_2_, f32[40,256]{1,0:T(8,128)S(1)} %collective-permute-done.3.refs_3_, ...), custom_call_target="tpu_custom_call" | custom-call | tf_op jit(solution)/shard_map/bin_modes/pallas_call | solution.py:420
  31.9 4.5 %all-to-all-start.3 = ((f32[8,16,128]{2,1,0:T(8,128)}), f32[8,16,128]{2,1,0:T(8,128)S(1)}, u32[]{:S(2)}, u32[]{:S(2)}) async-start(f32[8,16,128]{2,1,0:T(8,128)} %get-tuple-element.56), calls=%async_computation.3 | async-start | bytes 131072 | tf_op jit(solution)/shard_map/all_to_all | solution.py:598
  37.1 5.1 %all-to-all-done.3 = f32[8,16,128]{2,1,0:T(8,128)S(1)} async-done(((f32[8,16,128]{2,1,0:T(8,128)}), f32[8,16,128]{2,1,0:T(8,128)S(1)}, u32[]{:S(2)}, u32[]{:S(2)}) %all-to-all-start.3) | async-done | bytes 65568 | tf_op jit(solution)/shard_map/all_to_all | solution.py:598
  42.3 0.2 conditional.1
  42.5 11.2 %legendre_sums.1 = (f32[64,256]{1,0:T(8,128)S(1)}, f32[64,256]{1,0:T(8,128)S(1)}, f32[64,256]{1,0:T(8,128)S(1)}, f32[64,256]{1,0:T(8,128)S(1)}) custom-call(s32[1]{0:T(128)} %bitcast.15.me_ref, s32[32]{0:T(128)S(1)} %dynamic_slice.3.order_ref, f32[8,16,128]{2,1,0:T(8,128)S(1)} %get-tuple-element.57.recv_ref, f32[32,256,1024]{2,1,0:T(8,128)} %table_ref.1), custom_call_target="tpu_custom_call" | custom-call | tf_op jit(solution)/shard_map/legendre_sums/pallas_call | solution.py:511
  53.7 2.5 %collective-permute-start.7 = (f32[64,256]{1,0:T(8,128)S(1)}, f32[64,256]{1,0:T(8,128)S(1)}, u32[]{:S(2)}, u32[]{:S(2)}) collective-permute-start(f32[64,256]{1,0:T(8,128)S(1)} %get-tuple-element.58), channel_id=1, source_target_pairs={{0,3},{1,2},{2,1},{3,0},{4,7},{5,6},{6,5},{7,4},{8,11},{9,10},{10,... | collective-permute-start | bytes 196616 | tf_op jit(solution)/shard_map/ppermute | solution.py:584
  56.3 0.5 collective-permute-start.8
  56.8 0.5 collective-permute-start.9
  57.4 1.7 %collective-permute-done.7 = f32[64,256]{1,0:T(8,128)S(1)} collective-permute-done((f32[64,256]{1,0:T(8,128)S(1)}, f32[64,256]{1,0:T(8,128)S(1)}, u32[]{:S(2)}, u32[]{:S(2)}) %collective-permute-start.7) | collective-permute-done | bytes 65568 | tf_op jit(solution)/shard_map/ppermute | solution.py:584
  59.1 1.4 %collective-permute-done.8 = f32[64,256]{1,0:T(8,128)S(1)} collective-permute-done((f32[64,256]{1,0:T(8,128)S(1)}, f32[64,256]{1,0:T(8,128)S(1)}, u32[]{:S(2)}, u32[]{:S(2)}) %collective-permute-start.8) | collective-permute-done | bytes 65568 | tf_op jit(solution)/shard_map/ppermute | solution.py:584
  60.5 0.5 collective-permute-done.9
  61.0 0.6 %broadcast_select_fusion = f32[2,32,256]{2,1,0:T(8,128)} fusion(f32[2,32,256]{2,1,0:T(8,128)S(1)} %bitcast.57, pred[32,256]{1,0:T(8,128)(4,1)S(1)} %broadcast_compare_fusion), kind=kLoop, calls=%fused_computation.93 | loop fusion | flops 16384 | bytes 139264 | tf_op jit(solution)/shard_map/jit(_where)/select_n | solution.py:613
  (26 shorter events, 0.4 us)
Async XLA Ops:
  0.6 16.6 %copy-start.7 = (s32[256]{0:T(256)S(1)}, s32[256]{0:T(256)}, u32[]{:S(2)}) copy-start(s32[256]{0:T(256)} %param.14) | copy-start | bytes 3076
  0.6 41.6 %copy-start.1 = (f32[288,256]{1,0:T(8,128)S(1)}, f32[288,256]{1,0:T(8,128)}, u32[]{:S(2)}) copy-start(f32[288,256]{1,0:T(8,128)} %constant.68.clone.table_hbm) | copy-start | bytes 884740
  0.7 41.6 %copy-start.2 = (f32[8,4096]{1,0:T(8,128)S(1)}, f32[8,4096]{1,0:T(8,128)}, u32[]{:S(2)}) copy-start(f32[8,4096]{1,0:T(8,128)} %scan_hbm.1) | copy-start | bytes 393220
  0.7 41.6 %copy-start.3 = (f32[8,4096]{1,0:T(8,128)S(1)}, f32[8,4096]{1,0:T(8,128)}, u32[]{:S(2)}) copy-start(f32[8,4096]{1,0:T(8,128)} %resp_hbm.1) | copy-start | bytes 393220
  0.7 41.6 %copy-start.4 = (s32[8,4096]{1,0:T(8,128)S(1)}, s32[8,4096]{1,0:T(8,128)}, u32[]{:S(2)}) copy-start(s32[8,4096]{1,0:T(8,128)} %cycle_hbm.1) | copy-start | bytes 393220
  0.7 41.6 %copy-start.5 = (s32[8,4096]{1,0:T(8,128)S(1)}, s32[8,4096]{1,0:T(8,128)}, u32[]{:S(2)}) copy-start(s32[8,4096]{1,0:T(8,128)} %column_hbm.1) | copy-start | bytes 393220
  8.5 8.9 %collective-permute-start = (f32[40,256]{1,0:T(8,128)S(1)}, f32[40,256]{1,0:T(8,128)S(1)}, u32[]{:S(2)}, u32[]{:S(2)}) collective-permute-start(f32[40,256]{1,0:T(8,128)S(1)} %get-tuple-element.45), channel_id=1, source_target_pairs={{0,28},{4,24},{8,20},{12,16},{16,12},{20,8},{24,4},{28,0},{1,29},{... | collective-permute-start | bytes 122888 | tf_op jit(solution)/shard_map/ppermute | solution.py:584
  13.0 6.3 %collective-permute-start.1 = (f32[40,256]{1,0:T(8,128)S(1)}, f32[40,256]{1,0:T(8,128)S(1)}, u32[]{:S(2)}, u32[]{:S(2)}) collective-permute-start(f32[40,256]{1,0:T(8,128)S(1)} %get-tuple-element.46), channel_id=1, source_target_pairs={{0,24},{4,28},{8,16},{12,20},{16,8},{20,12},{24,0},{28,4},{1,25},{... | collective-permute-start | bytes 122888 | tf_op jit(solution)/shard_map/ppermute | solution.py:584
  13.7 6.4 %collective-permute-start.2 = (f32[40,256]{1,0:T(8,128)S(1)}, f32[40,256]{1,0:T(8,128)S(1)}, u32[]{:S(2)}, u32[]{:S(2)}) collective-permute-start(f32[40,256]{1,0:T(8,128)S(1)} %get-tuple-element.47), channel_id=1, source_target_pairs={{0,20},{4,16},{8,28},{12,24},{16,4},{20,0},{24,12},{28,8},{1,21},{... | collective-permute-start | bytes 122888 | tf_op jit(solution)/shard_map/ppermute | solution.py:584
  14.1 7.9 %collective-permute-start.3 = (f32[40,256]{1,0:T(8,128)S(1)}, f32[40,256]{1,0:T(8,128)S(1)}, u32[]{:S(2)}, u32[]{:S(2)}) collective-permute-start(f32[40,256]{1,0:T(8,128)S(1)} %get-tuple-element.48), channel_id=1, source_target_pairs={{0,16},{4,20},{8,24},{12,28},{16,0},{20,4},{24,8},{28,12},{1,17},{... | collective-permute-start | bytes 122888 | tf_op jit(solution)/shard_map/ppermute | solution.py:584
  16.3 5.7 %collective-permute-start.4 = (f32[40,256]{1,0:T(8,128)S(1)}, f32[40,256]{1,0:T(8,128)S(1)}, u32[]{:S(2)}, u32[]{:S(2)}) collective-permute-start(f32[40,256]{1,0:T(8,128)S(1)} %get-tuple-element.49), channel_id=1, source_target_pairs={{0,12},{4,8},{8,4},{12,0},{16,28},{20,24},{24,20},{28,16},{1,13},{... | collective-permute-start | bytes 122888 | tf_op jit(solution)/shard_map/ppermute | solution.py:584
  17.4 4.8 %collective-permute-start.5 = (f32[40,256]{1,0:T(8,128)S(1)}, f32[40,256]{1,0:T(8,128)S(1)}, u32[]{:S(2)}, u32[]{:S(2)}) collective-permute-start(f32[40,256]{1,0:T(8,128)S(1)} %get-tuple-element.50), channel_id=1, source_target_pairs={{0,8},{4,12},{8,0},{12,4},{16,24},{20,28},{24,16},{28,20},{1,9},{5... | collective-permute-start | bytes 122888 | tf_op jit(solution)/shard_map/ppermute | solution.py:584
  19.4 2.8 %collective-permute-start.6 = (f32[40,256]{1,0:T(8,128)S(1)}, f32[40,256]{1,0:T(8,128)S(1)}, u32[]{:S(2)}, u32[]{:S(2)}) collective-permute-start(f32[40,256]{1,0:T(8,128)S(1)} %get-tuple-element.51), channel_id=1, source_target_pairs={{0,4},{4,0},{8,12},{12,8},{16,20},{20,16},{24,28},{28,24},{1,5},{5... | collective-permute-start | bytes 122888 | tf_op jit(solution)/shard_map/ppermute | solution.py:584
  31.9 10.4 %all-to-all-start.3 = ((f32[8,16,128]{2,1,0:T(8,128)}), f32[8,16,128]{2,1,0:T(8,128)S(1)}, u32[]{:S(2)}, u32[]{:S(2)}) async-start(f32[8,16,128]{2,1,0:T(8,128)} %get-tuple-element.56), calls=%async_computation.3 | async-start | bytes 131072 | tf_op jit(solution)/shard_map/all_to_all | solution.py:598
  53.7 5.3 %collective-permute-start.7 = (f32[64,256]{1,0:T(8,128)S(1)}, f32[64,256]{1,0:T(8,128)S(1)}, u32[]{:S(2)}, u32[]{:S(2)}) collective-permute-start(f32[64,256]{1,0:T(8,128)S(1)} %get-tuple-element.58), channel_id=1, source_target_pairs={{0,3},{1,2},{2,1},{3,0},{4,7},{5,6},{6,5},{7,4},{8,11},{9,10},{10,... | collective-permute-start | bytes 196616 | tf_op jit(solution)/shard_map/ppermute | solution.py:584
  56.3 4.3 %collective-permute-start.8 = (f32[64,256]{1,0:T(8,128)S(1)}, f32[64,256]{1,0:T(8,128)S(1)}, u32[]{:S(2)}, u32[]{:S(2)}) collective-permute-start(f32[64,256]{1,0:T(8,128)S(1)} %get-tuple-element.59), channel_id=1, source_target_pairs={{0,2},{1,3},{2,0},{3,1},{4,6},{5,7},{6,4},{7,5},{8,10},{9,11},{10,... | collective-permute-start | bytes 196616 | tf_op jit(solution)/shard_map/ppermute | solution.py:584
  56.8 4.3 %collective-permute-start.9 = (f32[64,256]{1,0:T(8,128)S(1)}, f32[64,256]{1,0:T(8,128)S(1)}, u32[]{:S(2)}, u32[]{:S(2)}) collective-permute-start(f32[64,256]{1,0:T(8,128)S(1)} %get-tuple-element.60), channel_id=1, source_target_pairs={{0,1},{1,0},{2,3},{3,2},{4,5},{5,4},{6,7},{7,6},{8,9},{9,8},{10,11... | collective-permute-start | bytes 196616 | tf_op jit(solution)/shard_map/ppermute | solution.py:584

commit v10 on v9

--- a/solution.py
+++ b/solution.py
@@ -12,6 +12,7 @@
 LANES = 128
 SUB = 8
 WINDOWS = 2
+HEAD = 2
 ROW = 256
 PIECE, PIECES, STEP, TOP = jnp.float8_e4m3fn, 3, 32.0, 224.0
 KEEP = 2.0**20 + 1.0
@@ -161,6 +162,17 @@
     assert places.of == list(range(places.total_bits))
 
 
+def split2(x):
+    high = x.astype(jnp.bfloat16)
+    low = (x - high.astype(jnp.float32)).astype(jnp.bfloat16)
+    return high, low
+
+
+def three_products(left, right, dims):
+    dot = functools.partial(lax.dot_general, dimension_numbers=dims, preferred_element_type=jnp.float32)
+    return dot(left[0], right[0]) + (dot(left[1], right[0]) + dot(left[0], right[1]))
+
+
 def sort_kernel(
     me_ref, scan_hbm, resp_hbm, cycle_hbm, column_hbm, table_hbm, modes_hbm, *refs,
     buckets, span, rows, windows,
@@ -195,7 +207,8 @@
         spec_ref[here, LANES:] = im[k] * c - re[k] * s
     for load in loads[2:-1]:
         load.wait()
-    spec = jnp.dot(spec_ref[...], forward, precision=precise, preferred_element_type=jnp.float32)
+    forward_pieces = split2(forward)
+    spec = three_products(split2(spec_ref[...]), forward_pieces, (((1,), (0,)), ((), ())))
     resp = [resp_ref[:, n * LANES:(n + 1) * LANES] * (1.0 / length) for n in range(outer)]
     step = 1
     while step < outer:
@@ -206,9 +219,7 @@
         step *= 2
     resp = jnp.concatenate(resp, axis=0)
     spec = spec * jnp.concatenate([resp, resp], axis=1)
-    spec_ref[...] = lax.dot_general(
-        spec, forward, NT, precision=precise, preferred_element_type=jnp.float32
-    )
+    spec_ref[...] = three_products(split2(spec), forward_pieces, NT)
     re, im = [], []
     for k in range(outer):
         c, s = twiddle_row(k)
@@ -294,17 +305,15 @@
     )(me, *operands, mode_table)
 
 
-def split2(x):
-    high = x.astype(jnp.bfloat16)
-    low = (x - high.astype(jnp.float32)).astype(jnp.bfloat16)
-    return high, low
-
-
 def bin_kernel(
     *refs, sources, windows, rows, window_cycles
 ):
-    recv_refs, (pick_ref, table_ref, map_ref, send_ref, flag_ref) = refs[:sources], refs[sources:-6]
-    recv_ref, left_a, left_b, right_a, right_b, acc_ref = refs[-6:]
+    recv_refs, (pick_ref, table_ref, leg_hbm, map_ref, send_ref, flag_ref, head_ref) = (
+        refs[:sources], refs[sources:-7]
+    )
+    recv_ref, left_a, left_b, right_a, right_b, acc_ref, arrived = refs[-7:]
+    head_load = pltpu.make_async_copy(leg_hbm.at[pl.ds(0, head_ref.shape[0])], head_ref, arrived)
+    head_load.start()
     for e in range(sources):
         recv_ref[e] = recv_refs[e][...]
     left_refs, right_refs = (left_a, left_b), (right_a, right_b)
@@ -399,9 +408,10 @@
         for h in range(1, groups):
             out = jnp.where(lane_group == h, block[h * group_rows:(h + 1) * group_rows], out)
         send_ref[d] = out
-
-
-def bin_and_modes(mode_table, recv, order_slot, band_cycles):
+    head_load.wait()
+
+
+def bin_and_modes(mode_table, legendre, recv, order_slot, band_cycles):
     sources = len(recv)
     lines, row_len = recv[0].shape
     windows = WINDOWS
@@ -423,9 +433,10 @@
             jax.ShapeDtypeStruct((cycles, NPHI), jnp.float32),
             jax.ShapeDtypeStruct((sources, cycles // groups, LANES), jnp.float32),
             jax.ShapeDtypeStruct((1,), jnp.int32),
+            jax.ShapeDtypeStruct((HEAD,) + legendre.shape[1:], jnp.float32),
         ),
-        in_specs=[vmem] * (sources + 2),
-        out_specs=(vmem, vmem, pl.BlockSpec(memory_space=pltpu.SMEM)),
+        in_specs=[vmem] * (sources + 2) + [pl.BlockSpec(memory_space=pl.ANY)],
+        out_specs=(vmem, vmem, pl.BlockSpec(memory_space=pltpu.SMEM), vmem),
         scratch_shapes=[
             pltpu.VMEM((sources, lines, row_len), jnp.float32),
             pltpu.VMEM(((PIECES + 1) * area, depth), PIECE),
@@ -433,13 +444,14 @@
             pltpu.VMEM((ROW, depth), PIECE),
             pltpu.VMEM((ROW, depth), PIECE),
             pltpu.VMEM(((PIECES + 1) * area, ROW), jnp.float32),
+            pltpu.SemaphoreType.DMA,
         ],
         compiler_params=pltpu.CompilerParams(vmem_limit_bytes=40 * 1024 * 1024),
         name="bin_modes",
-    )(*recv, pick, mode_table)
-
-
-def legendre_kernel(me_ref, order_ref, recv_ref, table_ref, *refs, owners):
+    )(*recv, pick, mode_table, legendre)
+
+
+def legendre_kernel(me_ref, order_ref, recv_ref, head_ref, table_ref, *refs, owners):
     out_refs, (leg_ref, arrived, modes_ref, wide_ref, sums_ref) = refs[:owners], refs[owners:]
     slots, band_cycles, degrees = table_ref.shape
 
@@ -461,7 +473,7 @@
         load(slot, lambda copy: copy.start())
         return carry
 
-    lax.fori_loop(0, slots, start, 0)
+    lax.fori_loop(HEAD, slots, start, 0)
     sources, group_rows, lanes = recv_ref.shape
     groups = lanes // (2 * slots)
     width = out_refs[0].shape[1]
@@ -481,14 +493,15 @@
 
     widen(0, 0)
 
-    def body(slot, carry):
+    def body(source_ref, slot, carry):
         half = slot & 1
-        load(slot, lambda copy: copy.wait())
+        if source_ref is leg_ref:
+            load(slot, lambda copy: copy.wait())
         sums = [[jnp.zeros((SUB, LANES), jnp.float32) for _ in range(tiles)] for _ in range(2)]
         for r in range(0, band_cycles, SUB):
             factor = [wide_ref[half, c, r:r + SUB, :] for c in range(2)]
             for t in range(tiles):
-                block = leg_ref[slot, r:r + SUB, t * LANES:(t + 1) * LANES]
+                block = source_ref[slot, r:r + SUB, t * LANES:(t + 1) * LANES]
                 for c in range(2):
                     sums[c][t] = sums[c][t] + block * factor[c]
         widen(jnp.minimum(slot + 1, slots - 1), 1 - half)
@@ -500,18 +513,19 @@
                 sums_ref[d, pl.ds(c * slots + slot, 1), :] = line
         return carry
 
-    lax.fori_loop(0, slots, body, 0)
+    lax.fori_loop(0, HEAD, functools.partial(body, head_ref), 0)
+    lax.fori_loop(HEAD, slots, functools.partial(body, leg_ref), 0)
     for k in range(owners):
         out_refs[k][...] = sums_ref[me_ref[0] ^ k]
 
 
-def legendre_sums(me, orders, recv, legendre, owners):
+def legendre_sums(me, orders, recv, head, legendre, owners):
     slots, band_cycles, degrees = legendre.shape
     vmem = pl.BlockSpec(memory_space=pltpu.VMEM)
     return pl.pallas_call(
         functools.partial(legendre_kernel, owners=owners),
         out_shape=(jax.ShapeDtypeStruct((2 * slots, degrees // owners), jnp.float32),) * owners,
-        in_specs=[pl.BlockSpec(memory_space=pltpu.SMEM)] * 2 + [vmem, pl.BlockSpec(memory_space=pl.ANY)],
+        in_specs=[pl.BlockSpec(memory_space=pltpu.SMEM)] * 2 + [vmem, vmem, pl.BlockSpec(memory_space=pl.ANY)],
         out_specs=(vmem,) * owners,
         scratch_shapes=[
             pltpu.VMEM(legendre.shape, jnp.float32),
@@ -522,7 +536,7 @@
         ],
         compiler_params=pltpu.CompilerParams(vmem_limit_bytes=44 * 1024 * 1024),
         name="legendre_sums",
-    )(me, orders, recv, legendre)
+    )(me, orders, recv, head, legendre)
 
 
 def exchange_and_sum(x, axis, count):
@@ -594,7 +608,7 @@
         me, table, mode_table, scan_lines, response, cycle_offset, column, det_count, band_cycles
     )
     recv = swap_blocks(send, "det")
-    sky_map, modes, crowded = bin_and_modes(mode_copy, recv[::-1], order_slot, band_cycles)
+    sky_map, modes, crowded, head = bin_and_modes(mode_copy, legendre, recv[::-1], order_slot, band_cycles)
     modes = lax.all_to_all(modes, "det", split_axis=0, concat_axis=0, tiled=True)
     sky_map, modes = lax.cond(
         crowded[0] > 0,
@@ -605,7 +619,8 @@
     )
     band = lax.axis_index("band").astype(jnp.int32)
     local_orders = lax.dynamic_slice_in_dim(order_slot, lax.axis_index("det") * slots, slots, 0)
-    terms = swap_blocks(legendre_sums(band.reshape(1), local_orders, modes, legendre, band_count), "band")
+    terms = legendre_sums(band.reshape(1), local_orders, modes, head, legendre, band_count)
+    terms = swap_blocks(terms, "band")
     sums = functools.reduce(jnp.add, terms[::-1])
     width = degrees // band_count
     degree = band * width + jnp.arange(width, dtype=jnp.int32)

time: 61.9 us -> 63.8 us (1.031)
  local copies, waits for them, and re-layouts: 0.36 us -> 3.27 us
  Pallas kernels: 28.6 us -> 27.8 us
    unnamed x12, local copies, waits for them, and re-layouts: 0.03 us -> 2.94 us
  transfers between devices with their start and end apart: 11 -> 11, of which waited for: 8 -> 7; matrix products, arithmetic and copies ran while one was open for 1% -> 1% of each run, Pallas kernels for 0% -> 0%
where the time goes in v10:
time: 63.8 us; the launch traced here: 63.6 us
  Pallas kernels  27.8 us (44%)
  starting transfers between devices  17.6 us (28%)
  waiting for transfers between devices  12.5 us (20%)
  local copies, waits for them, and re-layouts  3.27 us (5%)
  between operations  1.41 us (2%)
  other arithmetic  0.81 us (1%)
    ppermute x10, starting transfers between devices, swap_blocks(): out[k] = lax.ppermute(blocks[k], axis, [(i, i ^ k) for i in range(count)])  13 us
    pallas_call x1, Pallas kernels, legendre_sums(): pl.pallas_call(functools.partial(legendre_kernel, owners=owners), out_sha...  10.7 us
    pallas_call x1, Pallas kernels, bin_and_modes(): pl.pallas_call(functools.partial(bin_kernel, sources=sources, windows=win...  9.75 us
    ppermute x10, waiting for transfers between devices, swap_blocks(): out[k] = lax.ppermute(blocks[k], axis, [(i, i ^ k) for i in range(count)])  7.4 us
    pallas_call x1, Pallas kernels, filter_and_sort(): pl.pallas_call(body, out_shape=(jax.ShapeDtypeStruct((2 * windows * rows,...  7.3 us
    all_to_all x1, waiting for transfers between devices, local(): lax.all_to_all(modes, 'det', split_axis=0, concat_axis=0, tiled=True)  5.15 us
    all_to_all x1, starting transfers between devices, local(): lax.all_to_all(modes, 'det', split_axis=0, concat_axis=0, tiled=True)  4.56 us
    unnamed x12, local copies, waits for them, and re-layouts  2.94 us
  transfers between devices with their start and end apart: 11, of which 7 were waited for; matrix products, arithmetic and copies ran while one was open for 1% of the time, Pallas kernels for 0%

profile of v10, /device:TPU:0, one launch (start us, length us, event | category | flops | bytes accessed | tf_op | source)
XLA Modules:
  0.0 63.6 jit_solution(2044200257295471966)
XLA Ops:
  0.6 7.3 %filter_sort.1 = (f32[40,256]{1,0:T(8,128)S(1)}, f32[40,256]{1,0:T(8,128)S(1)}, f32[40,256]{1,0:T(8,128)S(1)}, f32[40,256]{1,0:T(8,128)S(1)}, f32[40,256]{1,0:T(...) custom-call(s32[1]{0:T(128)} %bitcast.16.me_ref, ...), custom_call_target="tpu_custom_call" | custom-call | tf_op jit(solution)/shard_map/filter_sort/pallas_call | solution.py:288
  8.0 1.3 %copy-done = bf16[2,2,1024,256]{3,2,1,0:T(8,128)(2,1)} copy-done((bf16[2,2,1024,256]{3,2,1,0:T(8,128)(2,1)}, bf16[2,2,1024,256]{3,2,1,0:T(8,128)(2,1)S(1)}, u32[]{:S(2)}) %copy-start) | copy-done | bytes 2097176
  9.3 4.5 %collective-permute-start = (f32[40,256]{1,0:T(8,128)S(1)}, f32[40,256]{1,0:T(8,128)S(1)}, u32[]{:S(2)}, u32[]{:S(2)}) collective-permute-start(f32[40,256]{1,0:T(8,128)S(1)} %get-tuple-element.46), channel_id=1, source_target_pairs={{0,28},{4,24},{8,20},{12,16},{16,12},{20,8},{24,4},{28,0},{1,29},{... | collective-permute-start | bytes 122888 | tf_op jit(solution)/shard_map/ppermute | solution.py:598
  13.8 0.6 collective-permute-start.1
  14.4 0.5 collective-permute-start.2
  14.8 2.2 %collective-permute-start.3 = (f32[40,256]{1,0:T(8,128)S(1)}, f32[40,256]{1,0:T(8,128)S(1)}, u32[]{:S(2)}, u32[]{:S(2)}) collective-permute-start(f32[40,256]{1,0:T(8,128)S(1)} %get-tuple-element.49), channel_id=1, source_target_pairs={{0,16},{4,20},{8,24},{12,28},{16,0},{20,4},{24,8},{28,12},{1,17},{... | collective-permute-start | bytes 122888 | tf_op jit(solution)/shard_map/ppermute | solution.py:598
  17.0 1.0 %collective-permute-start.4 = (f32[40,256]{1,0:T(8,128)S(1)}, f32[40,256]{1,0:T(8,128)S(1)}, u32[]{:S(2)}, u32[]{:S(2)}) collective-permute-start(f32[40,256]{1,0:T(8,128)S(1)} %get-tuple-element.50), channel_id=1, source_target_pairs={{0,12},{4,8},{8,4},{12,0},{16,28},{20,24},{24,20},{28,16},{1,13},{... | collective-permute-start | bytes 122888 | tf_op jit(solution)/shard_map/ppermute | solution.py:598
  18.1 0.8 %collective-permute-start.5 = (f32[40,256]{1,0:T(8,128)S(1)}, f32[40,256]{1,0:T(8,128)S(1)}, u32[]{:S(2)}, u32[]{:S(2)}) collective-permute-start(f32[40,256]{1,0:T(8,128)S(1)} %get-tuple-element.51), channel_id=1, source_target_pairs={{0,8},{4,12},{8,0},{12,4},{16,24},{20,28},{24,16},{28,20},{1,9},{5... | collective-permute-start | bytes 122888 | tf_op jit(solution)/shard_map/ppermute | solution.py:598
  19.0 1.2 %collective-permute-done.1.refs_1_ = f32[40,256]{1,0:T(8,128)S(1)} collective-permute-done((f32[40,256]{1,0:T(8,128)S(1)}, f32[40,256]{1,0:T(8,128)S(1)}, u32[]{:S(2)}, u32[]{:S(2)}) %collective-permute-start.1) | collective-permute-done | bytes 40992 | tf_op jit(solution)/shard_map/ppermute | solution.py:598
  20.3 2.4 %collective-permute-done.3.refs_3_ = f32[40,256]{1,0:T(8,128)S(1)} collective-permute-done((f32[40,256]{1,0:T(8,128)S(1)}, f32[40,256]{1,0:T(8,128)S(1)}, u32[]{:S(2)}, u32[]{:S(2)}) %collective-permute-start.3) | collective-permute-done | bytes 40992 | tf_op jit(solution)/shard_map/ppermute | solution.py:598
  22.7 0.2 collective-permute-done.5.refs_5_
  22.9 1.6 %copy-done.1 = bf16[2,2,1024,256]{3,2,1,0:T(8,128)(2,1)S(1)} copy-done((bf16[2,2,1024,256]{3,2,1,0:T(8,128)(2,1)S(1)}, bf16[2,2,1024,256]{3,2,1,0:T(8,128)(2,1)}, u32[]{:S(2)}) %copy-start.1) | copy-done | bytes 2097176
  24.5 9.8 %bin_modes.1 = (f32[32,2048]{1,0:T(8,128)}, f32[8,16,128]{2,1,0:T(8,128)}, s32[1]{0:T(128)}, f32[2,256,1024]{2,1,0:T(8,128)S(1)}) custom-call(f32[40,256]{1,0:T(8,128)S(1)} %collective-permute-done.refs_0_, f32[40,256]{1,0:T(8,128)S(1)} %collective-permute-done.1.refs_1_, f32[40,256]{1,0:T(8,128)S(1)} %collective-permute-done.2.refs_2_, ...), custom_call_target="tpu_custom_call" | custom-call | tf_op jit(solution)/shard_map/bin_modes/pallas_call | solution.py:430
  34.2 4.6 %all-to-all-start.3 = ((f32[8,16,128]{2,1,0:T(8,128)}), f32[8,16,128]{2,1,0:T(8,128)S(1)}, u32[]{:S(2)}, u32[]{:S(2)}) async-start(f32[8,16,128]{2,1,0:T(8,128)} %get-tuple-element.57), calls=%async_computation.3 | async-start | bytes 131072 | tf_op jit(solution)/shard_map/all_to_all | solution.py:612
  39.6 5.1 %all-to-all-done.3 = f32[8,16,128]{2,1,0:T(8,128)S(1)} async-done(((f32[8,16,128]{2,1,0:T(8,128)}), f32[8,16,128]{2,1,0:T(8,128)S(1)}, u32[]{:S(2)}, u32[]{:S(2)}) %all-to-all-start.3) | async-done | bytes 65568 | tf_op jit(solution)/shard_map/all_to_all | solution.py:612
  44.7 0.2 conditional.1
  45.0 10.7 %legendre_sums.1 = (f32[64,256]{1,0:T(8,128)S(1)}, f32[64,256]{1,0:T(8,128)S(1)}, f32[64,256]{1,0:T(8,128)S(1)}, f32[64,256]{1,0:T(8,128)S(1)}) custom-call(s32[1]{0:T(128)} %bitcast.15.me_ref, s32[32]{0:T(128)S(1)} %dynamic_slice.3.order_ref, f32[8,16,128]{2,1,0:T(8,128)S(1)} %get-tuple-element.58.recv_ref, f32[2,256,1024]{2,1,0:T(8,128)S(1)} %get-tuple-element.59.head_ref, ...), custom_call_target="tpu_custom_call" | custom-call | tf_op jit(solution)/shard_map/legendre_sums/pallas_call | solution.py:525
  55.7 2.5 %collective-permute-start.7 = (f32[64,256]{1,0:T(8,128)S(1)}, f32[64,256]{1,0:T(8,128)S(1)}, u32[]{:S(2)}, u32[]{:S(2)}) collective-permute-start(f32[64,256]{1,0:T(8,128)S(1)} %get-tuple-element.60), channel_id=1, source_target_pairs={{0,3},{1,2},{2,1},{3,0},{4,7},{5,6},{6,5},{7,4},{8,11},{9,10},{10,... | collective-permute-start | bytes 196616 | tf_op jit(solution)/shard_map/ppermute | solution.py:598
  58.2 0.5 collective-permute-start.8
  58.7 0.5 collective-permute-start.9
  59.3 1.7 %collective-permute-done.7 = f32[64,256]{1,0:T(8,128)S(1)} collective-permute-done((f32[64,256]{1,0:T(8,128)S(1)}, f32[64,256]{1,0:T(8,128)S(1)}, u32[]{:S(2)}, u32[]{:S(2)}) %collective-permute-start.7) | collective-permute-done | bytes 65568 | tf_op jit(solution)/shard_map/ppermute | solution.py:598
  61.0 1.4 %collective-permute-done.8 = f32[64,256]{1,0:T(8,128)S(1)} collective-permute-done((f32[64,256]{1,0:T(8,128)S(1)}, f32[64,256]{1,0:T(8,128)S(1)}, u32[]{:S(2)}, u32[]{:S(2)}) %collective-permute-start.8) | collective-permute-done | bytes 65568 | tf_op jit(solution)/shard_map/ppermute | solution.py:598
  62.4 0.5 collective-permute-done.9
  63.0 0.6 %broadcast_select_fusion = f32[2,32,256]{2,1,0:T(8,128)} fusion(f32[2,32,256]{2,1,0:T(8,128)S(1)} %bitcast.57, pred[32,256]{1,0:T(8,128)(4,1)S(1)} %broadcast_compare_fusion), kind=kLoop, calls=%fused_computation.93 | loop fusion | flops 16384 | bytes 139264 | tf_op jit(solution)/shard_map/jit(_where)/select_n | solution.py:628
  (26 shorter events, 0.5 us)
Async XLA Ops:
  0.6 17.3 %copy-start.6 = (s32[256]{0:T(256)S(1)}, s32[256]{0:T(256)}, u32[]{:S(2)}) copy-start(s32[256]{0:T(256)} %param.14) | copy-start | bytes 3076
  8.0 1.3 %copy-start = (bf16[2,2,1024,256]{3,2,1,0:T(8,128)(2,1)}, bf16[2,2,1024,256]{3,2,1,0:T(8,128)(2,1)S(1)}, u32[]{:S(2)}) copy-start(bf16[2,2,1024,256]{3,2,1,0:T(8,128)(2,1)S(1)} %get-tuple-element.54.refs_9_) | copy-start | bytes 6291460
  9.3 8.8 %collective-permute-start = (f32[40,256]{1,0:T(8,128)S(1)}, f32[40,256]{1,0:T(8,128)S(1)}, u32[]{:S(2)}, u32[]{:S(2)}) collective-permute-start(f32[40,256]{1,0:T(8,128)S(1)} %get-tuple-element.46), channel_id=1, source_target_pairs={{0,28},{4,24},{8,20},{12,16},{16,12},{20,8},{24,4},{28,0},{1,29},{... | collective-permute-start | bytes 122888 | tf_op jit(solution)/shard_map/ppermute | solution.py:598
  13.8 6.3 %collective-permute-start.1 = (f32[40,256]{1,0:T(8,128)S(1)}, f32[40,256]{1,0:T(8,128)S(1)}, u32[]{:S(2)}, u32[]{:S(2)}) collective-permute-start(f32[40,256]{1,0:T(8,128)S(1)} %get-tuple-element.47), channel_id=1, source_target_pairs={{0,24},{4,28},{8,16},{12,20},{16,8},{20,12},{24,0},{28,4},{1,25},{... | collective-permute-start | bytes 122888 | tf_op jit(solution)/shard_map/ppermute | solution.py:598
  14.4 5.9 %collective-permute-start.2 = (f32[40,256]{1,0:T(8,128)S(1)}, f32[40,256]{1,0:T(8,128)S(1)}, u32[]{:S(2)}, u32[]{:S(2)}) collective-permute-start(f32[40,256]{1,0:T(8,128)S(1)} %get-tuple-element.48), channel_id=1, source_target_pairs={{0,20},{4,16},{8,28},{12,24},{16,4},{20,0},{24,12},{28,8},{1,21},{... | collective-permute-start | bytes 122888 | tf_op jit(solution)/shard_map/ppermute | solution.py:598
  14.8 7.8 %collective-permute-start.3 = (f32[40,256]{1,0:T(8,128)S(1)}, f32[40,256]{1,0:T(8,128)S(1)}, u32[]{:S(2)}, u32[]{:S(2)}) collective-permute-start(f32[40,256]{1,0:T(8,128)S(1)} %get-tuple-element.49), channel_id=1, source_target_pairs={{0,16},{4,20},{8,24},{12,28},{16,0},{20,4},{24,8},{28,12},{1,17},{... | collective-permute-start | bytes 122888 | tf_op jit(solution)/shard_map/ppermute | solution.py:598
  17.0 5.7 %collective-permute-start.4 = (f32[40,256]{1,0:T(8,128)S(1)}, f32[40,256]{1,0:T(8,128)S(1)}, u32[]{:S(2)}, u32[]{:S(2)}) collective-permute-start(f32[40,256]{1,0:T(8,128)S(1)} %get-tuple-element.50), channel_id=1, source_target_pairs={{0,12},{4,8},{8,4},{12,0},{16,28},{20,24},{24,20},{28,16},{1,13},{... | collective-permute-start | bytes 122888 | tf_op jit(solution)/shard_map/ppermute | solution.py:598
  18.1 4.8 %collective-permute-start.5 = (f32[40,256]{1,0:T(8,128)S(1)}, f32[40,256]{1,0:T(8,128)S(1)}, u32[]{:S(2)}, u32[]{:S(2)}) collective-permute-start(f32[40,256]{1,0:T(8,128)S(1)} %get-tuple-element.51), channel_id=1, source_target_pairs={{0,8},{4,12},{8,0},{12,4},{16,24},{20,28},{24,16},{28,20},{1,9},{5... | collective-permute-start | bytes 122888 | tf_op jit(solution)/shard_map/ppermute | solution.py:598
  20.1 2.8 %collective-permute-start.6 = (f32[40,256]{1,0:T(8,128)S(1)}, f32[40,256]{1,0:T(8,128)S(1)}, u32[]{:S(2)}, u32[]{:S(2)}) collective-permute-start(f32[40,256]{1,0:T(8,128)S(1)} %get-tuple-element.52), channel_id=1, source_target_pairs={{0,4},{4,0},{8,12},{12,8},{16,20},{20,16},{24,28},{28,24},{1,5},{5... | collective-permute-start | bytes 122888 | tf_op jit(solution)/shard_map/ppermute | solution.py:598
  22.9 1.6 %copy-start.1 = (bf16[2,2,1024,256]{3,2,1,0:T(8,128)(2,1)S(1)}, bf16[2,2,1024,256]{3,2,1,0:T(8,128)(2,1)}, u32[]{:S(2)}) copy-start(bf16[2,2,1024,256]{3,2,1,0:T(8,128)(2,1)} %copy-done) | copy-start | bytes 6291460
  24.5 20.2 %copy-start.2 = (f32[288,256]{1,0:T(8,128)S(1)}, f32[288,256]{1,0:T(8,128)}, u32[]{:S(2)}) copy-start(f32[288,256]{1,0:T(8,128)} %constant.68.clone.table_hbm) | copy-start | bytes 884740
  24.5 20.2 %copy-start.3 = (f32[8,4096]{1,0:T(8,128)S(1)}, f32[8,4096]{1,0:T(8,128)}, u32[]{:S(2)}) copy-start(f32[8,4096]{1,0:T(8,128)} %scan_hbm.1) | copy-start | bytes 393220
  24.5 20.2 %copy-start.4 = (f32[8,4096]{1,0:T(8,128)S(1)}, f32[8,4096]{1,0:T(8,128)}, u32[]{:S(2)}) copy-start(f32[8,4096]{1,0:T(8,128)} %resp_hbm.1) | copy-start | bytes 393220
  34.2 10.5 %all-to-all-start.3 = ((f32[8,16,128]{2,1,0:T(8,128)}), f32[8,16,128]{2,1,0:T(8,128)S(1)}, u32[]{:S(2)}, u32[]{:S(2)}) async-start(f32[8,16,128]{2,1,0:T(8,128)} %get-tuple-element.57), calls=%async_computation.3 | async-start | bytes 131072 | tf_op jit(solution)/shard_map/all_to_all | solution.py:612
  55.7 5.3 %collective-permute-start.7 = (f32[64,256]{1,0:T(8,128)S(1)}, f32[64,256]{1,0:T(8,128)S(1)}, u32[]{:S(2)}, u32[]{:S(2)}) collective-permute-start(f32[64,256]{1,0:T(8,128)S(1)} %get-tuple-element.60), channel_id=1, source_target_pairs={{0,3},{1,2},{2,1},{3,0},{4,7},{5,6},{6,5},{7,4},{8,11},{9,10},{10,... | collective-permute-start | bytes 196616 | tf_op jit(solution)/shard_map/ppermute | solution.py:598
  58.2 4.3 %collective-permute-start.8 = (f32[64,256]{1,0:T(8,128)S(1)}, f32[64,256]{1,0:T(8,128)S(1)}, u32[]{:S(2)}, u32[]{:S(2)}) collective-permute-start(f32[64,256]{1,0:T(8,128)S(1)} %get-tuple-element.61), channel_id=1, source_target_pairs={{0,2},{1,3},{2,0},{3,1},{4,6},{5,7},{6,4},{7,5},{8,10},{9,11},{10,... | collective-permute-start | bytes 196616 | tf_op jit(solution)/shard_map/ppermute | solution.py:598
  58.7 4.3 %collective-permute-start.9 = (f32[64,256]{1,0:T(8,128)S(1)}, f32[64,256]{1,0:T(8,128)S(1)}, u32[]{:S(2)}, u32[]{:S(2)}) collective-permute-start(f32[64,256]{1,0:T(8,128)S(1)} %get-tuple-element.62), channel_id=1, source_target_pairs={{0,1},{1,0},{2,3},{3,2},{4,5},{5,4},{6,7},{7,6},{8,9},{9,8},{10,11... | collective-permute-start | bytes 196616 | tf_op jit(solution)/shard_map/ppermute | solution.py:598

commit v11 on v9

--- a/solution.py
+++ b/solution.py
@@ -161,6 +161,17 @@
     assert places.of == list(range(places.total_bits))
 
 
+def split2(x):
+    high = x.astype(jnp.bfloat16)
+    low = (x - high.astype(jnp.float32)).astype(jnp.bfloat16)
+    return high, low
+
+
+def three_products(left, right, dims):
+    dot = functools.partial(lax.dot_general, dimension_numbers=dims, preferred_element_type=jnp.float32)
+    return dot(left[0], right[0]) + (dot(left[1], right[0]) + dot(left[0], right[1]))
+
+
 def sort_kernel(
     me_ref, scan_hbm, resp_hbm, cycle_hbm, column_hbm, table_hbm, modes_hbm, *refs,
     buckets, span, rows, windows,
@@ -195,7 +206,8 @@
         spec_ref[here, LANES:] = im[k] * c - re[k] * s
     for load in loads[2:-1]:
         load.wait()
-    spec = jnp.dot(spec_ref[...], forward, precision=precise, preferred_element_type=jnp.float32)
+    forward_pieces = split2(forward)
+    spec = three_products(split2(spec_ref[...]), forward_pieces, (((1,), (0,)), ((), ())))
     resp = [resp_ref[:, n * LANES:(n + 1) * LANES] * (1.0 / length) for n in range(outer)]
     step = 1
     while step < outer:
@@ -206,9 +218,7 @@
         step *= 2
     resp = jnp.concatenate(resp, axis=0)
     spec = spec * jnp.concatenate([resp, resp], axis=1)
-    spec_ref[...] = lax.dot_general(
-        spec, forward, NT, precision=precise, preferred_element_type=jnp.float32
-    )
+    spec_ref[...] = three_products(split2(spec), forward_pieces, NT)
     re, im = [], []
     for k in range(outer):
         c, s = twiddle_row(k)
@@ -292,12 +302,6 @@
         compiler_params=pltpu.CompilerParams(vmem_limit_bytes=24 * 1024 * 1024),
         name="filter_sort",
     )(me, *operands, mode_table)
-
-
-def split2(x):
-    high = x.astype(jnp.bfloat16)
-    low = (x - high.astype(jnp.float32)).astype(jnp.bfloat16)
-    return high, low
 
 
 def bin_kernel(

time: 61.9 us -> 61.4 us (level)
  no operation moved by 1% of the time
where the time goes in v11:
time: 61.4 us; the launch traced here: 61.2 us
  Pallas kernels  28.2 us (46%)
  starting transfers between devices  17.7 us (29%)
  waiting for transfers between devices  12.6 us (21%)
  between operations  1.46 us (2%)
  other arithmetic  0.81 us (1%)
    ppermute x10, starting transfers between devices, swap_blocks(): out[k] = lax.ppermute(blocks[k], axis, [(i, i ^ k) for i in range(count)])  13.1 us
    pallas_call x1, Pallas kernels, legendre_sums(): pl.pallas_call(functools.partial(legendre_kernel, owners=owners), out_sha...  11.2 us
    pallas_call x1, Pallas kernels, bin_and_modes(): pl.pallas_call(functools.partial(bin_kernel, sources=sources, windows=win...  9.66 us
    ppermute x10, waiting for transfers between devices, swap_blocks(): out[k] = lax.ppermute(blocks[k], axis, [(i, i ^ k) for i in range(count)])  7.41 us
    pallas_call x1, Pallas kernels, filter_and_sort(): pl.pallas_call(body, out_shape=(jax.ShapeDtypeStruct((2 * windows * rows,...  7.36 us
    all_to_all x1, waiting for transfers between devices, local(): lax.all_to_all(modes, 'det', split_axis=0, concat_axis=0, tiled=True)  5.14 us
    all_to_all x1, starting transfers between devices, local(): lax.all_to_all(modes, 'det', split_axis=0, concat_axis=0, tiled=True)  4.51 us
  transfers between devices with their start and end apart: 11, of which 8 were waited for; matrix products, arithmetic and copies ran while one was open for 1% of the time, Pallas kernels for 0%

profile of v11, /device:TPU:0, one launch (start us, length us, event | category | flops | bytes accessed | tf_op | source)
XLA Modules:
  0.0 61.2 jit_solution(6956338352571280962)
XLA Ops:
  0.7 7.4 %filter_sort.1 = (f32[40,256]{1,0:T(8,128)S(1)}, f32[40,256]{1,0:T(8,128)S(1)}, f32[40,256]{1,0:T(8,128)S(1)}, f32[40,256]{1,0:T(8,128)S(1)}, f32[40,256]{1,0:T(...) custom-call(s32[1]{0:T(128)} %bitcast.16.me_ref, ...), custom_call_target="tpu_custom_call" | custom-call | tf_op jit(solution)/shard_map/filter_sort/pallas_call | solution.py:287
  8.1 4.6 %collective-permute-start = (f32[40,256]{1,0:T(8,128)S(1)}, f32[40,256]{1,0:T(8,128)S(1)}, u32[]{:S(2)}, u32[]{:S(2)}) collective-permute-start(f32[40,256]{1,0:T(8,128)S(1)} %get-tuple-element.45), channel_id=1, source_target_pairs={{0,28},{4,24},{8,20},{12,16},{16,12},{20,8},{24,4},{28,0},{1,29},{... | collective-permute-start | bytes 122888 | tf_op jit(solution)/shard_map/ppermute | solution.py:588
  12.6 0.6 %collective-permute-start.1 = (f32[40,256]{1,0:T(8,128)S(1)}, f32[40,256]{1,0:T(8,128)S(1)}, u32[]{:S(2)}, u32[]{:S(2)}) collective-permute-start(f32[40,256]{1,0:T(8,128)S(1)} %get-tuple-element.46), channel_id=1, source_target_pairs={{0,24},{4,28},{8,16},{12,20},{16,8},{20,12},{24,0},{28,4},{1,25},{... | collective-permute-start | bytes 122888 | tf_op jit(solution)/shard_map/ppermute | solution.py:588
  13.3 0.4 collective-permute-start.2
  13.7 2.2 %collective-permute-start.3 = (f32[40,256]{1,0:T(8,128)S(1)}, f32[40,256]{1,0:T(8,128)S(1)}, u32[]{:S(2)}, u32[]{:S(2)}) collective-permute-start(f32[40,256]{1,0:T(8,128)S(1)} %get-tuple-element.48), channel_id=1, source_target_pairs={{0,16},{4,20},{8,24},{12,28},{16,0},{20,4},{24,8},{28,12},{1,17},{... | collective-permute-start | bytes 122888 | tf_op jit(solution)/shard_map/ppermute | solution.py:588
  15.8 1.0 %collective-permute-start.4 = (f32[40,256]{1,0:T(8,128)S(1)}, f32[40,256]{1,0:T(8,128)S(1)}, u32[]{:S(2)}, u32[]{:S(2)}) collective-permute-start(f32[40,256]{1,0:T(8,128)S(1)} %get-tuple-element.49), channel_id=1, source_target_pairs={{0,12},{4,8},{8,4},{12,0},{16,28},{20,24},{24,20},{28,16},{1,13},{... | collective-permute-start | bytes 122888 | tf_op jit(solution)/shard_map/ppermute | solution.py:588
  16.9 0.9 %collective-permute-start.5 = (f32[40,256]{1,0:T(8,128)S(1)}, f32[40,256]{1,0:T(8,128)S(1)}, u32[]{:S(2)}, u32[]{:S(2)}) collective-permute-start(f32[40,256]{1,0:T(8,128)S(1)} %get-tuple-element.50), channel_id=1, source_target_pairs={{0,8},{4,12},{8,0},{12,4},{16,24},{20,28},{24,16},{28,20},{1,9},{5... | collective-permute-start | bytes 122888 | tf_op jit(solution)/shard_map/ppermute | solution.py:588
  17.8 1.1 %collective-permute-done.1.refs_1_ = f32[40,256]{1,0:T(8,128)S(1)} collective-permute-done((f32[40,256]{1,0:T(8,128)S(1)}, f32[40,256]{1,0:T(8,128)S(1)}, u32[]{:S(2)}, u32[]{:S(2)}) %collective-permute-start.1) | collective-permute-done | bytes 40992 | tf_op jit(solution)/shard_map/ppermute | solution.py:588
  19.0 0.1 reshape.230.refs_8_
  19.1 0.5 collective-permute-done.2.refs_2_
  19.7 1.9 %collective-permute-done.3.refs_3_ = f32[40,256]{1,0:T(8,128)S(1)} collective-permute-done((f32[40,256]{1,0:T(8,128)S(1)}, f32[40,256]{1,0:T(8,128)S(1)}, u32[]{:S(2)}, u32[]{:S(2)}) %collective-permute-start.3) | collective-permute-done | bytes 40992 | tf_op jit(solution)/shard_map/ppermute | solution.py:588
  21.6 0.2 collective-permute-done.5.refs_5_
  21.8 9.7 %bin_modes.1 = (f32[32,2048]{1,0:T(8,128)}, f32[8,16,128]{2,1,0:T(8,128)}, s32[1]{0:T(128)}) custom-call(f32[40,256]{1,0:T(8,128)S(1)} %collective-permute-done.refs_0_, f32[40,256]{1,0:T(8,128)S(1)} %collective-permute-done.1.refs_1_, f32[40,256]{1,0:T(8,128)S(1)} %collective-permute-done.2.refs_2_, f32[40,256]{1,0:T(8,128)S(1)} %collective-permute-done.3.refs_3_, ...), custom_call_target="tpu_custom_call" | custom-call | tf_op jit(solution)/shard_map/bin_modes/pallas_call | solution.py:424
  31.4 4.5 %all-to-all-start.3 = ((f32[8,16,128]{2,1,0:T(8,128)}), f32[8,16,128]{2,1,0:T(8,128)S(1)}, u32[]{:S(2)}, u32[]{:S(2)}) async-start(f32[8,16,128]{2,1,0:T(8,128)} %get-tuple-element.56), calls=%async_computation.3 | async-start | bytes 131072 | tf_op jit(solution)/shard_map/all_to_all | solution.py:602
  36.7 5.1 %all-to-all-done.3 = f32[8,16,128]{2,1,0:T(8,128)S(1)} async-done(((f32[8,16,128]{2,1,0:T(8,128)}), f32[8,16,128]{2,1,0:T(8,128)S(1)}, u32[]{:S(2)}, u32[]{:S(2)}) %all-to-all-start.3) | async-done | bytes 65568 | tf_op jit(solution)/shard_map/all_to_all | solution.py:602
  41.9 0.2 conditional.1
  42.1 11.2 %legendre_sums.1 = (f32[64,256]{1,0:T(8,128)S(1)}, f32[64,256]{1,0:T(8,128)S(1)}, f32[64,256]{1,0:T(8,128)S(1)}, f32[64,256]{1,0:T(8,128)S(1)}) custom-call(s32[1]{0:T(128)} %bitcast.15.me_ref, s32[32]{0:T(128)S(1)} %dynamic_slice.3.order_ref, f32[8,16,128]{2,1,0:T(8,128)S(1)} %get-tuple-element.57.recv_ref, f32[32,256,1024]{2,1,0:T(8,128)} %table_ref.1), custom_call_target="tpu_custom_call" | custom-call | tf_op jit(solution)/shard_map/legendre_sums/pallas_call | solution.py:515
  53.3 2.5 %collective-permute-start.7 = (f32[64,256]{1,0:T(8,128)S(1)}, f32[64,256]{1,0:T(8,128)S(1)}, u32[]{:S(2)}, u32[]{:S(2)}) collective-permute-start(f32[64,256]{1,0:T(8,128)S(1)} %get-tuple-element.58), channel_id=1, source_target_pairs={{0,3},{1,2},{2,1},{3,0},{4,7},{5,6},{6,5},{7,4},{8,11},{9,10},{10,... | collective-permute-start | bytes 196616 | tf_op jit(solution)/shard_map/ppermute | solution.py:588
  55.8 0.5 collective-permute-start.8
  56.3 0.5 collective-permute-start.9
  56.9 1.7 %collective-permute-done.7 = f32[64,256]{1,0:T(8,128)S(1)} collective-permute-done((f32[64,256]{1,0:T(8,128)S(1)}, f32[64,256]{1,0:T(8,128)S(1)}, u32[]{:S(2)}, u32[]{:S(2)}) %collective-permute-start.7) | collective-permute-done | bytes 65568 | tf_op jit(solution)/shard_map/ppermute | solution.py:588
  58.6 1.4 %collective-permute-done.8 = f32[64,256]{1,0:T(8,128)S(1)} collective-permute-done((f32[64,256]{1,0:T(8,128)S(1)}, f32[64,256]{1,0:T(8,128)S(1)}, u32[]{:S(2)}, u32[]{:S(2)}) %collective-permute-start.8) | collective-permute-done | bytes 65568 | tf_op jit(solution)/shard_map/ppermute | solution.py:588
  60.1 0.5 collective-permute-done.9
  60.6 0.6 %broadcast_select_fusion = f32[2,32,256]{2,1,0:T(8,128)} fusion(f32[2,32,256]{2,1,0:T(8,128)S(1)} %bitcast.57, pred[32,256]{1,0:T(8,128)(4,1)S(1)} %broadcast_compare_fusion), kind=kLoop, calls=%fused_computation.93 | loop fusion | flops 16384 | bytes 139264 | tf_op jit(solution)/shard_map/jit(_where)/select_n | solution.py:617
  (26 shorter events, 0.4 us)
Async XLA Ops:
  0.6 16.2 %copy-start.7 = (s32[256]{0:T(256)S(1)}, s32[256]{0:T(256)}, u32[]{:S(2)}) copy-start(s32[256]{0:T(256)} %param.14) | copy-start | bytes 3076
  0.6 41.2 %copy-start.1 = (f32[288,256]{1,0:T(8,128)S(1)}, f32[288,256]{1,0:T(8,128)}, u32[]{:S(2)}) copy-start(f32[288,256]{1,0:T(8,128)} %constant.68.clone.table_hbm) | copy-start | bytes 884740
  0.7 41.2 %copy-start.2 = (f32[8,4096]{1,0:T(8,128)S(1)}, f32[8,4096]{1,0:T(8,128)}, u32[]{:S(2)}) copy-start(f32[8,4096]{1,0:T(8,128)} %scan_hbm.1) | copy-start | bytes 393220
  0.7 41.2 %copy-start.3 = (f32[8,4096]{1,0:T(8,128)S(1)}, f32[8,4096]{1,0:T(8,128)}, u32[]{:S(2)}) copy-start(f32[8,4096]{1,0:T(8,128)} %resp_hbm.1) | copy-start | bytes 393220
  0.7 41.2 %copy-start.4 = (s32[8,4096]{1,0:T(8,128)S(1)}, s32[8,4096]{1,0:T(8,128)}, u32[]{:S(2)}) copy-start(s32[8,4096]{1,0:T(8,128)} %cycle_hbm.1) | copy-start | bytes 393220
  0.7 41.2 %copy-start.5 = (s32[8,4096]{1,0:T(8,128)S(1)}, s32[8,4096]{1,0:T(8,128)}, u32[]{:S(2)}) copy-start(s32[8,4096]{1,0:T(8,128)} %column_hbm.1) | copy-start | bytes 393220
  8.1 8.9 %collective-permute-start = (f32[40,256]{1,0:T(8,128)S(1)}, f32[40,256]{1,0:T(8,128)S(1)}, u32[]{:S(2)}, u32[]{:S(2)}) collective-permute-start(f32[40,256]{1,0:T(8,128)S(1)} %get-tuple-element.45), channel_id=1, source_target_pairs={{0,28},{4,24},{8,20},{12,16},{16,12},{20,8},{24,4},{28,0},{1,29},{... | collective-permute-start | bytes 122888 | tf_op jit(solution)/shard_map/ppermute | solution.py:588
  12.6 6.3 %collective-permute-start.1 = (f32[40,256]{1,0:T(8,128)S(1)}, f32[40,256]{1,0:T(8,128)S(1)}, u32[]{:S(2)}, u32[]{:S(2)}) collective-permute-start(f32[40,256]{1,0:T(8,128)S(1)} %get-tuple-element.46), channel_id=1, source_target_pairs={{0,24},{4,28},{8,16},{12,20},{16,8},{20,12},{24,0},{28,4},{1,25},{... | collective-permute-start | bytes 122888 | tf_op jit(solution)/shard_map/ppermute | solution.py:588
  13.3 6.4 %collective-permute-start.2 = (f32[40,256]{1,0:T(8,128)S(1)}, f32[40,256]{1,0:T(8,128)S(1)}, u32[]{:S(2)}, u32[]{:S(2)}) collective-permute-start(f32[40,256]{1,0:T(8,128)S(1)} %get-tuple-element.47), channel_id=1, source_target_pairs={{0,20},{4,16},{8,28},{12,24},{16,4},{20,0},{24,12},{28,8},{1,21},{... | collective-permute-start | bytes 122888 | tf_op jit(solution)/shard_map/ppermute | solution.py:588
  13.7 7.9 %collective-permute-start.3 = (f32[40,256]{1,0:T(8,128)S(1)}, f32[40,256]{1,0:T(8,128)S(1)}, u32[]{:S(2)}, u32[]{:S(2)}) collective-permute-start(f32[40,256]{1,0:T(8,128)S(1)} %get-tuple-element.48), channel_id=1, source_target_pairs={{0,16},{4,20},{8,24},{12,28},{16,0},{20,4},{24,8},{28,12},{1,17},{... | collective-permute-start | bytes 122888 | tf_op jit(solution)/shard_map/ppermute | solution.py:588
  15.8 5.7 %collective-permute-start.4 = (f32[40,256]{1,0:T(8,128)S(1)}, f32[40,256]{1,0:T(8,128)S(1)}, u32[]{:S(2)}, u32[]{:S(2)}) collective-permute-start(f32[40,256]{1,0:T(8,128)S(1)} %get-tuple-element.49), channel_id=1, source_target_pairs={{0,12},{4,8},{8,4},{12,0},{16,28},{20,24},{24,20},{28,16},{1,13},{... | collective-permute-start | bytes 122888 | tf_op jit(solution)/shard_map/ppermute | solution.py:588
  16.9 4.8 %collective-permute-start.5 = (f32[40,256]{1,0:T(8,128)S(1)}, f32[40,256]{1,0:T(8,128)S(1)}, u32[]{:S(2)}, u32[]{:S(2)}) collective-permute-start(f32[40,256]{1,0:T(8,128)S(1)} %get-tuple-element.50), channel_id=1, source_target_pairs={{0,8},{4,12},{8,0},{12,4},{16,24},{20,28},{24,16},{28,20},{1,9},{5... | collective-permute-start | bytes 122888 | tf_op jit(solution)/shard_map/ppermute | solution.py:588
  19.0 2.8 %collective-permute-start.6 = (f32[40,256]{1,0:T(8,128)S(1)}, f32[40,256]{1,0:T(8,128)S(1)}, u32[]{:S(2)}, u32[]{:S(2)}) collective-permute-start(f32[40,256]{1,0:T(8,128)S(1)} %get-tuple-element.51), channel_id=1, source_target_pairs={{0,4},{4,0},{8,12},{12,8},{16,20},{20,16},{24,28},{28,24},{1,5},{5... | collective-permute-start | bytes 122888 | tf_op jit(solution)/shard_map/ppermute | solution.py:588
  31.4 10.4 %all-to-all-start.3 = ((f32[8,16,128]{2,1,0:T(8,128)}), f32[8,16,128]{2,1,0:T(8,128)S(1)}, u32[]{:S(2)}, u32[]{:S(2)}) async-start(f32[8,16,128]{2,1,0:T(8,128)} %get-tuple-element.56), calls=%async_computation.3 | async-start | bytes 131072 | tf_op jit(solution)/shard_map/all_to_all | solution.py:602
  53.3 5.3 %collective-permute-start.7 = (f32[64,256]{1,0:T(8,128)S(1)}, f32[64,256]{1,0:T(8,128)S(1)}, u32[]{:S(2)}, u32[]{:S(2)}) collective-permute-start(f32[64,256]{1,0:T(8,128)S(1)} %get-tuple-element.58), channel_id=1, source_target_pairs={{0,3},{1,2},{2,1},{3,0},{4,7},{5,6},{6,5},{7,4},{8,11},{9,10},{10,... | collective-permute-start | bytes 196616 | tf_op jit(solution)/shard_map/ppermute | solution.py:588
  55.8 4.3 %collective-permute-start.8 = (f32[64,256]{1,0:T(8,128)S(1)}, f32[64,256]{1,0:T(8,128)S(1)}, u32[]{:S(2)}, u32[]{:S(2)}) collective-permute-start(f32[64,256]{1,0:T(8,128)S(1)} %get-tuple-element.59), channel_id=1, source_target_pairs={{0,2},{1,3},{2,0},{3,1},{4,6},{5,7},{6,4},{7,5},{8,10},{9,11},{10,... | collective-permute-start | bytes 196616 | tf_op jit(solution)/shard_map/ppermute | solution.py:588
  56.3 4.3 %collective-permute-start.9 = (f32[64,256]{1,0:T(8,128)S(1)}, f32[64,256]{1,0:T(8,128)S(1)}, u32[]{:S(2)}, u32[]{:S(2)}) collective-permute-start(f32[64,256]{1,0:T(8,128)S(1)} %get-tuple-element.60), channel_id=1, source_target_pairs={{0,1},{1,0},{2,3},{3,2},{4,5},{5,4},{6,7},{7,6},{8,9},{9,8},{10,11... | collective-permute-start | bytes 196616 | tf_op jit(solution)/shard_map/ppermute | solution.py:588
